TPU v7x, 32 devices: a whole 2x2x4 slice. The times are simulated.
32 devices in a mesh: grp: 2 (over y), day: 4 (over z), cell: 4 (over x, core).
Axes of the slice: x: 2, y: 2, z: 4, core: 2. Of those that a mesh axis runs over, the one named last changes fastest.
Arguments:
- series: bfloat16 [6144, 8192], P(('grp', 'day'), 'cell'), parts along dimension 0, may hold values from -6 to 6
- eofs: bfloat16 [64, 64, 8192], P(None, 'day', 'cell'), may hold values from -0.1875 to 0.1875
Outputs:
- pcs: float32 [6144, 64], P(('grp', 'day')), parts along dimension 0
- reconstruction: float32 [6144, 8192], P(('grp', 'day'), 'cell'), parts along dimension 0
There are 2 independent parts, one for each index of `grp`. A program takes and returns all parts, laid end to end along the dimension named above; an argument that names none is the same for every part. Nothing has to cross between parts.
All inputs are finite; a program needn't handle non-finite values.
Results may differ from a plain program's by a relative error of at most 0.0029.
Values may be sent and summed in bfloat16 or wider, within the bound.
No kernel may reach another device: no remote copies, remote signals or barrier semaphores. Data moves between devices by JAX's collectives and lax.ppermute only.
A program may use at most 128 MiB of HBM per device.

v0:
```python
import jax
import jax.numpy as jnp
from jax import lax
from jax.sharding import PartitionSpec as P


def shifted(array, axis, by):
    size = lax.axis_size(axis)
    pairs = [(i, i + by) for i in range(size) if 0 <= i + by < size]
    return lax.ppermute(array, axis, pairs)


def lag_project(source, bank, count):
    width = bank.shape[0]
    modes = bank.shape[1]
    flat_bank = bank.reshape(width * modes, bank.shape[2])
    images = lax.dot_general(
        source, flat_bank, (((1,), (1,)), ((), ())), preferred_element_type=jnp.float32
    )
    images = images.reshape(source.shape[0], width, modes)
    total = images[0:count, 0, :]
    for lag_step in range(1, width):
        total = total + images[lag_step : lag_step + count, lag_step, :]
    return total


def on_device(series, eofs):
    width = eofs.shape[0]
    edge = width - 1
    days = series.shape[0]
    cells_loc = series.shape[1]
    total_days = days * lax.axis_size("day")
    rows = lax.axis_index("day") * days + jnp.arange(days, dtype=jnp.int32)
    ahead = shifted(series[:edge], "day", -1)
    source = jnp.concatenate([series, ahead], axis=0)
    bank = lax.all_gather(eofs, "day", axis=1, tiled=True)
    sums = lag_project(source, bank, days)
    valid = (rows <= total_days - width)[:, None]
    partial_value = jnp.where(valid, sums, 0.0)
    pcs = lax.psum(partial_value, "cell")
    narrow = pcs.astype(jnp.bfloat16)
    behind = shifted(narrow[days - edge :], "day", 1)
    extended = jnp.concatenate([behind, narrow], axis=0)
    all_modes = narrow.shape[1]
    flat_bank = bank.reshape(width * all_modes, cells_loc)
    block = min(512, days)
    outputs = []
    for begin in range(0, days, block):
        size = min(block, days - begin)
        stacked = jnp.concatenate(
            [
                extended[begin + edge - lag_step : begin + edge - lag_step + size]
                for lag_step in range(width)
            ],
            axis=1,
        )
        outputs.append(jnp.dot(stacked, flat_bank, preferred_element_type=jnp.float32))
    rebuilt = jnp.concatenate(outputs, axis=0)
    counts = (jnp.minimum(rows, total_days - width) - jnp.maximum(0, rows - edge) + 1).astype(
        jnp.float32
    )
    return (pcs, rebuilt / counts[:, None])


def solution(mesh):
    return jax.shard_map(
        on_device,
        mesh=mesh,
        in_specs=(P(("grp", "day"), "cell"), P(None, "day", "cell")),
        out_specs=(P(("grp", "day"), None), P(("grp", "day"), "cell")),
        check_vma=False,
    )
```

profile of v0, /device:TPU:0, one launch (start us, length us, event | category | flops | bytes accessed | tf_op | source)
XLA Modules:
  0.0 439.6 jit_solution(10309344894079717461)
XLA Ops:
  8.0 1.1 copy-done.1
  9.1 1.3 collective-permute-start
  10.4 10.0 %collective-permute-done = bf16[63,2048]{1,0:T(8,128)(2,1)} collective-permute-done((bf16[63,2048]{1,0:T(8,128)(2,1)S(1)}, bf16[63,2048]{1,0:T(8,128)(2,1)}, u32[]{:S(2)}, u32[]{:S(2)}) %collective-permute-start) | collective-permute-done | bytes 258080 | tf_op jit(solution)/shard_map/ppermute | solution.py:10
  20.4 278.7 %all-gather.2.cloned.1.call-done = bf16[64,64,2048]{2,1,0:T(8,128)(2,1)} async-done(((bf16[64,16,2048]{2,1,0:T(8,128)(2,1)}), bf16[64,64,2048]{2,1,0:T(8,128)(2,1)}) %all-gather.2.cloned.1.call-update) | async-done | bytes 16777232 | tf_op jit(solution)/shard_map/all_gather | solution.py:36
  299.1 20.4 %fusion = f32[831,64,64]{0,2,1:T(8,128)S(1)} fusion(bf16[64,64,2048]{2,1,0:T(8,128)(2,1)} %all-gather.2.cloned.1.call-done, bf16[63,2048]{1,0:T(8,128)(2,1)} %collective-permute-done, bf16[768,2048]{1,0:T(8,128)(2,1)S(1)} %copy-done.1), kind=kOutput, calls=%fused_computation.2 | convolution fusion | flops 13948674048 | bytes 33796096 | tf_op jit(solution)/shard_map/dot_general | solution.py:17
  319.5 3.9 fusion.4
  323.5 30.0 %all-reduce.2.cloned.1.call-done = f32[768,64]{0,1:T(8,128)} async-done(((f32[768,64]{0,1:T(8,128)}), f32[768,64]{0,1:T(8,128)}) %all-reduce.2.cloned.1.call-update) | async-done | bytes 196624 | tf_op jit(solution)/shard_map/psum | solution.py:40
  353.5 0.9 convert_element_type.10
  354.5 3.6 collective-permute-start.1
  363.3 8.3 %fusion.117 = f32[256,2048]{1,0:T(8,128)S(1)} fusion(bf16[256,4096]{0,1:T(8,128)(2,1)S(1)} %constant_dynamic-update-slice_fusion.64, bf16[4096,2048]{1,0:T(8,128)(2,1)} %bitcast.295), kind=kOutput, calls=%fused_computation.375 | convolution fusion | flops 4294967296 | bytes 20971520 | tf_op jit(solution)/shard_map/dot_general | solution.py:57
  372.3 0.7 constant_dynamic-update-slice_fusion.62
  373.0 0.7 constant_dynamic-update-slice_fusion.61
  373.7 0.7 constant_dynamic-update-slice_fusion.60
  374.5 0.7 constant_dynamic-update-slice_fusion.59
  375.2 0.7 constant_dynamic-update-slice_fusion.58
  375.9 0.7 constant_dynamic-update-slice_fusion.57
  377.4 0.7 constant_dynamic-update-slice_fusion.55
  378.1 0.7 constant_dynamic-update-slice_fusion.54
  378.8 0.7 constant_dynamic-update-slice_fusion.53
  379.5 0.7 constant_dynamic-update-slice_fusion.52
  380.3 0.7 constant_dynamic-update-slice_fusion.51
  381.0 0.7 constant_dynamic-update-slice_fusion.50
  417.9 10.7 %fusion.116 = f32[512,2048]{1,0:T(8,128)S(1)} fusion(bf16[512,4096]{0,1:T(8,128)(2,1)} %constant_dynamic-update-slice_fusion, bf16[4096,2048]{1,0:T(8,128)(2,1)S(1)} %bitcast.298), kind=kOutput, calls=%fused_computation.374 | convolution fusion | flops 8589934592 | bytes 25165824 | tf_op jit(solution)/shard_map/dot_general | solution.py:57
  428.6 3.5 maximum_divide_fusion
  (138 shorter events, 44.3 us)
Async XLA Ops:
  7.2 1.9 copy-start.1
  7.2 291.9 %all-gather.2.cloned.1.call-start = ((), (), s32[]{:S(2)}) async-start(), calls=%async_computation | async-start | bytes 20971520 | tf_op jit(solution)/shard_map/all_gather | solution.py:36
  7.9 345.6 %all-reduce.2.cloned.1.call-start = ((), (), s32[]{:S(2)}) async-start(), calls=%async_computation.1 | async-start | bytes 393216 | tf_op jit(solution)/shard_map/psum | solution.py:40
  9.1 11.3 %collective-permute-start = (bf16[63,2048]{1,0:T(8,128)(2,1)S(1)}, bf16[63,2048]{1,0:T(8,128)(2,1)}, u32[]{:S(2)}, u32[]{:S(2)}) collective-permute-start(bf16[63,2048]{1,0:T(8,128)(2,1)S(1)} %slice.582), channel_id=1, source_target_pairs={{4,0},{8,4},{12,8},{5,1},{9,5},{13,9},{6,2},{10,6},{14,10},{7,3},{... | collective-permute-start | bytes 774152 | tf_op jit(solution)/shard_map/ppermute | solution.py:10
  354.5 17.8 %collective-permute-start.1 = (bf16[63,64]{0,1:T(8,128)(2,1)S(1)}, bf16[63,64]{0,1:T(8,128)(2,1)S(1)}, u32[]{:S(2)}, u32[]{:S(2)}) collective-permute-start(bf16[63,64]{0,1:T(8,128)(2,1)S(1)} %slice.841), channel_id=1, source_target_pairs={{0,4},{4,8},{8,12},{1,5},{5,9},{9,13},{2,6},{6,10},{10,14},{3,7},{... | collective-permute-start | bytes 24200 | tf_op jit(solution)/shard_map/ppermute | solution.py:10
  363.3 54.6 %slice-start = ((s8[16777216]{0:T(1024)(128)(4,1)}), s8[4194304]{0:T(1024)(128)(4,1)S(1)}, s32[]{:S(2)}) async-start(s8[16777216]{0:T(1024)(128)(4,1)} %bitcast.296), calls=%async_computation.2 | async-start | bytes 8388608
  363.3 54.6 %slice-start.1 = ((s8[16777216]{0:T(1024)(128)(4,1)}), s8[4194304]{0:T(1024)(128)(4,1)S(1)}, s32[]{:S(2)}) async-start(s8[16777216]{0:T(1024)(128)(4,1)} %bitcast.296), calls=%async_computation.3 | async-start | bytes 8388608
  363.3 54.6 %slice-start.2 = ((s8[16777216]{0:T(1024)(128)(4,1)}), s8[4194304]{0:T(1024)(128)(4,1)S(1)}, s32[]{:S(2)}) async-start(s8[16777216]{0:T(1024)(128)(4,1)} %bitcast.296), calls=%async_computation.4 | async-start | bytes 8388608
  378.8 39.1 %slice-start.3 = ((s8[16777216]{0:T(1024)(128)(4,1)}), s8[4194304]{0:T(1024)(128)(4,1)S(1)}, s32[]{:S(2)}) async-start(s8[16777216]{0:T(1024)(128)(4,1)} %bitcast.296), calls=%async_computation.5 | async-start | bytes 8388608
  428.6 3.5 copy-start
Sparse Core Ops, SparseCore 0:
  9.6 289.4 all-gather.1
  323.6 29.8 all-reduce.1
where the time goes:
time: 440 us
  waiting for transfers between devices  319 us (72%)
  other arithmetic  53.9 us (12%)
  matrix products  39.4 us (9%)
  between operations  14.2 us (3%)
  local copies, waits for them, and re-layouts  7.7 us (2%)
  starting transfers between devices  4.93 us (1%)
    all_gather x1, waiting for transfers between devices, on_device(): bank = lax.all_gather(eofs, 'day', axis=1, tiled=True)  279 us
    unnamed x63, other arithmetic  44.8 us
    psum x1, waiting for transfers between devices, on_device(): pcs = lax.psum(partial_value, 'cell')  30 us
    dot_general x1, matrix products, lag_project(): lax.dot_general(source, flat_bank, (((1,), (1,)), ((), ())), preferred_el...  20.4 us
    dot_general x2, matrix products, on_device(): jnp.dot(stacked, flat_bank, preferred_element_type=jnp.float32)  19 us
    ppermute x2, waiting for transfers between devices, shifted(): return lax.ppermute(array, axis, pairs)  10 us
  transfers between devices with their start and end apart: 4, of which 3 were waited for; matrix products, arithmetic and copies ran while one was open for 3% of the time, Pallas kernels for 0%

commit v1 on v0

v1 whole, which is shorter than its diff:
```python
import functools

import jax
import jax.numpy as jnp
from jax import lax
from jax.experimental import pallas as pl
from jax.experimental.pallas import tpu as pltpu
from jax.sharding import PartitionSpec as P

LANES = 128
WIDE = 256
HALO = 64
VMEM_BYTES = 40 * 1024 * 1024

ENDS, MIDS = (0, 3), (1, 2)
PAIRED = ((0, 1), (1, 0), (2, 3), (3, 2))
MIDDLE = ((1, 2), (2, 1))
OUTWARD = ((1, 0), (2, 3))


def lane_group(shape, modes):
    return lax.broadcasted_iota(jnp.int32, shape, len(shape) - 1) // modes


def add_lane_groups(x, modes):
    shift = LANES // 2
    while shift >= modes:
        x = x + pltpu.roll(x, shift, 1)
        shift //= 2
    return x


def pack_rows(x, modes):
    rows, groups = x.shape[0], LANES // modes
    x = x.reshape(rows // groups, groups, LANES)
    place = lax.broadcasted_iota(jnp.int32, x.shape, 1)
    return jnp.sum(jnp.where(place == lane_group(x.shape, modes), x, 0.0), axis=1)


def unpack_rows(x, modes):
    rows, groups = x.shape[0], LANES // modes
    x = jnp.broadcast_to(x[:, None, :], (rows, groups, LANES))
    place = lax.broadcasted_iota(jnp.int32, x.shape, 1)
    x = jnp.where(place == lane_group(x.shape, modes), x, 0.0)
    return add_lane_groups(x.reshape(rows * groups, LANES), modes)


def load_pieces(plan, refs, bank, sems, meta):
    waits = []
    for i, (row, rows, sources) in enumerate(plan):
        target = bank.at[pl.ds(row, rows), :]
        if len(sources) == 1:
            pltpu.make_async_copy(refs[sources[0]], target, sems.at[i]).start()
        else:
            for choice, source in enumerate(sources):

                @pl.when(meta[3] == choice)
                def _():
                    pltpu.make_async_copy(refs[source], target, sems.at[i]).start()

        waits.append(pltpu.make_async_copy(refs[sources[0]], target, sems.at[i]))
    return waits


def lag_start(part, meta, half, lags):
    if half is None:
        return part * lags
    here, index = half
    side = meta[2] if here else 1 - meta[2]
    return pl.multiple_of((side * half_parts(part) + index) * lags, 16)


def half_parts(total):
    return total // 2


def project_kernel(plan, parts, total_parts, modes, n_refs, finish, has_acc, *refs):
    meta, behind, series, ahead = refs[:4]
    pieces = refs[4 : 4 + n_refs]
    at = 4 + n_refs
    acc_in = None
    if has_acc:
        acc_in = refs[at]
        at += 1
    out, source, bank, acc, sems, src_sems = refs[at:]
    lags = WIDE // modes
    days = series.shape[0]
    halo = behind.shape[0]
    copies = [
        pltpu.make_async_copy(behind, source.at[pl.ds(0, halo), :], src_sems.at[0]),
        pltpu.make_async_copy(series, source.at[pl.ds(halo, days), :], src_sems.at[1]),
        pltpu.make_async_copy(ahead, source.at[pl.ds(halo + days, halo), :], src_sems.at[2]),
    ]
    for copy in copies:
        copy.start()
    waits = load_pieces(plan, pieces, bank, sems, meta)
    for copy in copies + waits:
        copy.wait()
    rows = acc.shape[0]
    for slot, half in enumerate(parts):
        start = lag_start(slot if half is None else total_parts, meta, half, lags)
        term = lax.dot_general(
            source[pl.ds(start, rows), :],
            bank[slot * WIDE : (slot + 1) * WIDE, :],
            (((1,), (1,)), ((), ())),
            preferred_element_type=jnp.float32,
        )
        if slot == 0:
            acc[...] = acc_in[...] + term if has_acc else term
        else:
            acc[...] += term
    if not finish:
        out[...] = acc[...]
        return
    total = acc[...]
    group = lane_group(total.shape, modes)
    bit = 1
    while bit < lags:
        total = jnp.where((group & bit) != 0, pltpu.roll(total, rows - bit, 0), total)
        bit *= 2
    total = total[: days + halo]
    total = total[:, :LANES] + total[:, LANES:]
    out[...] = pack_rows(add_lane_groups(total, modes), modes)


def rebuild_kernel(
    plan, parts, total_parts, modes, n_sums, n_refs, has_in, last, total_days, width, *refs
):
    meta = refs[0]
    sums = refs[1 : 1 + n_sums]
    pieces = refs[1 + n_sums : 1 + n_sums + n_refs]
    at = 1 + n_sums + n_refs
    rec_in = pcs_in = None
    if has_in:
        rec_in, pcs_in = refs[at : at + 2]
        at += 2
    rec_out, pcs_out, bank, stacked, sems = refs[at:]
    lags = WIDE // modes
    days = rec_out.shape[0]
    step = pl.program_id(0)

    @pl.when(step == 0)
    def _():
        waits = load_pieces(plan, pieces, bank, sems, meta)
        level = [ref[...] for ref in sums]
        while len(level) > 1:
            level = [level[i] + level[i + 1] for i in range(0, len(level), 2)]
        value = unpack_rows(level[0], modes)
        rows = value.shape[0]
        day = meta[0] + lax.broadcasted_iota(jnp.int32, value.shape, 0) - HALO
        value = jnp.where((day >= 0) & (day <= total_days - width), value, 0.0)
        own = value[HALO:, : pcs_out.shape[1]]
        mine = lane_group(own.shape, modes) == meta[1]
        pcs_out[...] = jnp.where(mine, own, pcs_in[...] if has_in else 0.0)
        narrow = value.astype(jnp.bfloat16).astype(jnp.float32)
        spread = jnp.concatenate([narrow, narrow], axis=1)
        group = lane_group(spread.shape, modes)
        bit = 1
        while bit < lags:
            spread = jnp.where((group & bit) != 0, pltpu.roll(spread, bit, 0), spread)
            bit *= 2
        stacked[...] = spread[lags:].astype(jnp.bfloat16)
        for copy in waits:
            copy.wait()

    columns = pl.ds(pl.multiple_of(step * rec_out.shape[1], rec_out.shape[1]), rec_out.shape[1])
    acc = None
    for slot, half in enumerate(parts):
        start = lag_start(slot if half is None else total_parts, meta, half, lags)
        offset = pl.multiple_of(width - lags - start, 16)
        term = jnp.dot(
            stacked[pl.ds(offset, days), :],
            bank[slot * WIDE : (slot + 1) * WIDE, columns],
            preferred_element_type=jnp.float32,
        )
        acc = term if acc is None else acc + term
    if has_in:
        acc = acc + rec_in[...]
    if last:
        day = meta[0] + lax.broadcasted_iota(jnp.int32, (days, 1), 0)
        count = jnp.minimum(day, total_days - width) - jnp.maximum(0, day - width + 1) + 1
        acc = acc * (1.0 / count.astype(jnp.float32))
    rec_out[...] = acc


def smem():
    return pl.BlockSpec(memory_space=pltpu.SMEM)


def anywhere():
    return pl.BlockSpec(memory_space=pl.ANY)


def in_vmem():
    return pl.BlockSpec(memory_space=pltpu.VMEM)


def flatten(pieces):
    arrays, plan, row = [], [], 0
    for choices in pieces:
        ids = []
        for array in choices:
            ids.append(len(arrays))
            arrays.append(array)
        rows = choices[0].shape[0]
        plan.append((row, rows, tuple(ids)))
        row += rows
    return plan, arrays, row


def project(meta, source, pieces, parts, modes, width, acc=None, finish=True):
    behind, series, ahead = source
    days, cells = series.shape
    lags = WIDE // modes
    plan, arrays, bank_rows = flatten(pieces)
    rows = days + HALO + lags
    if finish:
        shape = ((days + HALO) * modes // LANES, LANES)
    else:
        shape = (rows, WIDE)
    return pl.pallas_call(
        functools.partial(
            project_kernel,
            plan,
            parts,
            width // lags,
            modes,
            len(arrays),
            finish,
            acc is not None,
        ),
        out_shape=jax.ShapeDtypeStruct(shape, jnp.float32),
        in_specs=[smem()]
        + [anywhere()] * (3 + len(arrays))
        + ([in_vmem()] if acc is not None else []),
        out_specs=in_vmem(),
        scratch_shapes=[
            pltpu.VMEM((days + 2 * HALO, cells), jnp.bfloat16),
            pltpu.VMEM((bank_rows, cells), jnp.bfloat16),
            pltpu.VMEM((rows, WIDE), jnp.float32),
            pltpu.SemaphoreType.DMA((len(plan),)),
            pltpu.SemaphoreType.DMA((3,)),
        ],
        compiler_params=pltpu.CompilerParams(vmem_limit_bytes=VMEM_BYTES),
        cost_estimate=pl.CostEstimate(
            flops=2 * rows * bank_rows * cells,
            bytes_accessed=2 * cells * (bank_rows + days + 2 * HALO),
            transcendentals=0,
        ),
        name="project",
    )(meta, behind, series, ahead, *arrays, *([] if acc is None else [acc]))


def rebuild(meta, sums, pieces, parts, modes, width, days, cells, total_days, all_modes, so_far, last):
    lags = WIDE // modes
    plan, arrays, bank_rows = flatten(pieces)
    tile = min(WIDE, cells)
    rec_spec = pl.BlockSpec((days, tile), lambda i: (0, i))
    pcs_spec = pl.BlockSpec((days, all_modes), lambda i: (0, 0))
    has_in = so_far is not None
    n_before = 1 + len(sums) + len(arrays)
    return pl.pallas_call(
        functools.partial(
            rebuild_kernel,
            plan,
            parts,
            width // lags,
            modes,
            len(sums),
            len(arrays),
            has_in,
            last,
            total_days,
            width,
        ),
        grid=(cells // tile,),
        out_shape=(
            jax.ShapeDtypeStruct((days, cells), jnp.float32),
            jax.ShapeDtypeStruct((days, all_modes), jnp.float32),
        ),
        in_specs=[smem()]
        + [in_vmem()] * len(sums)
        + [anywhere()] * len(arrays)
        + ([rec_spec, pcs_spec] if has_in else []),
        out_specs=(rec_spec, pcs_spec),
        scratch_shapes=[
            pltpu.VMEM((bank_rows, cells), jnp.bfloat16),
            pltpu.VMEM((days + HALO - lags, WIDE), jnp.bfloat16),
            pltpu.SemaphoreType.DMA((len(plan),)),
        ],
        input_output_aliases={n_before: 0, n_before + 1: 1} if has_in else {},
        compiler_params=pltpu.CompilerParams(
            vmem_limit_bytes=VMEM_BYTES, dimension_semantics=("arbitrary",)
        ),
        cost_estimate=pl.CostEstimate(
            flops=2 * days * bank_rows * cells,
            bytes_accessed=2 * cells * bank_rows + 8 * days * cells,
            transcendentals=0,
        ),
        name="rebuild",
    )(meta, *sums, *arrays, *(so_far if has_in else ()))


def exchange(packed):
    size = lax.axis_size("cell")
    return [packed] + [
        lax.ppermute(packed, "cell", [(i, i ^ step) for i in range(size)]) for step in range(1, size)
    ]


def on_device(series, eofs):
    width, modes, cells = eofs.shape
    days = series.shape[0]
    n = lax.axis_size("day")
    groups = lax.axis_size("grp")
    total_days = days * n
    all_modes = modes * n
    day = lax.axis_index("day")
    grp = lax.axis_index("grp")
    lags = WIDE // modes
    n_parts = width // lags
    bank = eofs.reshape(width * modes, cells)
    behind = lax.ppermute(series[days - HALO :], "day", [(i, i + 1) for i in range(n - 1)])
    ahead = lax.ppermute(series[:HALO], "day", [(i + 1, i) for i in range(n - 1)])
    middle = ((day > 0) & (day < n - 1)).astype(jnp.int32)

    def meta(block):
        return jnp.stack(
            [(day * days).astype(jnp.int32), jnp.asarray(block, jnp.int32), grp.astype(jnp.int32), middle]
        )

    whole = [None] * n_parts
    shape = dict(modes=modes, width=width)
    rest = dict(days=days, cells=cells, total_days=total_days, all_modes=all_modes)

    if n != 4 or groups != 2 or n_parts != 4:
        every = lax.all_gather(bank, "day", axis=0, tiled=False)
        source = (behind, series, ahead)
        so_far = None
        for block in range(n):
            pieces = [(every[block],)]
            sums = exchange(project(meta(block), source, pieces, whole, **shape))
            so_far = rebuild(
                meta(block), sums, pieces, whole, so_far=so_far, last=block == n - 1, **shape, **rest
            )
        return so_far[1], so_far[0]

    cuts = 4
    half = width * modes // 2
    size = half // cuts
    first = lax.dynamic_slice_in_dim(bank, grp * half, half, axis=0)
    held = {("own", i): first[i * size : (i + 1) * size] for i in range(cuts)}
    held["behind"], held["ahead"] = behind, ahead
    sent_from = {
        "p1": "own", "p2": "own", "q1": "p2", "q2": "p1", "f": "q2",
        "yp1": "p1", "yp2": "p2", "yq1": "q1", "yq2": "q2", "yf": "f",
    }

    def across(array, members):
        return lax.ppermute(
            array,
            ("grp", "day"),
            [(g * n + d, (1 - g) * n + d) for g in (0, 1) for d in members],
        )

    def send(name, array):
        if name == "p1":
            return lax.ppermute(array, "day", PAIRED)
        if name in ("p2", "q2"):
            return lax.ppermute(array, "day", MIDDLE)
        if name in ("q1", "f"):
            return lax.ppermute(array, "day", OUTWARD)
        return across(array, {"yp1": ENDS + MIDS, "yp2": MIDS, "yq1": ENDS, "yq2": MIDS, "yf": ENDS}[name])

    def table(values):
        return jnp.asarray(values, jnp.int32)[day]

    metas = {
        "own": meta(day),
        "a": meta(table([1, 0, 3, 2])),
        "b": meta(table([2, 2, 1, 1])),
        "c": meta(table([3, 3, 0, 0])),
    }
    halves = [(True, 0), (True, 1), (False, 0), (False, 1)]

    def pieces_of(block, which=range(2 * cuts)):
        names = {"a": ("p1",), "b": ("q1", "p2"), "c": ("f", "q2")}[block]
        picked = []
        for i in which:
            prefix = "" if i < cuts else "y"
            picked.append(tuple(held[(prefix + name, i % cuts)] for name in names))
        return picked

    def run(task):
        kind, block = task
        if kind == "project":
            source = (held["behind"], series, held["ahead"])
            if block == "own":
                held["packed", block] = project(metas[block], source, [(bank,)], whole, **shape)
            elif block == "c1":
                held["acc"] = project(
                    metas["c"], source, pieces_of("c", range(6)), halves[:3], finish=False, **shape
                )
            elif block == "c2":
                held["packed", "c"] = project(
                    metas["c"], source, pieces_of("c", range(6, 8)), halves[3:], acc=held["acc"], **shape
                )
            else:
                held["packed", block] = project(metas[block], source, pieces_of(block), halves, **shape)
        elif kind == "exchange":
            for i, array in enumerate(exchange(held["packed", block])):
                held["sum", block, i] = array
        else:
            count = lax.axis_size("cell")
            sums = [held["sum", block, i] for i in range(count)]
            own = block == "own"
            so_far = None if own else (held["rec"], held["pcs"])
            held["rec"], held["pcs"] = rebuild(
                metas[block], sums, [(bank,)] if own else pieces_of(block),
                whole if own else halves, so_far=so_far, last=block == "c", **shape, **rest,
            )

    tasks = {
        2: ("project", "own"), 3: ("exchange", "own"), 5: ("rebuild", "own"),
        7: ("project", "a"), 8: ("exchange", "a"), 10: ("rebuild", "a"),
        11: ("project", "b"), 12: ("exchange", "b"), 14: ("rebuild", "b"),
        13: ("project", "c1"), 15: ("project", "c2"), 16: ("exchange", "c"), 17: ("rebuild", "c"),
    }

    lag = 2
    done_at = []
    for slot in range(18):
        sends = []
        if slot < cuts:
            sends += [("p1", slot), ("p2", slot)]
        elif slot < 2 * cuts:
            sends += [("q1", slot - cuts), ("q2", slot - cuts)]
        elif slot < 3 * cuts:
            sends += [("f", slot - 2 * cuts)]
        late = slot - lag
        if 0 <= late < cuts:
            sends += [("yp1", late)]
        elif cuts <= late < 2 * cuts:
            sends += [("yp2", late - cuts), ("yq1", late - cuts)]
        elif 2 * cuts <= late < 3 * cuts:
            sends += [("yq2", late - 2 * cuts), ("yf", late - 2 * cuts)]
        if lag <= slot < 16:
            keys = [(sent_from[name], i) for name, i in sends] + done_at[slot - lag]
            keys = list(dict.fromkeys(keys))
            values = lax.optimization_barrier(tuple(held[key] for key in keys))
            held.update(zip(keys, values))
        before = dict(held)
        for name, i in sends:
            held[name, i] = send(name, held[sent_from[name], i])
        if slot in tasks:
            run(tasks[slot])
        done_at.append([key for key, value in held.items() if before.get(key) is not value])
    return held["pcs"], held["rec"]


def solution(mesh):
    return jax.shard_map(
        on_device,
        mesh=mesh,
        in_specs=(P(("grp", "day"), "cell"), P(None, "day", "cell")),
        out_specs=(P(("grp", "day"), None), P(("grp", "day"), "cell")),
        check_vma=False,
    )
```

time: 440 us -> 252 us (0.57)
  waiting for transfers between devices: 319 us -> 75.8 us
  starting transfers between devices: 4.93 us -> 82.5 us
  Pallas kernels: 0 us -> 66.7 us
  other arithmetic: 53.9 us -> 2.24 us
  matrix products: 39.4 us -> 0 us
  local copies, waits for them, and re-layouts: 7.7 us -> 21 us
  between operations: 14.2 us -> 1.42 us
    all_gather x1 -> x0, waiting for transfers between devices: 279 us -> none  [on_device(): bank = lax.all_gather(eofs, 'day', axis=1, tiled=True)]
    ppermute x2 -> x54, starting transfers between devices: 4.85 us -> 82.5 us  [the longest x20 31.9 us: across(): lax.ppermute(array, ('grp', 'day'), [(g * n + d, (1 - g) * n + d) for g i...]
    pallas_call x0 -> x9, Pallas kernels: none -> 66.7 us  [the longest x4 41.1 us: rebuild(): pl.pallas_call(functools.partial(rebuild_kernel, plan, parts, width // la...]
    ppermute x2 -> x54, waiting for transfers between devices: 10 us -> 75.8 us  [the longest x8 23.3 us: send(): return lax.ppermute(array, 'day', OUTWARD)]
    unnamed x63 -> x0, other arithmetic: 44.8 us -> none
    dot_general x3 -> x0, matrix products: 39.4 us -> none  [the longest x1 20.4 us: lag_project(): lax.dot_general(source, flat_bank, (((1,), (1,)), ((), ())), preferred_el...]
    psum x1 -> x0, waiting for transfers between devices: 30 us -> none  [on_device(): pcs = lax.psum(partial_value, 'cell')]
    unnamed x77 -> x67, local copies, waits for them, and re-layouts: 7.52 us -> 15.4 us
  transfers between devices with their start and end apart: 4 -> 54, of which waited for: 3 -> 18; matrix products, arithmetic and copies ran while one was open for 3% -> 2% of each run, Pallas kernels for 0% -> 21%
where the time goes in v1:
time: 252 us; the launch traced here: 250 us
  starting transfers between devices  82.5 us (33%)
  waiting for transfers between devices  75.8 us (30%)
  Pallas kernels  66.7 us (26%)
  local copies, waits for them, and re-layouts  21 us (8%)
    pallas_call x4, Pallas kernels, rebuild(): pl.pallas_call(functools.partial(rebuild_kernel, plan, parts, width // la...  41.1 us
    ppermute x20, starting transfers between devices, across(): lax.ppermute(array, ('grp', 'day'), [(g * n + d, (1 - g) * n + d) for g i...  31.9 us
    pallas_call x5, Pallas kernels, project(): pl.pallas_call(functools.partial(project_kernel, plan, parts, width // la...  25.6 us
    ppermute x8, waiting for transfers between devices, send(): return lax.ppermute(array, 'day', OUTWARD)  23.3 us
    ppermute x12, waiting for transfers between devices, exchange(): lax.ppermute(packed, 'cell', [(i, i ^ step) for i in range(size)])  20.5 us
    ppermute x4, waiting for transfers between devices, send(): return lax.ppermute(array, 'day', PAIRED)  17.3 us
    unnamed x67, local copies, waits for them, and re-layouts  15.4 us
    ppermute x4, starting transfers between devices, send(): return lax.ppermute(array, 'day', PAIRED)  15.2 us
  transfers between devices with their start and end apart: 54, of which 18 were waited for; matrix products, arithmetic and copies ran while one was open for 2% of the time, Pallas kernels for 21%

profile of v1, /device:TPU:0, one launch (start us, length us, event | category | flops | bytes accessed | tf_op | source)
XLA Modules:
  0.0 249.7 jit_solution(12908735037509826294)
XLA Ops:
  5.5 6.8 %collective-permute-start.17 = (bf16[128,2048]{1,0:T(8,128)(2,1)S(1)}, bf16[128,2048]{1,0:T(8,128)(2,1)}, u32[]{:S(2)}, u32[]{:S(2)}) collective-permute-start(bf16[128,2048]{1,0:T(8,128)(2,1)S(1)} %get-tuple-element.178), channel_id=1, source_target_pairs={{0,4},{4,0},{8,12},{12,8},{1,5},{5,1},{9,13},{13,9},{2,6},{6,2},{1... | collective-permute-start | bytes 1572872 | tf_op jit(solution)/shard_map/ppermute | solution.py:368
  14.8 10.3 %collective-permute-start = (bf16[64,2048]{1,0:T(8,128)(2,1)S(1)}, bf16[64,2048]{1,0:T(8,128)(2,1)S(1)}, u32[]{:S(2)}, u32[]{:S(2)}) collective-permute-start(bf16[64,2048]{1,0:T(8,128)(2,1)S(1)} %get-tuple-element.183), channel_id=1, source_target_pairs={{0,4},{4,8},{8,12},{1,5},{5,9},{9,13},{2,6},{6,10},{10,14},{3,7},{... | collective-permute-start | bytes 786440 | tf_op jit(solution)/shard_map/ppermute | solution.py:323
  25.1 11.4 %collective-permute-done.2.refs_4_.refs_5_ = bf16[128,2048]{1,0:T(8,128)(2,1)} collective-permute-done((bf16[128,2048]{1,0:T(8,128)(2,1)S(1)}, bf16[128,2048]{1,0:T(8,128)(2,1)}, u32[]{:S(2)}, u32[]{:S(2)}) %collective-permute-start.2) | collective-permute-done | bytes 524320 | tf_op jit(solution)/shard_map/ppermute | solution.py:368
  38.8 4.9 %collective-permute-start.4 = (bf16[128,2048]{1,0:T(8,128)(2,1)}, bf16[128,2048]{1,0:T(8,128)(2,1)}, u32[]{:S(2)}, u32[]{:S(2)}) collective-permute-start(bf16[128,2048]{1,0:T(8,128)(2,1)} %get-tuple-element.91), channel_id=1, source_target_pairs={{0,4},{4,0},{8,12},{12,8},{1,5},{5,1},{9,13},{13,9},{2,6},{6,2},{1... | collective-permute-start | bytes 1572872 | tf_op jit(solution)/shard_map/ppermute | solution.py:368
  48.3 5.3 %project.5.refs_1_ = f32[104,128]{1,0:T(8,128)S(1)} custom-call(s32[4]{0:T(128)S(1)} %add_add_fusion.1.refs_0_, bf16[64,2048]{1,0:T(8,128)(2,1)S(1)} %collective-permute-done.refs_1_, bf16[768,2048]{1,0:T(8,128)(2,1)S(1)} %copy-done, bf16[64,2048]{1,0:T(8,128)(2,1)S(1)} %collective-permute-done.1.refs_3_, bf16[1024,2048]{1,0:T(8,128)(2,1)S(1)} %bitcast.6), custom_call_target="tpu_custom_call" | custom-call | flops 3556769792 | bytes 7864320 | tf_op jit(solution)/shard_map/project/pallas_call | solution.py:221
  55.0 4.1 %collective-permute-done.24.refs_4_ = f32[104,128]{1,0:T(8,128)S(1)} collective-permute-done((f32[104,128]{1,0:T(8,128)S(1)}, f32[104,128]{1,0:T(8,128)S(1)}, u32[]{:S(2)}, u32[]{:S(2)}) %collective-permute-start.24) | collective-permute-done | bytes 53280 | tf_op jit(solution)/shard_map/ppermute | solution.py:307
  60.5 3.5 %collective-permute-start.19 = (bf16[128,2048]{1,0:T(8,128)(2,1)S(1)}, bf16[128,2048]{1,0:T(8,128)(2,1)}, u32[]{:S(2)}, u32[]{:S(2)}) collective-permute-start(bf16[128,2048]{1,0:T(8,128)(2,1)S(1)} %copy-done.29), channel_id=1, source_target_pairs={{0,4},{4,0},{8,12},{12,8},{1,5},{5,1},{9,13},{13,9},{2,6},{6,2},{1... | collective-permute-start | bytes 1572872 | tf_op jit(solution)/shard_map/ppermute | solution.py:368
  70.9 5.9 %collective-permute-done.19.refs_7_.refs_8_ = bf16[128,2048]{1,0:T(8,128)(2,1)} collective-permute-done((bf16[128,2048]{1,0:T(8,128)(2,1)S(1)}, bf16[128,2048]{1,0:T(8,128)(2,1)}, u32[]{:S(2)}, u32[]{:S(2)}) %collective-permute-start.19) | collective-permute-done | bytes 524320 | tf_op jit(solution)/shard_map/ppermute | solution.py:368
  78.2 5.0 %collective-permute-done.9.refs_10_.refs_11_ = bf16[128,2048]{1,0:T(8,128)(2,1)S(1)} collective-permute-done((bf16[128,2048]{1,0:T(8,128)(2,1)}, bf16[128,2048]{1,0:T(8,128)(2,1)S(1)}, u32[]{:S(2)}, u32[]{:S(2)}) %collective-permute-start.9) | collective-permute-done | bytes 524320 | tf_op jit(solution)/shard_map/ppermute | solution.py:360
  94.5 4.7 %collective-permute-done.25.refs_6_.refs_7_ = bf16[128,2048]{1,0:T(8,128)(2,1)S(1)} collective-permute-done((bf16[128,2048]{1,0:T(8,128)(2,1)S(1)}, bf16[128,2048]{1,0:T(8,128)(2,1)S(1)}, u32[]{:S(2)}, u32[]{:S(2)}) %collective-permute-start.25) | collective-permute-done | bytes 524320 | tf_op jit(solution)/shard_map/ppermute | solution.py:372
  102.0 8.1 %rebuild.4 = (f32[768,2048]{1,0:T(8,128)}, f32[768,64]{1,0:T(8,128)S(1)}) custom-call(s32[4]{0:T(128)S(1)} %add_add_fusion.1.refs_0_, f32[104,128]{1,0:T(8,128)S(1)} %project.5.refs_1_, f32[104,128]{1,0:T(8,128)S(1)} %collective-permute-done.22.refs_2_, f32[104,128]{1,0:T(8,128)S(1)} %collective-permute-done.23.refs_3_, ...), custom_call_target="tpu_custom_call" | custom-call | flops 3221225472 | bytes 16777216 | tf_op jit(solution)/shard_map/rebuild/pallas_call | solution.py:262
  120.1 7.1 %project.6.refs_1_ = f32[104,128]{1,0:T(8,128)S(1)} custom-call(s32[4]{0:T(128)S(1)} %add_add_fusion.2.refs_0_, bf16[64,2048]{1,0:T(8,128)(2,1)S(1)} %copy-done.8, bf16[768,2048]{1,0:T(8,128)(2,1)S(1)} %copy-done.1, bf16[64,2048]{1,0:T(8,128)(2,1)S(1)} %copy-done.5, bf16[128,2048]{1,0:T(8,128)(2,1)} %collective-permute-done.2.refs_4_.refs_5_, ...), custom_call_target="tpu_custom_call" | custom-call | flops 3556769792 | bytes 7864320 | tf_op jit(solution)/shard_map/project/pallas_call | solution.py:221
  127.3 4.0 %collective-permute-start.39 = (bf16[128,2048]{1,0:T(8,128)(2,1)S(1)}, bf16[128,2048]{1,0:T(8,128)(2,1)S(1)}, u32[]{:S(2)}, u32[]{:S(2)}) collective-permute-start(bf16[128,2048]{1,0:T(8,128)(2,1)S(1)} %copy-done.17), channel_id=1, source_target_pairs={{0,16},{12,28},{16,0},{28,12},{1,17},{13,29},{17,1},{29,13},{2,18}... | collective-permute-start | bytes 1572872 | tf_op jit(solution)/shard_map/ppermute | solution.py:360
  132.1 3.7 %collective-permute-done.30.refs_4_ = f32[104,128]{1,0:T(8,128)S(1)} collective-permute-done((f32[104,128]{1,0:T(8,128)S(1)}, f32[104,128]{1,0:T(8,128)S(1)}, u32[]{:S(2)}, u32[]{:S(2)}) %collective-permute-start.30) | collective-permute-done | bytes 53280 | tf_op jit(solution)/shard_map/ppermute | solution.py:307
  141.6 4.1 %collective-permute-done.29.refs_3_ = f32[104,128]{1,0:T(8,128)S(1)} collective-permute-done((f32[104,128]{1,0:T(8,128)S(1)}, f32[104,128]{1,0:T(8,128)S(1)}, u32[]{:S(2)}, u32[]{:S(2)}) %collective-permute-start.29) | collective-permute-done | bytes 53280 | tf_op jit(solution)/shard_map/ppermute | solution.py:307
  147.0 4.4 %collective-permute-start.42 = (bf16[128,2048]{1,0:T(8,128)(2,1)}, bf16[128,2048]{1,0:T(8,128)(2,1)S(1)}, u32[]{:S(2)}, u32[]{:S(2)}) collective-permute-start(bf16[128,2048]{1,0:T(8,128)(2,1)} %collective-permute-done.36.refs_10_.refs_11_), channel_id=1, source_target_pairs={{0,16},{12,28},{16,0},{28,12},{1,17},{13,29},{17,1},{29,13},{2,18}... | collective-permute-start | bytes 1572872 | tf_op jit(solution)/shard_map/ppermute | solution.py:360
  158.1 6.9 %collective-permute-done.40.refs_6_.refs_7_ = bf16[128,2048]{1,0:T(8,128)(2,1)S(1)} collective-permute-done((bf16[128,2048]{1,0:T(8,128)(2,1)}, bf16[128,2048]{1,0:T(8,128)(2,1)S(1)}, u32[]{:S(2)}, u32[]{:S(2)}) %collective-permute-start.40) | collective-permute-done | bytes 524320 | tf_op jit(solution)/shard_map/ppermute | solution.py:372
  169.6 6.6 %collective-permute-done.31.refs_8_.refs_9_ = bf16[128,2048]{1,0:T(8,128)(2,1)S(1)} collective-permute-done((bf16[128,2048]{1,0:T(8,128)(2,1)}, bf16[128,2048]{1,0:T(8,128)(2,1)S(1)}, u32[]{:S(2)}, u32[]{:S(2)}) %collective-permute-start.31) | collective-permute-done | bytes 524320 | tf_op jit(solution)/shard_map/ppermute | solution.py:372
  178.9 11.3 %rebuild.5 = (f32[768,2048]{1,0:T(8,128)}, f32[768,64]{1,0:T(8,128)S(1)}) custom-call(s32[4]{0:T(128)S(1)} %add_add_fusion.2.refs_0_, f32[104,128]{1,0:T(8,128)S(1)} %project.6.refs_1_, f32[104,128]{1,0:T(8,128)S(1)} %collective-permute-done.28.refs_2_, ...), custom_call_target="tpu_custom_call", output_to_operand_aliasing={{0}: (13, {}), {1}: (14, {})} | custom-call | flops 3221225472 | bytes 16777216 | tf_op jit(solution)/shard_map/rebuild/pallas_call | solution.py:262
  190.2 6.4 %project.7.refs_1_ = f32[104,128]{1,0:T(8,128)S(1)} custom-call(s32[4]{0:T(128)S(1)} %add_add_fusion.3.refs_0_, bf16[64,2048]{1,0:T(8,128)(2,1)S(1)} %copy-done.9, bf16[768,2048]{1,0:T(8,128)(2,1)S(1)} %copy-done.1, bf16[64,2048]{1,0:T(8,128)(2,1)S(1)} %copy-done.6, bf16[128,2048]{1,0:T(8,128)(2,1)} %collective-permute-done.7.refs_4_.refs_5_, ...), custom_call_target="tpu_custom_call" | custom-call | flops 3556769792 | bytes 7864320 | tf_op jit(solution)/shard_map/project/pallas_call | solution.py:221
  211.9 4.0 %project.8.refs_8_ = f32[848,256]{1,0:T(8,128)S(1)} custom-call(s32[4]{0:T(128)S(1)} %add_add_fusion.refs_0_, bf16[64,2048]{1,0:T(8,128)(2,1)S(1)} %copy-done.9, bf16[768,2048]{1,0:T(8,128)(2,1)S(1)} %copy-done.1, bf16[64,2048]{1,0:T(8,128)(2,1)S(1)} %copy-done.6, bf16[128,2048]{1,0:T(8,128)(2,1)S(1)} %collective-permute-done.14.refs_4_.refs_5_, ...), custom_call_target="tpu_custom_call" | custom-call | flops 2667577344 | bytes 6815744 | tf_op jit(solution)/shard_map/project/pallas_call | solution.py:221
  216.0 6.5 %collective-permute-done.50.refs_6_.refs_19_ = bf16[128,2048]{1,0:T(8,128)(2,1)S(1)} collective-permute-done((bf16[128,2048]{1,0:T(8,128)(2,1)S(1)}, bf16[128,2048]{1,0:T(8,128)(2,1)S(1)}, u32[]{:S(2)}, u32[]{:S(2)}) %collective-permute-start.50) | collective-permute-done | bytes 524320 | tf_op jit(solution)/shard_map/ppermute | solution.py:360
  227.1 11.0 %rebuild.6 = (f32[768,2048]{1,0:T(8,128)}, f32[768,64]{1,0:T(8,128)S(1)}) custom-call(s32[4]{0:T(128)S(1)} %add_add_fusion.3.refs_0_, f32[104,128]{1,0:T(8,128)S(1)} %project.7.refs_1_, f32[104,128]{1,0:T(8,128)S(1)} %collective-permute-done.43.refs_2_, ...), custom_call_target="tpu_custom_call", output_to_operand_aliasing={{0}: (21, {}), {1}: (22, {})} | custom-call | flops 3221225472 | bytes 16777216 | tf_op jit(solution)/shard_map/rebuild/pallas_call | solution.py:262
  238.2 10.7 %rebuild.7 = (f32[768,2048]{1,0:T(8,128)}, f32[768,64]{1,0:T(8,128)S(1)}) custom-call(s32[4]{0:T(128)S(1)} %add_add_fusion.refs_0_, f32[104,128]{1,0:T(8,128)S(1)} %project.9.refs_1_, f32[104,128]{1,0:T(8,128)S(1)} %collective-permute-done.51.refs_2_, ...), custom_call_target="tpu_custom_call", output_to_operand_aliasing={{0}: (21, {}), {1}: (22, {})} | custom-call | flops 3221225472 | bytes 16777216 | tf_op jit(solution)/shard_map/rebuild/pallas_call | solution.py:262
  (169 shorter events, 91.5 us)
Async XLA Ops:
  4.8 33.3 %collective-permute-start.18 = (bf16[128,2048]{1,0:T(8,128)(2,1)S(1)}, bf16[128,2048]{1,0:T(8,128)(2,1)S(1)}, u32[]{:S(2)}, u32[]{:S(2)}) collective-permute-start(bf16[128,2048]{1,0:T(8,128)(2,1)S(1)} %get-tuple-element.178), channel_id=1, source_target_pairs={{4,8},{8,4},{5,9},{9,5},{6,10},{10,6},{7,11},{11,7},{20,24},{24,20... | collective-permute-start | bytes 1572872 | tf_op jit(solution)/shard_map/ppermute | solution.py:370
  5.5 33.3 %collective-permute-start.17 = (bf16[128,2048]{1,0:T(8,128)(2,1)S(1)}, bf16[128,2048]{1,0:T(8,128)(2,1)}, u32[]{:S(2)}, u32[]{:S(2)}) collective-permute-start(bf16[128,2048]{1,0:T(8,128)(2,1)S(1)} %get-tuple-element.178), channel_id=1, source_target_pairs={{0,4},{4,0},{8,12},{12,8},{1,5},{5,1},{9,13},{13,9},{2,6},{6,2},{1... | collective-permute-start | bytes 1572872 | tf_op jit(solution)/shard_map/ppermute | solution.py:368
  12.3 24.2 %collective-permute-start.2 = (bf16[128,2048]{1,0:T(8,128)(2,1)S(1)}, bf16[128,2048]{1,0:T(8,128)(2,1)}, u32[]{:S(2)}, u32[]{:S(2)}) collective-permute-start(bf16[128,2048]{1,0:T(8,128)(2,1)S(1)} %get-tuple-element.180), channel_id=1, source_target_pairs={{0,4},{4,0},{8,12},{12,8},{1,5},{5,1},{9,13},{13,9},{2,6},{6,2},{1... | collective-permute-start | bytes 1572872 | tf_op jit(solution)/shard_map/ppermute | solution.py:368
  13.5 30.2 %collective-permute-start.1 = (bf16[64,2048]{1,0:T(8,128)(2,1)S(1)}, bf16[64,2048]{1,0:T(8,128)(2,1)S(1)}, u32[]{:S(2)}, u32[]{:S(2)}) collective-permute-start(bf16[64,2048]{1,0:T(8,128)(2,1)S(1)} %get-tuple-element.182), channel_id=1, source_target_pairs={{4,0},{8,4},{12,8},{5,1},{9,5},{13,9},{6,2},{10,6},{14,10},{7,3},{... | collective-permute-start | bytes 786440 | tf_op jit(solution)/shard_map/ppermute | solution.py:324
  14.8 29.4 %collective-permute-start = (bf16[64,2048]{1,0:T(8,128)(2,1)S(1)}, bf16[64,2048]{1,0:T(8,128)(2,1)S(1)}, u32[]{:S(2)}, u32[]{:S(2)}) collective-permute-start(bf16[64,2048]{1,0:T(8,128)(2,1)S(1)} %get-tuple-element.183), channel_id=1, source_target_pairs={{0,4},{4,8},{8,12},{1,5},{5,9},{9,13},{2,6},{6,10},{10,14},{3,7},{... | collective-permute-start | bytes 786440 | tf_op jit(solution)/shard_map/ppermute | solution.py:323
  36.5 24.0 %collective-permute-start.6 = (bf16[128,2048]{1,0:T(8,128)(2,1)}, bf16[128,2048]{1,0:T(8,128)(2,1)}, u32[]{:S(2)}, u32[]{:S(2)}) collective-permute-start(bf16[128,2048]{1,0:T(8,128)(2,1)} %collective-permute-done.2.refs_4_.refs_5_), channel_id=1, source_target_pairs={{0,16},{12,28},{4,20},{8,24},{16,0},{28,12},{20,4},{24,8},{1,17},{... | collective-permute-start | bytes 1572872 | tf_op jit(solution)/shard_map/ppermute | solution.py:360
  38.1 25.9 %collective-permute-start.5 = (bf16[128,2048]{1,0:T(8,128)(2,1)}, bf16[128,2048]{1,0:T(8,128)(2,1)S(1)}, u32[]{:S(2)}, u32[]{:S(2)}) collective-permute-start(bf16[128,2048]{1,0:T(8,128)(2,1)} %get-tuple-element.91), channel_id=1, source_target_pairs={{4,8},{8,4},{5,9},{9,5},{6,10},{10,6},{7,11},{11,7},{20,24},{24,20... | collective-permute-start | bytes 1572872 | tf_op jit(solution)/shard_map/ppermute | solution.py:370
  38.8 26.2 %collective-permute-start.4 = (bf16[128,2048]{1,0:T(8,128)(2,1)}, bf16[128,2048]{1,0:T(8,128)(2,1)}, u32[]{:S(2)}, u32[]{:S(2)}) collective-permute-start(bf16[128,2048]{1,0:T(8,128)(2,1)} %get-tuple-element.91), channel_id=1, source_target_pairs={{0,4},{4,0},{8,12},{12,8},{1,5},{5,1},{9,13},{13,9},{2,6},{6,2},{1... | collective-permute-start | bytes 1572872 | tf_op jit(solution)/shard_map/ppermute | solution.py:368
  43.7 25.7 %collective-permute-start.21 = (bf16[128,2048]{1,0:T(8,128)(2,1)}, bf16[128,2048]{1,0:T(8,128)(2,1)S(1)}, u32[]{:S(2)}, u32[]{:S(2)}) collective-permute-start(bf16[128,2048]{1,0:T(8,128)(2,1)} %collective-permute-done.17.refs_5_.refs_6_), channel_id=1, source_target_pairs={{0,16},{12,28},{4,20},{8,24},{16,0},{28,12},{20,4},{24,8},{1,17},{... | collective-permute-start | bytes 1572872 | tf_op jit(solution)/shard_map/ppermute | solution.py:360
  76.9 22.3 %collective-permute-start.25 = (bf16[128,2048]{1,0:T(8,128)(2,1)S(1)}, bf16[128,2048]{1,0:T(8,128)(2,1)S(1)}, u32[]{:S(2)}, u32[]{:S(2)}) collective-permute-start(bf16[128,2048]{1,0:T(8,128)(2,1)S(1)} %copy-done.12), channel_id=1, source_target_pairs={{4,0},{8,12},{5,1},{9,13},{6,2},{10,14},{7,3},{11,15},{20,16},{24,... | collective-permute-start | bytes 1572872 | tf_op jit(solution)/shard_map/ppermute | solution.py:372
  84.0 26.1 %collective-permute-start.26 = (bf16[128,2048]{1,0:T(8,128)(2,1)}, bf16[128,2048]{1,0:T(8,128)(2,1)}, u32[]{:S(2)}, u32[]{:S(2)}) collective-permute-start(bf16[128,2048]{1,0:T(8,128)(2,1)} %collective-permute-done.17.refs_5_.refs_6_), channel_id=1, source_target_pairs={{4,8},{8,4},{5,9},{9,5},{6,10},{10,6},{7,11},{11,7},{20,24},{24,20... | collective-permute-start | bytes 1572872 | tf_op jit(solution)/shard_map/ppermute | solution.py:370
  88.1 23.3 %collective-permute-start.10 = (bf16[128,2048]{1,0:T(8,128)(2,1)S(1)}, bf16[128,2048]{1,0:T(8,128)(2,1)S(1)}, u32[]{:S(2)}, u32[]{:S(2)}) collective-permute-start(bf16[128,2048]{1,0:T(8,128)(2,1)S(1)} %collective-permute-done.5.refs_9_.refs_10_), channel_id=1, source_target_pairs={{4,0},{8,12},{5,1},{9,13},{6,2},{10,14},{7,3},{11,15},{20,16},{24,... | collective-permute-start | bytes 1572872 | tf_op jit(solution)/shard_map/ppermute | solution.py:372
  89.4 37.9 %collective-permute-start.11 = (bf16[128,2048]{1,0:T(8,128)(2,1)}, bf16[128,2048]{1,0:T(8,128)(2,1)}, u32[]{:S(2)}, u32[]{:S(2)}) collective-permute-start(bf16[128,2048]{1,0:T(8,128)(2,1)} %collective-permute-done.4.refs_6_.refs_7_), channel_id=1, source_target_pairs={{4,8},{8,4},{5,9},{9,5},{6,10},{10,6},{7,11},{11,7},{20,24},{24,20... | collective-permute-start | bytes 1572872 | tf_op jit(solution)/shard_map/ppermute | solution.py:370
  93.0 38.3 %collective-permute-start.12 = (bf16[128,2048]{1,0:T(8,128)(2,1)}, bf16[128,2048]{1,0:T(8,128)(2,1)}, u32[]{:S(2)}, u32[]{:S(2)}) collective-permute-start(bf16[128,2048]{1,0:T(8,128)(2,1)} %collective-permute-done.3.refs_5_.refs_6_), channel_id=1, source_target_pairs={{4,20},{8,24},{20,4},{24,8},{5,21},{9,25},{21,5},{25,9},{6,22},{10... | collective-permute-start | bytes 1572872 | tf_op jit(solution)/shard_map/ppermute | solution.py:360
  100.0 32.0 %collective-permute-start.13 = (bf16[128,2048]{1,0:T(8,128)(2,1)}, bf16[128,2048]{1,0:T(8,128)(2,1)}, u32[]{:S(2)}, u32[]{:S(2)}) collective-permute-start(bf16[128,2048]{1,0:T(8,128)(2,1)} %collective-permute-done.7.refs_4_.refs_5_), channel_id=1, source_target_pairs={{0,16},{12,28},{16,0},{28,12},{1,17},{13,29},{17,1},{29,13},{2,18}... | collective-permute-start | bytes 1572872 | tf_op jit(solution)/shard_map/ppermute | solution.py:360
  110.1 27.0 %collective-permute-start.36 = (bf16[128,2048]{1,0:T(8,128)(2,1)}, bf16[128,2048]{1,0:T(8,128)(2,1)}, u32[]{:S(2)}, u32[]{:S(2)}) collective-permute-start(bf16[128,2048]{1,0:T(8,128)(2,1)} %collective-permute-done.20.refs_11_.refs_12_), channel_id=1, source_target_pairs={{4,0},{8,12},{5,1},{9,13},{6,2},{10,14},{7,3},{11,15},{20,16},{24,... | collective-permute-start | bytes 1572872 | tf_op jit(solution)/shard_map/ppermute | solution.py:372
  112.2 25.6 %collective-permute-start.37 = (bf16[128,2048]{1,0:T(8,128)(2,1)}, bf16[128,2048]{1,0:T(8,128)(2,1)}, u32[]{:S(2)}, u32[]{:S(2)}) collective-permute-start(bf16[128,2048]{1,0:T(8,128)(2,1)} %collective-permute-done.19.refs_7_.refs_8_), channel_id=1, source_target_pairs={{4,8},{8,4},{5,9},{9,5},{6,10},{10,6},{7,11},{11,7},{20,24},{24,20... | collective-permute-start | bytes 1572872 | tf_op jit(solution)/shard_map/ppermute | solution.py:370
  154.6 21.7 %collective-permute-start.31 = (bf16[128,2048]{1,0:T(8,128)(2,1)}, bf16[128,2048]{1,0:T(8,128)(2,1)S(1)}, u32[]{:S(2)}, u32[]{:S(2)}) collective-permute-start(bf16[128,2048]{1,0:T(8,128)(2,1)} %collective-permute-done.11.refs_9_.refs_10_), channel_id=1, source_target_pairs={{4,0},{8,12},{5,1},{9,13},{6,2},{10,14},{7,3},{11,15},{20,16},{24,... | collective-permute-start | bytes 1572872 | tf_op jit(solution)/shard_map/ppermute | solution.py:372
  157.2 39.5 %collective-permute-start.32 = (bf16[128,2048]{1,0:T(8,128)(2,1)S(1)}, bf16[128,2048]{1,0:T(8,128)(2,1)S(1)}, u32[]{:S(2)}, u32[]{:S(2)}) collective-permute-start(bf16[128,2048]{1,0:T(8,128)(2,1)S(1)} %copy-done.3), channel_id=1, source_target_pairs={{4,20},{8,24},{20,4},{24,8},{5,21},{9,25},{21,5},{25,9},{6,22},{10... | collective-permute-start | bytes 1572872 | tf_op jit(solution)/shard_map/ppermute | solution.py:360
  165.0 31.7 %collective-permute-start.33 = (bf16[128,2048]{1,0:T(8,128)(2,1)S(1)}, bf16[128,2048]{1,0:T(8,128)(2,1)S(1)}, u32[]{:S(2)}, u32[]{:S(2)}) collective-permute-start(bf16[128,2048]{1,0:T(8,128)(2,1)S(1)} %collective-permute-done.14.refs_4_.refs_5_), channel_id=1, source_target_pairs={{0,16},{12,28},{16,0},{28,12},{1,17},{13,29},{17,1},{29,13},{2,18}... | collective-permute-start | bytes 1572872 | tf_op jit(solution)/shard_map/ppermute | solution.py:360
  167.6 33.0 %collective-permute-start.46 = (bf16[128,2048]{1,0:T(8,128)(2,1)}, bf16[128,2048]{1,0:T(8,128)(2,1)S(1)}, u32[]{:S(2)}, u32[]{:S(2)}) collective-permute-start(bf16[128,2048]{1,0:T(8,128)(2,1)} %collective-permute-done.37.refs_11_.refs_12_), channel_id=1, source_target_pairs={{4,0},{8,12},{5,1},{9,13},{6,2},{10,14},{7,3},{11,15},{20,16},{24,... | collective-permute-start | bytes 1572872 | tf_op jit(solution)/shard_map/ppermute | solution.py:372
  168.9 31.7 %collective-permute-start.47 = (bf16[128,2048]{1,0:T(8,128)(2,1)}, bf16[128,2048]{1,0:T(8,128)(2,1)S(1)}, u32[]{:S(2)}, u32[]{:S(2)}) collective-permute-start(bf16[128,2048]{1,0:T(8,128)(2,1)} %collective-permute-done.26.refs_7_.refs_8_), channel_id=1, source_target_pairs={{4,20},{8,24},{20,4},{24,8},{5,21},{9,25},{21,5},{25,9},{6,22},{10... | collective-permute-start | bytes 1572872 | tf_op jit(solution)/shard_map/ppermute | solution.py:360
  176.2 24.4 %collective-permute-start.48 = (bf16[128,2048]{1,0:T(8,128)(2,1)S(1)}, bf16[128,2048]{1,0:T(8,128)(2,1)S(1)}, u32[]{:S(2)}, u32[]{:S(2)}) collective-permute-start(bf16[128,2048]{1,0:T(8,128)(2,1)S(1)} %collective-permute-done.40.refs_6_.refs_7_), channel_id=1, source_target_pairs={{0,16},{12,28},{16,0},{28,12},{1,17},{13,29},{17,1},{29,13},{2,18}... | collective-permute-start | bytes 1572872 | tf_op jit(solution)/shard_map/ppermute | solution.py:360
  201.4 21.1 %collective-permute-start.50 = (bf16[128,2048]{1,0:T(8,128)(2,1)S(1)}, bf16[128,2048]{1,0:T(8,128)(2,1)S(1)}, u32[]{:S(2)}, u32[]{:S(2)}) collective-permute-start(bf16[128,2048]{1,0:T(8,128)(2,1)S(1)} %collective-permute-done.46.refs_10_.refs_11_), channel_id=1, source_target_pairs={{0,16},{12,28},{16,0},{28,12},{1,17},{13,29},{17,1},{29,13},{2,18}... | collective-permute-start | bytes 1572872 | tf_op jit(solution)/shard_map/ppermute | solution.py:360
  (63 other events, 1022.6 us)

commit v2 on v0

v2 whole, which is shorter than its diff:
```python
import functools

import jax
import jax.numpy as jnp
from jax import lax
from jax.experimental import pallas as pl
from jax.experimental.pallas import tpu as pltpu
from jax.sharding import PartitionSpec as P

LANES = 128
WIDE = 256
TILE = 512
HALO = 64
VMEM_BYTES = 20 * 1024 * 1024
DAY, GRP, MIDDLE_FLAG, BLOCKS = 0, 1, 2, 3

ENDS, MIDS = (0, 3), (1, 2)
PAIRED = ((0, 1), (1, 0), (2, 3), (3, 2))
MIDDLE = ((1, 2), (2, 1))
OUTWARD = ((1, 0), (2, 3))


def lane_group(shape, modes):
    return lax.broadcasted_iota(jnp.int32, shape, len(shape) - 1) // modes


def pack_skewed(acc, scratch, rows, modes):
    groups = LANES // modes
    long = rows + groups
    scratch[...] = acc[:long, :LANES] + acc[groups : long + groups, LANES:]
    count = long // groups
    group = lane_group((count, LANES), modes)
    here = before = None
    for i in range(groups):
        plane = scratch[pl.ds(i, count, stride=groups), :]
        plane = pltpu.roll(plane, modes * (groups - 1 - i), 1) if i < groups - 1 else plane
        stays = group >= groups - 1 - i
        kept, moved = jnp.where(stays, plane, 0.0), jnp.where(stays, 0.0, plane)
        here = kept if here is None else here + kept
        before = moved if before is None else before + moved
    return here[: rows // groups] + before[1:]


def spread_skewed(packed, scratch, modes):
    groups = LANES // modes
    count = packed.shape[0]
    group = lane_group((count - 1, LANES), modes)
    here, before = packed[1:], packed[:-1]
    for i in range(groups):
        shift = modes * (i + 1) % LANES
        plane = jnp.where(group >= groups - 1 - i, here, before)
        plane = pltpu.roll(plane, shift, 1) if shift else plane
        scratch[pl.ds(groups + i, count - 1, stride=groups), :] = plane


def unpack_modes(blocks, out, modes, skip):
    groups = LANES // modes
    rows = out.shape[0] // groups
    wide = out.shape[1]
    placed = []
    for index, packed in blocks:
        placed.append((index, pltpu.roll(packed, index * modes, 1)))
    group = lane_group((placed[0][1].shape[0], LANES), modes)
    for s in range(groups):
        total = None
        for index, packed in placed:
            shift = modes * (s + 1) % LANES
            value = pltpu.roll(packed, shift, 1) if shift else packed
            value = jnp.where(group == index, value, 0.0)
            total = value if total is None else total + value
        out[pl.ds(s, rows, stride=groups), :] = total[skip // groups :, :wide]


def load_pieces(plan, refs, bank, sems, meta):
    waits = []
    for i, (row, rows, start, sources) in enumerate(plan):
        target = bank.at[pl.ds(row, rows), :]

        def copy_of(source):
            return pltpu.make_async_copy(refs[source].at[pl.ds(start, rows), :], target, sems.at[i])

        if len(sources) == 1:
            copy_of(sources[0]).start()
        else:
            for choice, source in enumerate(sources):

                @pl.when(meta[MIDDLE_FLAG] == choice)
                def _():
                    copy_of(source).start()

        waits.append(copy_of(sources[0]))
    return waits


def first_lag(meta, part, count, lags):
    if isinstance(part, int):
        return part * lags
    here, index = part
    side = meta[GRP] if here else 1 - meta[GRP]
    return pl.multiple_of((side * (count // 2) + index) * lags, 16)


def stage_kernel(behind, series, ahead, out, sems):
    days = series.shape[0]
    copies = [
        pltpu.make_async_copy(behind, out.at[pl.ds(0, HALO), :], sems.at[0]),
        pltpu.make_async_copy(series, out.at[pl.ds(HALO, days), :], sems.at[1]),
        pltpu.make_async_copy(ahead, out.at[pl.ds(HALO + days, HALO), :], sems.at[2]),
    ]
    for copy in copies:
        copy.start()
    for copy in copies:
        copy.wait()


def project_kernel(plan, parts, first_slot, count, modes, n_refs, finish, *refs):
    meta, source = refs[:2]
    pieces = refs[2 : 2 + n_refs]
    at = 2 + n_refs
    acc_in = None
    if first_slot > 0:
        acc_in = refs[at]
        at += 2
    out, bank, acc, scratch, sems = refs[at:]
    lags = WIDE // modes
    for copy in load_pieces(plan, pieces, bank, sems, meta):
        copy.wait()
    rows = acc.shape[0]
    for slot, part in enumerate(parts, first_slot):
        term = lax.dot_general(
            source[pl.ds(first_lag(meta, part, count, lags), rows), :],
            bank[slot * WIDE : (slot + 1) * WIDE, :],
            (((1,), (1,)), ((), ())),
            preferred_element_type=jnp.float32,
        )
        if slot > first_slot:
            acc[...] += term
        elif first_slot > 0:
            acc[...] = acc_in[...] + term
        else:
            acc[...] = term
    if finish:
        out[...] = pack_skewed(acc, scratch, rows - lags, modes)
    else:
        out[...] = acc[...]


def rebuild_kernel(parts, count, modes, n_sums, n_old, has_in, last, order, total_days, width, days, *refs):
    meta = refs[0]
    n_blocks = len(n_sums)
    at = 1
    sums = []
    for size in n_sums:
        sums.append(refs[at : at + size])
        at += size
    banks = refs[at : at + n_blocks]
    at += n_blocks
    olds = refs[at : at + n_old]
    at += n_old
    rec_in = None
    if has_in:
        rec_in = refs[at]
        at += 1
    rec_out = refs[at]
    at += 1
    if last:
        pcs_out = refs[at]
        at += 1
        stacked, scratch, done, pcs_done, sems = refs[at:]
    else:
        packed_out = refs[at : at + n_blocks]
        at += n_blocks
        stacked, scratch = refs[at:]
    lags = WIDE // modes
    groups = LANES // modes
    per_block = len(parts) // n_blocks
    cells = banks[0].shape[1]
    values = []
    for block in range(n_blocks):
        level = [ref[...] for ref in sums[block]]
        while len(level) > 1:
            level = [level[i] + level[i + 1] for i in range(0, len(level), 2)]
        packed = level[0]
        day = groups * lax.broadcasted_iota(jnp.int32, packed.shape, 0)
        day = day + (groups - 1 - lane_group(packed.shape, modes)) + meta[DAY] - HALO
        packed = jnp.where((day >= 0) & (day <= total_days - width), packed, 0.0)
        values.append(packed)
        if not last:
            packed_out[block][...] = packed
        narrow = packed.astype(jnp.bfloat16).astype(jnp.float32)
        spread_skewed(narrow, scratch, modes)
        for index in range(per_block):
            slot = block * per_block + index
            lag = first_lag(meta, parts[slot], count, lags)
            low = pl.multiple_of(HALO - lag, 8)
            high = pl.multiple_of(HALO - groups - lag, 8)
            start = slot * WIDE
            stacked[:, start : start + LANES] = scratch[pl.ds(low, days), :].astype(jnp.bfloat16)
            stacked[:, start + LANES : start + WIDE] = scratch[pl.ds(high, days), :].astype(jnp.bfloat16)
    if last:
        day = meta[DAY] + lax.broadcasted_iota(jnp.int32, (days, 1), 0)
        windows = jnp.minimum(day, total_days - width) - jnp.maximum(0, day - width + 1) + 1
        scale = 1.0 / windows.astype(jnp.float32)
    copies = []
    depth = per_block * WIDE
    for i, start in enumerate(range(0, cells, TILE)):
        tile = slice(start, start + TILE)
        total = rec_in[:, tile] if has_in else None
        for block, bank in enumerate(banks):
            term = jnp.dot(
                stacked[:, block * depth : (block + 1) * depth],
                bank[:, tile],
                preferred_element_type=jnp.float32,
            )
            total = term if total is None else total + term
        if last:
            done[:, tile] = total * scale
            copies.append(pltpu.make_async_copy(done.at[:, tile], rec_out.at[:, tile], sems.at[i]))
            copies[-1].start()
        else:
            rec_out[:, tile] = total
    if last:
        values = [ref[...] for ref in olds] + values
        unpack_modes([(meta[BLOCKS + i], v) for i, v in zip(order, values)], pcs_done, modes, HALO)
        copies.append(pltpu.make_async_copy(pcs_done, pcs_out, sems.at[len(copies)]))
        copies[-1].start()
        for copy in copies:
            copy.wait()


def space(kind):
    return pl.BlockSpec(memory_space=kind)


def pinned(x):
    return pltpu.with_memory_space_constraint(x, pltpu.VMEM)


def flatten(pieces, row):
    arrays, plan = [], []
    for choices in pieces:
        ids = tuple(range(len(arrays), len(arrays) + len(choices)))
        arrays.extend(choices)
        rows = choices[0].shape[0]
        plan.append((row, rows, 0, ids))
        row += rows
    return plan, arrays


def stage(behind, series, ahead):
    days, cells = series.shape
    return pl.pallas_call(
        stage_kernel,
        out_shape=pltpu.VMEM((days + 2 * HALO, cells), jnp.bfloat16),
        in_specs=[space(pltpu.HBM)] * 3,
        out_specs=space(pltpu.VMEM),
        scratch_shapes=[pltpu.SemaphoreType.DMA((3,))],
        compiler_params=pltpu.CompilerParams(vmem_limit_bytes=VMEM_BYTES),
        name="stage",
    )(behind, series, ahead)


def project(meta, source, pieces, parts, modes, width, before=None, finish=True):
    cells = source.shape[1]
    lags = WIDE // modes
    slots = width // lags
    first_slot = slots - len(parts) if before else 0
    plan, arrays = flatten(pieces, first_slot * WIDE)
    long = source.shape[0] - HALO
    rows = long + lags
    if finish:
        out = jax.ShapeDtypeStruct((long * modes // LANES, LANES), jnp.float32)
    else:
        out = pltpu.VMEM((rows, WIDE), jnp.float32)
    before = [pinned(x) for x in before] if before else []
    return pl.pallas_call(
        functools.partial(project_kernel, plan, parts, first_slot, slots, modes, len(arrays), finish),
        out_shape=(out, pltpu.VMEM((slots * WIDE, cells), jnp.bfloat16)),
        in_specs=[space(pltpu.SMEM), space(pltpu.VMEM)]
        + [space(pltpu.HBM)] * len(arrays)
        + [space(pltpu.VMEM)] * len(before),
        out_specs=(space(pltpu.VMEM), space(pltpu.VMEM)),
        scratch_shapes=[
            pltpu.VMEM((rows, WIDE), jnp.float32),
            pltpu.VMEM((rows - lags // 2, LANES), jnp.float32),
            pltpu.SemaphoreType.DMA((len(plan),)),
        ],
        input_output_aliases={3 + len(arrays): 1} if before else {},
        compiler_params=pltpu.CompilerParams(vmem_limit_bytes=VMEM_BYTES),
        cost_estimate=pl.CostEstimate(
            flops=2 * rows * len(parts) * WIDE * cells,
            bytes_accessed=2 * cells * len(parts) * WIDE,
            transcendentals=0,
        ),
        name="project",
    )(meta, pinned(source), *arrays, *before)


def rebuild(meta, blocks, modes, width, days, total_days, all_modes, so_far=None, old=(), last=False):
    lags = WIDE // modes
    banks = [pinned(block[2]) for block in blocks]
    parts = [part for block in blocks for part in block[3]]
    sums = [value for block in blocks for value in block[1]]
    cells = banks[0].shape[1]
    packed = sums[0].shape
    has_in = so_far is not None
    olds = [value for _, value in old] if last else []
    order = tuple([index for index, _ in old] + [block[0] for block in blocks]) if last else ()
    scratch = [
        pltpu.VMEM((days, len(parts) * WIDE), jnp.bfloat16),
        pltpu.VMEM((days + HALO, LANES), jnp.float32),
    ]
    if last:
        out_shape = [jax.ShapeDtypeStruct((days, cells), jnp.float32)]
        out_shape += [jax.ShapeDtypeStruct((days, all_modes), jnp.float32)]
        out_specs = [space(pltpu.HBM), space(pltpu.HBM)]
        scratch += [
            pltpu.VMEM((days, cells), jnp.float32),
            pltpu.VMEM((days, all_modes), jnp.float32),
            pltpu.SemaphoreType.DMA((cells // TILE + 1,)),
        ]
    else:
        out_shape = [pltpu.VMEM((days, cells), jnp.float32)]
        out_shape += [jax.ShapeDtypeStruct(packed, jnp.float32) for _ in blocks]
        out_specs = [space(pltpu.VMEM)] * len(out_shape)
    before = 1 + len(sums) + len(banks)
    return pl.pallas_call(
        functools.partial(
            rebuild_kernel,
            parts,
            width // lags,
            modes,
            [len(block[1]) for block in blocks],
            len(olds),
            has_in,
            last,
            order,
            total_days,
            width,
            days,
        ),
        out_shape=out_shape,
        in_specs=[space(pltpu.SMEM)] + [space(pltpu.VMEM)] * (len(sums) + len(banks) + len(olds) + has_in),
        out_specs=out_specs,
        scratch_shapes=scratch,
        input_output_aliases={before: 0} if has_in and not last else {},
        compiler_params=pltpu.CompilerParams(vmem_limit_bytes=VMEM_BYTES),
        cost_estimate=pl.CostEstimate(
            flops=2 * days * len(parts) * WIDE * cells,
            bytes_accessed=4 * days * cells,
            transcendentals=0,
        ),
        name="rebuild",
    )(meta, *sums, *banks, *olds, *([pinned(so_far)] if has_in else []))


def exchange(packed):
    size = lax.axis_size("cell")
    return [packed] + [
        lax.ppermute(packed, "cell", [(i, i ^ step) for i in range(size)]) for step in range(1, size)
    ]


def on_device(series, eofs):
    width, modes, cells = eofs.shape
    days = series.shape[0]
    n = lax.axis_size("day")
    total_days = days * n
    day = lax.axis_index("day").astype(jnp.int32)
    grp = lax.axis_index("grp").astype(jnp.int32)
    n_parts = width * modes // WIDE
    bank = eofs.reshape(width * modes, cells)
    behind = lax.ppermute(series[days - HALO :], "day", [(i, i + 1) for i in range(n - 1)])
    ahead = lax.ppermute(series[:HALO], "day", [(i + 1, i) for i in range(n - 1)])
    middle = ((day > 0) & (day < n - 1)).astype(jnp.int32)
    whole = list(range(n_parts))
    shape = dict(modes=modes, width=width)
    rest = dict(days=days, total_days=total_days, all_modes=modes * n)

    if n != 4 or lax.axis_size("grp") != 2 or n_parts != 4:
        every = lax.all_gather(bank, "day", axis=0, tiled=False)
        meta = jnp.stack([day * days, grp, middle] + [jnp.int32(i) for i in range(n)])
        source = stage(behind, series, ahead)
        rec, old = None, []
        for block in range(n):
            pieces = [(every[block],)]
            packed, bank = project(meta, source, pieces, whole, **shape)
            rec, small = rebuild(
                meta, [(block, exchange(packed), bank, whole)], so_far=rec, old=old, last=block == n - 1, **shape, **rest
            )
            old.append((block, small))
        return small, rec

    def table(values):
        return jnp.asarray(values, jnp.int32)[day]

    meta = jnp.stack(
        [day * days, grp, middle, day, table([1, 0, 3, 2]), table([2, 2, 1, 1]), table([3, 3, 0, 0])]
    )
    cuts = 4
    half = width * modes // 2
    size = half // cuts
    first = lax.dynamic_slice_in_dim(bank, grp * half, half, axis=0)
    held = {("own", i): first[i * size : (i + 1) * size] for i in range(cuts)}
    held["behind"], held["ahead"] = behind, ahead
    sent_from = {
        "p1": "own", "p2": "own", "q1": "p2", "q2": "p1", "f": "q2",
        "yp1": "p1", "yp2": "p2", "yq1": "q1", "yq2": "q2", "yf": "f", "h": "yp1", "g": "h",
    }

    def across(array, members):
        return lax.ppermute(
            array,
            ("grp", "day"),
            [(g * n + d, (1 - g) * n + d) for g in (0, 1) for d in members],
        )

    def send(name, array):
        if name == "p1":
            return lax.ppermute(array, "day", PAIRED)
        if name in ("p2", "q2", "h"):
            return lax.ppermute(array, "day", MIDDLE)
        if name in ("q1", "f", "g"):
            return lax.ppermute(array, "day", OUTWARD)
        return across(array, {"yp1": ENDS + MIDS, "yp2": MIDS, "yq1": ENDS, "yq2": MIDS, "yf": ENDS}[name])

    halves = [(True, 0), (True, 1), (False, 0), (False, 1)]
    arrivals = {"a": ("p1",), "b": ("q1", "p2"), "c": ("f", "q2")}
    place = {"own": 0, "a": 1, "b": 2, "c": 3}

    def pieces_of(block, which=range(2 * cuts)):
        if block == "own":
            return [(bank,)]
        picked = []
        for i in which:
            names = arrivals[block] if i < cuts else ["y" + name for name in arrivals[block]]
            if block == "c" and i == 2 * cuts - 1:
                names = ("g", "h")
            picked.append(tuple(held[name, i % cuts] for name in names))
        return picked

    def run(kind, which):
        if kind == "stage":
            held["source"] = stage(held["behind"], series, held["ahead"])
        elif kind == "project":
            source = held["source"]
            if which == "c1":
                held["acc"], held["bank", "c"] = project(
                    meta, source, pieces_of("c", range(6)), halves[:3], finish=False, **shape
                )
            elif which == "c2":
                before = (held["acc"], held["bank", "c"])
                held["packed", "c"], held["bank", "c"] = project(
                    meta, source, pieces_of("c", range(6, 8)), halves[3:], before=before, **shape
                )
            else:
                parts = whole if which == "own" else halves
                held["packed", which], held["bank", which] = project(
                    meta, source, pieces_of(which), parts, **shape
                )
        elif kind == "exchange":
            for i, array in enumerate(exchange(held["packed", which])):
                held["sum", which, i] = array
        else:
            blocks = []
            for block in which:
                sums = [held["sum", block, i] for i in range(lax.axis_size("cell"))]
                parts = whole if block == "own" else halves
                blocks.append((place[block], sums, held["bank", block], parts))
            last = "c" in which
            old = [(place[b], held["old", b]) for b in place if ("old", b) in held]
            done = rebuild(meta, blocks, so_far=held.get("rec"), old=old, last=last, **shape, **rest)
            held["rec"] = done[0]
            if last:
                held["pcs"] = done[1]
            else:
                held.update({("old", block): value for block, value in zip(which, done[1:])})

    tasks = {
        2: [("stage", None), ("project", "own")],
        3: [("exchange", "own")],
        5: [("rebuild", ("own",))],
        7: [("project", "a")],
        8: [("exchange", "a")],
        10: [("rebuild", ("a",))],
        11: [("project", "b")],
        12: [("exchange", "b"), ("project", "c1")],
        13: [("rebuild", ("b",)), ("project", "c2")],
        14: [("exchange", "c")],
        15: [("rebuild", ("c",))],
    }

    lag = 2
    done_at = []
    for slot in range(16):
        sends = []
        if slot < cuts:
            sends += [("p1", slot), ("p2", slot)]
        elif slot < 2 * cuts:
            sends += [("q1", slot - cuts), ("q2", slot - cuts)]
        elif slot < 3 * cuts:
            sends += [("f", slot - 2 * cuts)]
        late = slot - lag
        if 0 <= late < cuts:
            sends += [("yp1", late)]
        elif cuts <= late < 2 * cuts:
            sends += [("yp2", late - cuts), ("yq1", late - cuts)]
        elif 2 * cuts <= late < 3 * cuts - 1:
            sends += [("yq2", late - 2 * cuts), ("yf", late - 2 * cuts)]
        if slot == 2 * cuts:
            sends += [("h", cuts - 1)]
        if slot == 3 * cuts:
            sends = [("g", cuts - 1)] + sends
        if lag <= slot < 3 * cuts + 1:
            keys = [(sent_from[name], i) for name, i in sends] + done_at[slot - lag]
            keys = list(dict.fromkeys(keys))
            values = lax.optimization_barrier(tuple(held[key] for key in keys))
            held.update(zip(keys, values))
        before = dict(held)
        for name, i in sends:
            held[name, i] = send(name, held[sent_from[name], i])
        for task in tasks.get(slot, []):
            run(*task)
        done_at.append([key for key, value in held.items() if before.get(key) is not value])
    return held["pcs"], held["rec"]


def solution(mesh):
    return jax.shard_map(
        on_device,
        mesh=mesh,
        in_specs=(P(("grp", "day"), "cell"), P(None, "day", "cell")),
        out_specs=(P(("grp", "day"), None), P(("grp", "day"), "cell")),
        check_vma=False,
    )
```

time: 440 us -> 200 us (0.45)
  waiting for transfers between devices: 319 us -> 76.8 us
  starting transfers between devices: 4.93 us -> 70.1 us
  other arithmetic: 53.9 us -> 0 us
  Pallas kernels: 0 us -> 41.1 us
  matrix products: 39.4 us -> 0 us
  between operations: 14.2 us -> 1.29 us
    all_gather x1 -> x0, waiting for transfers between devices: 279 us -> none  [on_device(): bank = lax.all_gather(eofs, 'day', axis=1, tiled=True)]
    ppermute x2 -> x54, waiting for transfers between devices: 10 us -> 76.8 us  [the longest x9 36.7 us: send(): return lax.ppermute(array, 'day', OUTWARD)]
    ppermute x2 -> x54, starting transfers between devices: 4.85 us -> 70.1 us  [the longest x18 30.7 us: across(): lax.ppermute(array, ('grp', 'day'), [(g * n + d, (1 - g) * n + d) for g i...]
    unnamed x63 -> x0, other arithmetic: 44.8 us -> none
    pallas_call x0 -> x10, Pallas kernels: none -> 41.1 us  [the longest x5 21.3 us: project(): pl.pallas_call(functools.partial(project_kernel, plan, parts, first_slot,...]
    dot_general x3 -> x0, matrix products: 39.4 us -> none  [the longest x1 20.4 us: lag_project(): lax.dot_general(source, flat_bank, (((1,), (1,)), ((), ())), preferred_el...]
    psum x1 -> x0, waiting for transfers between devices: 30 us -> none  [on_device(): pcs = lax.psum(partial_value, 'cell')]
    unnamed x77 -> x15, local copies, waits for them, and re-layouts: 7.52 us -> 0.87 us
  transfers between devices with their start and end apart: 4 -> 54, of which waited for: 3 -> 20; matrix products, arithmetic and copies ran while one was open for 3% -> 3% of each run, Pallas kernels for 0% -> 18%
where the time goes in v2:
time: 200 us; the launch traced here: 199 us
  waiting for transfers between devices  76.8 us (38%)
  starting transfers between devices  70.1 us (35%)
  Pallas kernels  41.1 us (21%)
  local copies, waits for them, and re-layouts  9.62 us (5%)
    ppermute x9, waiting for transfers between devices, send(): return lax.ppermute(array, 'day', OUTWARD)  36.7 us
    ppermute x18, starting transfers between devices, across(): lax.ppermute(array, ('grp', 'day'), [(g * n + d, (1 - g) * n + d) for g i...  30.7 us
    pallas_call x5, Pallas kernels, project(): pl.pallas_call(functools.partial(project_kernel, plan, parts, first_slot,...  21.3 us
    ppermute x4, waiting for transfers between devices, send(): return lax.ppermute(array, 'day', PAIRED)  18.8 us
    pallas_call x4, Pallas kernels, rebuild(): pl.pallas_call(functools.partial(rebuild_kernel, parts, width // lags, mo...  18.5 us
    ppermute x12, waiting for transfers between devices, exchange(): lax.ppermute(packed, 'cell', [(i, i ^ step) for i in range(size)])  12.7 us
    ppermute x9, starting transfers between devices, send(): return lax.ppermute(array, 'day', OUTWARD)  11.5 us
    ppermute x4, starting transfers between devices, send(): return lax.ppermute(array, 'day', PAIRED)  9.1 us
  transfers between devices with their start and end apart: 54, of which 20 were waited for; matrix products, arithmetic and copies ran while one was open for 3% of the time, Pallas kernels for 18%

profile of v2, /device:TPU:0, one launch (start us, length us, event | category | flops | bytes accessed | tf_op | source)
XLA Modules:
  0.0 199.0 jit_solution(4101053345837119011)
XLA Ops:
  2.7 4.9 %collective-permute-start.5 = (bf16[64,2048]{1,0:T(8,128)(2,1)}, bf16[64,2048]{1,0:T(8,128)(2,1)S(1)}, u32[]{:S(2)}, u32[]{:S(2)}) collective-permute-start(bf16[64,2048]{1,0:T(8,128)(2,1)} %get-tuple-element.189), channel_id=1, source_target_pairs={{0,4},{4,8},{8,12},{1,5},{5,9},{9,13},{2,6},{6,10},{10,14},{3,7},{... | collective-permute-start | bytes 786440 | tf_op jit(solution)/shard_map/ppermute | solution.py:373
  16.0 4.3 %collective-permute-start = (bf16[128,2048]{1,0:T(8,128)(2,1)}, bf16[128,2048]{1,0:T(8,128)(2,1)}, u32[]{:S(2)}, u32[]{:S(2)}) collective-permute-start(bf16[128,2048]{1,0:T(8,128)(2,1)} %get-tuple-element.186), channel_id=1, source_target_pairs={{0,4},{4,0},{8,12},{12,8},{1,5},{5,1},{9,13},{13,9},{2,6},{6,2},{1... | collective-permute-start | bytes 1572872 | tf_op jit(solution)/shard_map/ppermute | solution.py:420
  26.4 4.7 %project.5 = (f32[104,128]{1,0:T(8,128)S(1)}, bf16[1024,2048]{1,0:T(8,128)(2,1)S(1)}) custom-call(s32[7]{0:T(128)S(1)} %stack.23.refs_0_, bf16[896,2048]{1,0:T(8,128)(2,1)S(1)} %stage.1.refs_1_, bf16[1024,2048]{1,0:T(8,128)(2,1)S(1)} %bitcast.6), custom_call_target="tpu_custom_call" | custom-call | flops 3556769792 | bytes 4194304 | tf_op jit(solution)/shard_map/project/pallas_call | solution.py:276
  35.7 5.9 %collective-permute-done.refs_2_ = bf16[128,2048]{1,0:T(8,128)(2,1)} collective-permute-done((bf16[128,2048]{1,0:T(8,128)(2,1)}, bf16[128,2048]{1,0:T(8,128)(2,1)}, u32[]{:S(2)}, u32[]{:S(2)}) %collective-permute-start) | collective-permute-done | bytes 524320 | tf_op jit(solution)/shard_map/ppermute | solution.py:420
  47.5 5.2 %collective-permute-done.13.refs_5_ = bf16[128,2048]{1,0:T(8,128)(2,1)S(1)} collective-permute-done((bf16[128,2048]{1,0:T(8,128)(2,1)S(1)}, bf16[128,2048]{1,0:T(8,128)(2,1)S(1)}, u32[]{:S(2)}, u32[]{:S(2)}) %collective-permute-start.13) | collective-permute-done | bytes 524320 | tf_op jit(solution)/shard_map/ppermute | solution.py:420
  56.2 7.7 %collective-permute-done.2.refs_4_ = bf16[128,2048]{1,0:T(8,128)(2,1)S(1)} collective-permute-done((bf16[128,2048]{1,0:T(8,128)(2,1)S(1)}, bf16[128,2048]{1,0:T(8,128)(2,1)S(1)}, u32[]{:S(2)}, u32[]{:S(2)}) %collective-permute-start.2) | collective-permute-done | bytes 524320 | tf_op jit(solution)/shard_map/ppermute | solution.py:420
  67.4 7.7 %collective-permute-done.19.refs_4_ = bf16[128,2048]{1,0:T(8,128)(2,1)S(1)} collective-permute-done((bf16[128,2048]{1,0:T(8,128)(2,1)}, bf16[128,2048]{1,0:T(8,128)(2,1)S(1)}, u32[]{:S(2)}, u32[]{:S(2)}) %collective-permute-start.19) | collective-permute-done | bytes 524320 | tf_op jit(solution)/shard_map/ppermute | solution.py:424
  76.7 4.2 %rebuild.4 = (f32[768,2048]{1,0:T(8,128)S(1)}, f32[104,128]{1,0:T(8,128)S(1)}) custom-call(s32[7]{0:T(128)S(1)} %stack.23.refs_0_, f32[104,128]{1,0:T(8,128)S(1)} %get-tuple-element.111.refs_1_, f32[104,128]{1,0:T(8,128)S(1)} %collective-permute-done.16.refs_2_, f32[104,128]{1,0:T(8,128)S(1)} %collective-permute-done.17.refs_3_, ...), custom_call_target="tpu_custom_call" | custom-call | flops 3221225472 | bytes 6291456 | tf_op jit(solution)/shard_map/rebuild/pallas_call | solution.py:327
  80.9 4.1 %collective-permute-done.7.refs_2_ = bf16[128,2048]{1,0:T(8,128)(2,1)S(1)} collective-permute-done((bf16[128,2048]{1,0:T(8,128)(2,1)S(1)}, bf16[128,2048]{1,0:T(8,128)(2,1)S(1)}, u32[]{:S(2)}, u32[]{:S(2)}) %collective-permute-start.7) | collective-permute-done | bytes 524320 | tf_op jit(solution)/shard_map/ppermute | solution.py:424
  89.1 3.4 %collective-permute-start.24 = (bf16[128,2048]{1,0:T(8,128)(2,1)S(1)}, bf16[128,2048]{1,0:T(8,128)(2,1)S(1)}, u32[]{:S(2)}, u32[]{:S(2)}) collective-permute-start(bf16[128,2048]{1,0:T(8,128)(2,1)S(1)} %collective-permute-done.7.refs_2_), channel_id=1, source_target_pairs={{0,16},{12,28},{16,0},{28,12},{1,17},{13,29},{17,1},{29,13},{2,18}... | collective-permute-start | bytes 1572872 | tf_op jit(solution)/shard_map/ppermute | solution.py:412
  92.5 5.7 %project.6 = (f32[104,128]{1,0:T(8,128)S(1)}, bf16[1024,2048]{1,0:T(8,128)(2,1)S(1)}) custom-call(s32[7]{0:T(128)S(1)} %stack.23.refs_0_, bf16[896,2048]{1,0:T(8,128)(2,1)S(1)} %stage.1.refs_1_, bf16[128,2048]{1,0:T(8,128)(2,1)} %collective-permute-done.refs_2_, bf16[128,2048]{1,0:T(8,128)(2,1)} %collective-permute-done.11.refs_3_, ...), custom_call_target="tpu_custom_call" | custom-call | flops 3556769792 | bytes 4194304 | tf_op jit(solution)/shard_map/project/pallas_call | solution.py:276
  102.8 3.4 %collective-permute-start.36 = (bf16[128,2048]{1,0:T(8,128)(2,1)S(1)}, bf16[128,2048]{1,0:T(8,128)(2,1)S(1)}, u32[]{:S(2)}, u32[]{:S(2)}) collective-permute-start(bf16[128,2048]{1,0:T(8,128)(2,1)S(1)} %collective-permute-done.19.refs_4_), channel_id=1, source_target_pairs={{0,16},{12,28},{16,0},{28,12},{1,17},{13,29},{17,1},{29,13},{2,18}... | collective-permute-start | bytes 1572872 | tf_op jit(solution)/shard_map/ppermute | solution.py:412
  106.3 4.1 %collective-permute-done.30.refs_3_ = f32[104,128]{1,0:T(8,128)S(1)} collective-permute-done((f32[104,128]{1,0:T(8,128)S(1)}, f32[104,128]{1,0:T(8,128)S(1)}, u32[]{:S(2)}, u32[]{:S(2)}) %collective-permute-start.30) | collective-permute-done | bytes 53280 | tf_op jit(solution)/shard_map/ppermute | solution.py:360
  111.7 6.4 %collective-permute-done.33.refs_8_ = bf16[128,2048]{1,0:T(8,128)(2,1)S(1)} collective-permute-done((bf16[128,2048]{1,0:T(8,128)(2,1)S(1)}, bf16[128,2048]{1,0:T(8,128)(2,1)S(1)}, u32[]{:S(2)}, u32[]{:S(2)}) %collective-permute-start.33) | collective-permute-done | bytes 524320 | tf_op jit(solution)/shard_map/ppermute | solution.py:424
  122.2 3.6 %collective-permute-done.31.refs_4_ = f32[104,128]{1,0:T(8,128)S(1)} collective-permute-done((f32[104,128]{1,0:T(8,128)S(1)}, f32[104,128]{1,0:T(8,128)S(1)}, u32[]{:S(2)}, u32[]{:S(2)}) %collective-permute-start.31) | collective-permute-done | bytes 53280 | tf_op jit(solution)/shard_map/ppermute | solution.py:360
  136.5 10.0 %collective-permute-done.42.refs_4_ = bf16[128,2048]{1,0:T(8,128)(2,1)S(1)} collective-permute-done((bf16[128,2048]{1,0:T(8,128)(2,1)S(1)}, bf16[128,2048]{1,0:T(8,128)(2,1)S(1)}, u32[]{:S(2)}, u32[]{:S(2)}) %collective-permute-start.42) | collective-permute-done | bytes 524320 | tf_op jit(solution)/shard_map/ppermute | solution.py:424
  150.2 3.4 %collective-permute-start.46 = (bf16[128,2048]{1,0:T(8,128)(2,1)S(1)}, bf16[128,2048]{1,0:T(8,128)(2,1)S(1)}, u32[]{:S(2)}, u32[]{:S(2)}) collective-permute-start(bf16[128,2048]{1,0:T(8,128)(2,1)S(1)} %collective-permute-done.42.refs_4_), channel_id=1, source_target_pairs={{0,16},{12,28},{16,0},{28,12},{1,17},{13,29},{17,1},{29,13},{2,18}... | collective-permute-start | bytes 1572872 | tf_op jit(solution)/shard_map/ppermute | solution.py:412
  153.7 4.1 %collective-permute-done.32.refs_6_ = bf16[128,2048]{1,0:T(8,128)(2,1)S(1)} collective-permute-done((bf16[128,2048]{1,0:T(8,128)(2,1)S(1)}, bf16[128,2048]{1,0:T(8,128)(2,1)S(1)}, u32[]{:S(2)}, u32[]{:S(2)}) %collective-permute-start.32) | collective-permute-done | bytes 524320 | tf_op jit(solution)/shard_map/ppermute | solution.py:424
  158.4 4.4 %rebuild.5 = (f32[768,2048]{1,0:T(8,128)S(1)}, f32[104,128]{1,0:T(8,128)S(1)}) custom-call(s32[7]{0:T(128)S(1)} %stack.23.refs_0_, f32[104,128]{1,0:T(8,128)S(1)} %get-tuple-element.134.refs_1_, f32[104,128]{1,0:T(8,128)S(1)} %collective-permute-done.29.refs_2_, f32[104,128]{1,0:T(8,128)S(1)} %collective-permute-done.30.refs_3_, ...), custom_call_target="tpu_custom_call", output_to_operand_aliasing={{0}: (6, {})} | custom-call | flops 3221225472 | bytes 6291456 | tf_op jit(solution)/shard_map/rebuild/pallas_call | solution.py:327
  169.8 4.9 %project.9 = (f32[104,128]{1,0:T(8,128)S(1)}, bf16[1024,2048]{1,0:T(8,128)(2,1)S(1)}) custom-call(s32[7]{0:T(128)S(1)} %stack.23.refs_0_, bf16[896,2048]{1,0:T(8,128)(2,1)S(1)} %stage.1.refs_1_, bf16[128,2048]{1,0:T(8,128)(2,1)S(1)} %collective-permute-done.7.refs_2_, bf16[128,2048]{1,0:T(8,128)(2,1)S(1)} %collective-permute-done.1.refs_3_, ...), custom_call_target="tpu_custom_call" | custom-call | flops 3556769792 | bytes 4194304 | tf_op jit(solution)/shard_map/project/pallas_call | solution.py:276
  175.6 3.8 %project.7 = (f32[848,256]{1,0:T(8,128)S(1)}, bf16[1024,2048]{1,0:T(8,128)(2,1)S(1)}) custom-call(s32[7]{0:T(128)S(1)} %stack.23.refs_0_, bf16[896,2048]{1,0:T(8,128)(2,1)S(1)} %stage.1.refs_1_, bf16[128,2048]{1,0:T(8,128)(2,1)S(1)} %collective-permute-done.25.refs_2_, bf16[128,2048]{1,0:T(8,128)(2,1)S(1)} %collective-permute-done.8.refs_3_, ...), custom_call_target="tpu_custom_call" | custom-call | flops 2667577344 | bytes 3145728 | tf_op jit(solution)/shard_map/project/pallas_call | solution.py:276
  179.4 4.5 %collective-permute-done.39.refs_2_ = bf16[128,2048]{1,0:T(8,128)(2,1)S(1)} collective-permute-done((bf16[128,2048]{1,0:T(8,128)(2,1)S(1)}, bf16[128,2048]{1,0:T(8,128)(2,1)S(1)}, u32[]{:S(2)}, u32[]{:S(2)}) %collective-permute-start.39) | collective-permute-done | bytes 524320 | tf_op jit(solution)/shard_map/ppermute | solution.py:412
  188.2 4.4 %rebuild.6 = (f32[768,2048]{1,0:T(8,128)S(1)}, f32[104,128]{1,0:T(8,128)S(1)}) custom-call(s32[7]{0:T(128)S(1)} %stack.23.refs_0_, f32[104,128]{1,0:T(8,128)S(1)} %get-tuple-element.175.refs_1_, f32[104,128]{1,0:T(8,128)S(1)} %collective-permute-done.51.refs_2_, f32[104,128]{1,0:T(8,128)S(1)} %collective-permute-done.52.refs_3_, ...), custom_call_target="tpu_custom_call", output_to_operand_aliasing={{0}: (6, {})} | custom-call | flops 3221225472 | bytes 6291456 | tf_op jit(solution)/shard_map/rebuild/pallas_call | solution.py:327
  192.7 5.5 %rebuild.7 = (f32[768,2048]{1,0:T(8,128)}, f32[768,64]{1,0:T(8,128)S(1)}) custom-call(s32[7]{0:T(128)S(1)} %stack.23.refs_0_, f32[104,128]{1,0:T(8,128)S(1)} %get-tuple-element.163.refs_1_, f32[104,128]{1,0:T(8,128)S(1)} %collective-permute-done.48.refs_2_, f32[104,128]{1,0:T(8,128)S(1)} %collective-permute-done.49.refs_3_, ...), custom_call_target="tpu_custom_call" | custom-call | flops 3221225472 | bytes 6291456 | tf_op jit(solution)/shard_map/rebuild/pallas_call | solution.py:327
  (115 shorter events, 77.3 us)
Async XLA Ops:
  2.7 21.5 %collective-permute-start.5 = (bf16[64,2048]{1,0:T(8,128)(2,1)}, bf16[64,2048]{1,0:T(8,128)(2,1)S(1)}, u32[]{:S(2)}, u32[]{:S(2)}) collective-permute-start(bf16[64,2048]{1,0:T(8,128)(2,1)} %get-tuple-element.189), channel_id=1, source_target_pairs={{0,4},{4,8},{8,12},{1,5},{5,9},{9,13},{2,6},{6,10},{10,14},{3,7},{... | collective-permute-start | bytes 786440 | tf_op jit(solution)/shard_map/ppermute | solution.py:373
  11.9 19.4 %collective-permute-start.11 = (bf16[128,2048]{1,0:T(8,128)(2,1)}, bf16[128,2048]{1,0:T(8,128)(2,1)}, u32[]{:S(2)}, u32[]{:S(2)}) collective-permute-start(bf16[128,2048]{1,0:T(8,128)(2,1)} %get-tuple-element.184), channel_id=1, source_target_pairs={{0,4},{4,0},{8,12},{12,8},{1,5},{5,1},{9,13},{13,9},{2,6},{6,2},{1... | collective-permute-start | bytes 1572872 | tf_op jit(solution)/shard_map/ppermute | solution.py:420
  16.0 25.6 %collective-permute-start = (bf16[128,2048]{1,0:T(8,128)(2,1)}, bf16[128,2048]{1,0:T(8,128)(2,1)}, u32[]{:S(2)}, u32[]{:S(2)}) collective-permute-start(bf16[128,2048]{1,0:T(8,128)(2,1)} %get-tuple-element.186), channel_id=1, source_target_pairs={{0,4},{4,0},{8,12},{12,8},{1,5},{5,1},{9,13},{13,9},{2,6},{6,2},{1... | collective-permute-start | bytes 1572872 | tf_op jit(solution)/shard_map/ppermute | solution.py:420
  24.2 18.9 %collective-permute-start.1 = (bf16[128,2048]{1,0:T(8,128)(2,1)}, bf16[128,2048]{1,0:T(8,128)(2,1)S(1)}, u32[]{:S(2)}, u32[]{:S(2)}) collective-permute-start(bf16[128,2048]{1,0:T(8,128)(2,1)} %get-tuple-element.186), channel_id=1, source_target_pairs={{4,8},{8,4},{5,9},{9,5},{6,10},{10,6},{7,11},{11,7},{20,24},{24,20... | collective-permute-start | bytes 1572872 | tf_op jit(solution)/shard_map/ppermute | solution.py:422
  31.3 21.4 %collective-permute-start.13 = (bf16[128,2048]{1,0:T(8,128)(2,1)S(1)}, bf16[128,2048]{1,0:T(8,128)(2,1)S(1)}, u32[]{:S(2)}, u32[]{:S(2)}) collective-permute-start(bf16[128,2048]{1,0:T(8,128)(2,1)S(1)} %copy-done.3), channel_id=1, source_target_pairs={{0,4},{4,0},{8,12},{12,8},{1,5},{5,1},{9,13},{13,9},{2,6},{6,2},{1... | collective-permute-start | bytes 1572872 | tf_op jit(solution)/shard_map/ppermute | solution.py:420
  33.4 20.8 %collective-permute-start.14 = (bf16[128,2048]{1,0:T(8,128)(2,1)S(1)}, bf16[128,2048]{1,0:T(8,128)(2,1)S(1)}, u32[]{:S(2)}, u32[]{:S(2)}) collective-permute-start(bf16[128,2048]{1,0:T(8,128)(2,1)S(1)} %copy-done.3), channel_id=1, source_target_pairs={{4,8},{8,4},{5,9},{9,5},{6,10},{10,6},{7,11},{11,7},{20,24},{24,20... | collective-permute-start | bytes 1572872 | tf_op jit(solution)/shard_map/ppermute | solution.py:422
  34.1 20.1 %collective-permute-start.15 = (bf16[128,2048]{1,0:T(8,128)(2,1)}, bf16[128,2048]{1,0:T(8,128)(2,1)S(1)}, u32[]{:S(2)}, u32[]{:S(2)}) collective-permute-start(bf16[128,2048]{1,0:T(8,128)(2,1)} %collective-permute-done.11.refs_3_), channel_id=1, source_target_pairs={{0,16},{12,28},{4,20},{8,24},{16,0},{28,12},{20,4},{24,8},{1,17},{... | collective-permute-start | bytes 1572872 | tf_op jit(solution)/shard_map/ppermute | solution.py:412
  46.8 18.6 %collective-permute-start.3 = (bf16[128,2048]{1,0:T(8,128)(2,1)S(1)}, bf16[128,2048]{1,0:T(8,128)(2,1)S(1)}, u32[]{:S(2)}, u32[]{:S(2)}) collective-permute-start(bf16[128,2048]{1,0:T(8,128)(2,1)S(1)} %copy-done.2), channel_id=1, source_target_pairs={{4,8},{8,4},{5,9},{9,5},{6,10},{10,6},{7,11},{11,7},{20,24},{24,20... | collective-permute-start | bytes 1572872 | tf_op jit(solution)/shard_map/ppermute | solution.py:422
  54.2 20.9 %collective-permute-start.19 = (bf16[128,2048]{1,0:T(8,128)(2,1)}, bf16[128,2048]{1,0:T(8,128)(2,1)S(1)}, u32[]{:S(2)}, u32[]{:S(2)}) collective-permute-start(bf16[128,2048]{1,0:T(8,128)(2,1)} %collective-permute-done.12.refs_5_), channel_id=1, source_target_pairs={{4,0},{8,12},{5,1},{9,13},{6,2},{10,14},{7,3},{11,15},{20,16},{24,... | collective-permute-start | bytes 1572872 | tf_op jit(solution)/shard_map/ppermute | solution.py:424
  55.5 25.4 %collective-permute-start.20 = (bf16[128,2048]{1,0:T(8,128)(2,1)}, bf16[128,2048]{1,0:T(8,128)(2,1)S(1)}, u32[]{:S(2)}, u32[]{:S(2)}) collective-permute-start(bf16[128,2048]{1,0:T(8,128)(2,1)} %collective-permute-done.11.refs_3_), channel_id=1, source_target_pairs={{4,8},{8,4},{5,9},{9,5},{6,10},{10,6},{7,11},{11,7},{20,24},{24,20... | collective-permute-start | bytes 1572872 | tf_op jit(solution)/shard_map/ppermute | solution.py:422
  65.4 19.5 %collective-permute-start.7 = (bf16[128,2048]{1,0:T(8,128)(2,1)S(1)}, bf16[128,2048]{1,0:T(8,128)(2,1)S(1)}, u32[]{:S(2)}, u32[]{:S(2)}) collective-permute-start(bf16[128,2048]{1,0:T(8,128)(2,1)S(1)} %collective-permute-done.1.refs_3_), channel_id=1, source_target_pairs={{4,0},{8,12},{5,1},{9,13},{6,2},{10,14},{7,3},{11,15},{20,16},{24,... | collective-permute-start | bytes 1572872 | tf_op jit(solution)/shard_map/ppermute | solution.py:424
  99.5 18.5 %collective-permute-start.33 = (bf16[128,2048]{1,0:T(8,128)(2,1)S(1)}, bf16[128,2048]{1,0:T(8,128)(2,1)S(1)}, u32[]{:S(2)}, u32[]{:S(2)}) collective-permute-start(bf16[128,2048]{1,0:T(8,128)(2,1)S(1)} %collective-permute-done.14.refs_9_), channel_id=1, source_target_pairs={{4,0},{8,12},{5,1},{9,13},{6,2},{10,14},{7,3},{11,15},{20,16},{24,... | collective-permute-start | bytes 1572872 | tf_op jit(solution)/shard_map/ppermute | solution.py:424
  102.1 18.7 %collective-permute-start.35 = (bf16[128,2048]{1,0:T(8,128)(2,1)}, bf16[128,2048]{1,0:T(8,128)(2,1)S(1)}, u32[]{:S(2)}, u32[]{:S(2)}) collective-permute-start(bf16[128,2048]{1,0:T(8,128)(2,1)} %collective-permute-done.12.refs_5_), channel_id=1, source_target_pairs={{4,20},{8,24},{20,4},{24,8},{5,21},{9,25},{21,5},{25,9},{6,22},{10... | collective-permute-start | bytes 1572872 | tf_op jit(solution)/shard_map/ppermute | solution.py:412
  102.8 18.9 %collective-permute-start.36 = (bf16[128,2048]{1,0:T(8,128)(2,1)S(1)}, bf16[128,2048]{1,0:T(8,128)(2,1)S(1)}, u32[]{:S(2)}, u32[]{:S(2)}) collective-permute-start(bf16[128,2048]{1,0:T(8,128)(2,1)S(1)} %collective-permute-done.19.refs_4_), channel_id=1, source_target_pairs={{0,16},{12,28},{16,0},{28,12},{1,17},{13,29},{17,1},{29,13},{2,18}... | collective-permute-start | bytes 1572872 | tf_op jit(solution)/shard_map/ppermute | solution.py:412
  110.4 18.4 %collective-permute-start.25 = (bf16[128,2048]{1,0:T(8,128)(2,1)S(1)}, bf16[128,2048]{1,0:T(8,128)(2,1)S(1)}, u32[]{:S(2)}, u32[]{:S(2)}) collective-permute-start(bf16[128,2048]{1,0:T(8,128)(2,1)S(1)} %collective-permute-done.8.refs_3_), channel_id=1, source_target_pairs={{4,0},{8,12},{5,1},{9,13},{6,2},{10,14},{7,3},{11,15},{20,16},{24,... | collective-permute-start | bytes 1572872 | tf_op jit(solution)/shard_map/ppermute | solution.py:424
  125.8 20.7 %collective-permute-start.42 = (bf16[128,2048]{1,0:T(8,128)(2,1)S(1)}, bf16[128,2048]{1,0:T(8,128)(2,1)S(1)}, u32[]{:S(2)}, u32[]{:S(2)}) collective-permute-start(bf16[128,2048]{1,0:T(8,128)(2,1)S(1)} %collective-permute-done.20.refs_5_), channel_id=1, source_target_pairs={{4,0},{8,12},{5,1},{9,13},{6,2},{10,14},{7,3},{11,15},{20,16},{24,... | collective-permute-start | bytes 1572872 | tf_op jit(solution)/shard_map/ppermute | solution.py:424
  128.8 20.1 %collective-permute-start.43 = (bf16[128,2048]{1,0:T(8,128)(2,1)S(1)}, bf16[128,2048]{1,0:T(8,128)(2,1)S(1)}, u32[]{:S(2)}, u32[]{:S(2)}) collective-permute-start(bf16[128,2048]{1,0:T(8,128)(2,1)S(1)} %collective-permute-done.14.refs_9_), channel_id=1, source_target_pairs={{4,20},{8,24},{20,4},{24,8},{5,21},{9,25},{21,5},{25,9},{6,22},{10... | collective-permute-start | bytes 1572872 | tf_op jit(solution)/shard_map/ppermute | solution.py:412
  129.5 19.4 %collective-permute-start.44 = (bf16[128,2048]{1,0:T(8,128)(2,1)S(1)}, bf16[128,2048]{1,0:T(8,128)(2,1)S(1)}, u32[]{:S(2)}, u32[]{:S(2)}) collective-permute-start(bf16[128,2048]{1,0:T(8,128)(2,1)S(1)} %collective-permute-done.33.refs_8_), channel_id=1, source_target_pairs={{0,16},{12,28},{16,0},{28,12},{1,17},{13,29},{17,1},{29,13},{2,18}... | collective-permute-start | bytes 1572872 | tf_op jit(solution)/shard_map/ppermute | solution.py:412
  134.5 23.3 %collective-permute-start.32 = (bf16[128,2048]{1,0:T(8,128)(2,1)S(1)}, bf16[128,2048]{1,0:T(8,128)(2,1)S(1)}, u32[]{:S(2)}, u32[]{:S(2)}) collective-permute-start(bf16[128,2048]{1,0:T(8,128)(2,1)S(1)} %collective-permute-done.22.refs_7_), channel_id=1, source_target_pairs={{4,0},{8,12},{5,1},{9,13},{6,2},{10,14},{7,3},{11,15},{20,16},{24,... | collective-permute-start | bytes 1572872 | tf_op jit(solution)/shard_map/ppermute | solution.py:424
  135.8 27.1 %collective-permute-start.37 = (bf16[128,2048]{1,0:T(8,128)(2,1)S(1)}, bf16[128,2048]{1,0:T(8,128)(2,1)S(1)}, u32[]{:S(2)}, u32[]{:S(2)}) collective-permute-start(bf16[128,2048]{1,0:T(8,128)(2,1)S(1)} %collective-permute-done.8.refs_3_), channel_id=1, source_target_pairs={{4,20},{8,24},{20,4},{24,8},{5,21},{9,25},{21,5},{25,9},{6,22},{10... | collective-permute-start | bytes 1572872 | tf_op jit(solution)/shard_map/ppermute | solution.py:412
  148.9 19.6 %collective-permute-start.45 = (bf16[128,2048]{1,0:T(8,128)(2,1)S(1)}, bf16[128,2048]{1,0:T(8,128)(2,1)S(1)}, u32[]{:S(2)}, u32[]{:S(2)}) collective-permute-start(bf16[128,2048]{1,0:T(8,128)(2,1)S(1)} %collective-permute-done.34.refs_9_), channel_id=1, source_target_pairs={{4,0},{8,12},{5,1},{9,13},{6,2},{10,14},{7,3},{11,15},{20,16},{24,... | collective-permute-start | bytes 1572872 | tf_op jit(solution)/shard_map/ppermute | solution.py:424
  150.2 24.5 %collective-permute-start.46 = (bf16[128,2048]{1,0:T(8,128)(2,1)S(1)}, bf16[128,2048]{1,0:T(8,128)(2,1)S(1)}, u32[]{:S(2)}, u32[]{:S(2)}) collective-permute-start(bf16[128,2048]{1,0:T(8,128)(2,1)S(1)} %collective-permute-done.42.refs_4_), channel_id=1, source_target_pairs={{0,16},{12,28},{16,0},{28,12},{1,17},{13,29},{17,1},{29,13},{2,18}... | collective-permute-start | bytes 1572872 | tf_op jit(solution)/shard_map/ppermute | solution.py:412
  163.2 20.6 %collective-permute-start.39 = (bf16[128,2048]{1,0:T(8,128)(2,1)S(1)}, bf16[128,2048]{1,0:T(8,128)(2,1)S(1)}, u32[]{:S(2)}, u32[]{:S(2)}) collective-permute-start(bf16[128,2048]{1,0:T(8,128)(2,1)S(1)} %collective-permute-done.32.refs_6_), channel_id=1, source_target_pairs={{0,16},{12,28},{16,0},{28,12},{1,17},{13,29},{17,1},{29,13},{2,18}... | collective-permute-start | bytes 1572872 | tf_op jit(solution)/shard_map/ppermute | solution.py:412
  165.6 18.3 %collective-permute-start.40 = (bf16[128,2048]{1,0:T(8,128)(2,1)S(1)}, bf16[128,2048]{1,0:T(8,128)(2,1)S(1)}, u32[]{:S(2)}, u32[]{:S(2)}) collective-permute-start(bf16[128,2048]{1,0:T(8,128)(2,1)S(1)} %collective-permute-done.22.refs_7_), channel_id=1, source_target_pairs={{4,20},{8,24},{20,4},{24,8},{5,21},{9,25},{21,5},{25,9},{6,22},{10... | collective-permute-start | bytes 1572872 | tf_op jit(solution)/shard_map/ppermute | solution.py:412
  (37 other events, 460.8 us)

commit v3 on v2

--- a/solution.py
+++ b/solution.py
@@ -8,11 +8,13 @@
 from jax.sharding import PartitionSpec as P
 
 LANES = 128
+CUTS = (1, 1, 1, 1)
+EXTENDED = 1
 WIDE = 256
 TILE = 512
 HALO = 64
 VMEM_BYTES = 20 * 1024 * 1024
-DAY, GRP, MIDDLE_FLAG, BLOCKS = 0, 1, 2, 3
+DAY, GRP, MIDDLE_FLAG, EVEN, BLOCKS = 0, 1, 2, 3, 4
 
 ENDS, MIDS = (0, 3), (1, 2)
 PAIRED = ((0, 1), (1, 0), (2, 3), (3, 2))
@@ -53,10 +55,10 @@
         scratch[pl.ds(groups + i, count - 1, stride=groups), :] = plane
 
 
-def unpack_modes(blocks, out, modes, skip):
+def unpack_modes(blocks, out, scratch, modes, skip):
     groups = LANES // modes
-    rows = out.shape[0] // groups
-    wide = out.shape[1]
+    rows = out.shape[1] // groups
+    wide = out.shape[0]
     placed = []
     for index, packed in blocks:
         placed.append((index, pltpu.roll(packed, index * modes, 1)))
@@ -68,16 +70,18 @@
             value = pltpu.roll(packed, shift, 1) if shift else packed
             value = jnp.where(group == index, value, 0.0)
             total = value if total is None else total + value
-        out[pl.ds(s, rows, stride=groups), :] = total[skip // groups :, :wide]
+        scratch[pl.ds(s, rows, stride=groups), :] = total[skip // groups :]
+    out[...] = scratch[: out.shape[1], :].T[:wide]
 
 
 def load_pieces(plan, refs, bank, sems, meta):
     waits = []
-    for i, (row, rows, start, sources) in enumerate(plan):
+    for i, (row, rows, sources) in enumerate(plan):
         target = bank.at[pl.ds(row, rows), :]
 
         def copy_of(source):
-            return pltpu.make_async_copy(refs[source].at[pl.ds(start, rows), :], target, sems.at[i])
+            ref, start = source
+            return pltpu.make_async_copy(refs[ref].at[pl.ds(start, rows), :], target, sems.at[i])
 
         if len(sources) == 1:
             copy_of(sources[0]).start()
@@ -100,16 +104,24 @@
     return pl.multiple_of((side * (count // 2) + index) * lags, 16)
 
 
-def stage_kernel(behind, series, ahead, out, sems):
+def stage_kernel(starts, meta, paired, series, other, out, sems):
     days = series.shape[0]
-    copies = [
-        pltpu.make_async_copy(behind, out.at[pl.ds(0, HALO), :], sems.at[0]),
-        pltpu.make_async_copy(series, out.at[pl.ds(HALO, days), :], sems.at[1]),
-        pltpu.make_async_copy(ahead, out.at[pl.ds(HALO + days, HALO), :], sems.at[2]),
-    ]
-    for copy in copies:
-        copy.start()
-    for copy in copies:
+    places = (pl.ds(0, HALO), pl.ds(HALO + days, HALO))
+    middle = pltpu.make_async_copy(series, out.at[pl.ds(HALO, days), :], sems.at[0])
+    middle.start()
+    waits = [middle]
+    for i, (ref, start) in enumerate(zip((paired, other), starts)):
+        for even in (0, 1):
+            copy = pltpu.make_async_copy(
+                ref.at[pl.ds(start, HALO), :], out.at[places[even ^ i], :], sems.at[i + 1]
+            )
+
+            @pl.when(meta[EVEN] == even)
+            def _():
+                copy.start()
+
+        waits.append(copy)
+    for copy in waits:
         copy.wait()
 
 
@@ -178,6 +190,8 @@
     values = []
     for block in range(n_blocks):
         level = [ref[...] for ref in sums[block]]
+        if len(level) == 1:
+            level = [level[0][i] for i in range(level[0].shape[0])]
         while len(level) > 1:
             level = [level[i] + level[i + 1] for i in range(0, len(level), 2)]
         packed = level[0]
@@ -221,7 +235,7 @@
             rec_out[:, tile] = total
     if last:
         values = [ref[...] for ref in olds] + values
-        unpack_modes([(meta[BLOCKS + i], v) for i, v in zip(order, values)], pcs_done, modes, HALO)
+        unpack_modes([(meta[BLOCKS + i], v) for i, v in zip(order, values)], pcs_done, scratch, modes, HALO)
         copies.append(pltpu.make_async_copy(pcs_done, pcs_out, sems.at[len(copies)]))
         copies[-1].start()
         for copy in copies:
@@ -236,28 +250,99 @@
     return pltpu.with_memory_space_constraint(x, pltpu.VMEM)
 
 
+def left(x):
+    return pltpu.with_memory_space_constraint(x, pltpu.HBM)
+
+
 def flatten(pieces, row):
     arrays, plan = [], []
-    for choices in pieces:
-        ids = tuple(range(len(arrays), len(arrays) + len(choices)))
-        arrays.extend(choices)
-        rows = choices[0].shape[0]
-        plan.append((row, rows, 0, ids))
+    for rows, choices in pieces:
+        sources = []
+        for array, start in choices:
+            same = [i for i, other in enumerate(arrays) if other is array]
+            if not same:
+                arrays.append(array)
+            sources.append((same[0] if same else len(arrays) - 1, start))
+        plan.append((row, rows, sources))
         row += rows
     return plan, arrays
 
 
-def stage(behind, series, ahead):
+def stage(meta, paired, series, other, starts=(0, 0)):
     days, cells = series.shape
     return pl.pallas_call(
-        stage_kernel,
+        functools.partial(stage_kernel, starts),
         out_shape=pltpu.VMEM((days + 2 * HALO, cells), jnp.bfloat16),
-        in_specs=[space(pltpu.HBM)] * 3,
+        in_specs=[space(pltpu.SMEM)] + [space(pltpu.HBM)] * 3,
         out_specs=space(pltpu.VMEM),
         scratch_shapes=[pltpu.SemaphoreType.DMA((3,))],
         compiler_params=pltpu.CompilerParams(vmem_limit_bytes=VMEM_BYTES),
         name="stage",
-    )(behind, series, ahead)
+    )(meta, paired, series, other)
+
+
+def cut_kernel(pieces, extended, half, meta, bank, series, *refs):
+    outs, sems = refs[:-1], refs[-1]
+    days = series.shape[0]
+    copies = []
+    for i, out in enumerate(outs):
+        edge = i - extended if extended <= i < extended + 2 else None
+        start, size = pieces[i if i <= extended else i - 1]
+        first = pl.multiple_of(meta[GRP] * half + start, 16)
+        copies.append(
+            pltpu.make_async_copy(bank.at[pl.ds(first, size), :], out.at[pl.ds(0, size), :], sems.at[i])
+        )
+        copies[-1].start()
+        if edge is not None:
+            tail = meta[EVEN] if edge == 0 else (meta[DAY] == days).astype(jnp.int32)
+            first = pl.multiple_of(tail * (days - HALO), 16)
+            copies.append(
+                pltpu.make_async_copy(
+                    series.at[pl.ds(first, HALO), :], out.at[pl.ds(size, HALO), :], sems.at[len(outs) + edge]
+                )
+            )
+            copies[-1].start()
+    for copy in copies:
+        copy.wait()
+
+
+def cut(meta, bank, series, pieces, extended, half):
+    cells = bank.shape[1]
+    rows = [size for _, size in pieces]
+    rows = rows[:extended] + [rows[extended] + HALO] * 2 + rows[extended + 1 :]
+    return pl.pallas_call(
+        functools.partial(cut_kernel, pieces, extended, half),
+        out_shape=[jax.ShapeDtypeStruct((size, cells), bank.dtype) for size in rows],
+        in_specs=[space(pltpu.SMEM)] + [space(pltpu.HBM)] * 2,
+        out_specs=[space(pltpu.HBM)] * len(rows),
+        scratch_shapes=[pltpu.SemaphoreType.DMA((len(rows) + 2,))],
+        compiler_params=pltpu.CompilerParams(vmem_limit_bytes=VMEM_BYTES),
+        name="cut",
+    )(meta, left(bank), left(series))
+
+
+def trim_kernel(*refs):
+    sems = refs[-1]
+    count = len(refs) // 2
+    copies = []
+    for i in range(count):
+        out = refs[count + i]
+        copies.append(pltpu.make_async_copy(refs[i].at[pl.ds(0, out.shape[0]), :], out, sems.at[i]))
+        copies[-1].start()
+    for copy in copies:
+        copy.wait()
+
+
+def trim(arrays, rows):
+    return pl.pallas_call(
+        trim_kernel,
+        out_shape=[jax.ShapeDtypeStruct((rows, x.shape[1]), x.dtype) for x in arrays],
+        in_specs=[space(pltpu.HBM)] * len(arrays),
+        out_specs=[space(pltpu.HBM)] * len(arrays),
+        scratch_shapes=[pltpu.SemaphoreType.DMA((len(arrays),))],
+        compiler_params=pltpu.CompilerParams(vmem_limit_bytes=VMEM_BYTES),
+        name="trim",
+    )(*arrays)
 
 
 def project(meta, source, pieces, parts, modes, width, before=None, finish=True):
@@ -302,7 +387,7 @@
     parts = [part for block in blocks for part in block[3]]
     sums = [value for block in blocks for value in block[1]]
     cells = banks[0].shape[1]
-    packed = sums[0].shape
+    packed = sums[0].shape[-2:]
     has_in = so_far is not None
     olds = [value for _, value in old] if last else []
     order = tuple([index for index, _ in old] + [block[0] for block in blocks]) if last else ()
@@ -312,11 +397,11 @@
     ]
     if last:
         out_shape = [jax.ShapeDtypeStruct((days, cells), jnp.float32)]
-        out_shape += [jax.ShapeDtypeStruct((days, all_modes), jnp.float32)]
+        out_shape += [jax.ShapeDtypeStruct((all_modes, days), jnp.float32)]
         out_specs = [space(pltpu.HBM), space(pltpu.HBM)]
         scratch += [
             pltpu.VMEM((days, cells), jnp.float32),
-            pltpu.VMEM((days, all_modes), jnp.float32),
+            pltpu.VMEM((all_modes, days), jnp.float32),
             pltpu.SemaphoreType.DMA((cells // TILE + 1,)),
         ]
     else:
@@ -370,8 +455,7 @@
     grp = lax.axis_index("grp").astype(jnp.int32)
     n_parts = width * modes // WIDE
     bank = eofs.reshape(width * modes, cells)
-    behind = lax.ppermute(series[days - HALO :], "day", [(i, i + 1) for i in range(n - 1)])
-    ahead = lax.ppermute(series[:HALO], "day", [(i + 1, i) for i in range(n - 1)])
+
     middle = ((day > 0) & (day < n - 1)).astype(jnp.int32)
     whole = list(range(n_parts))
     shape = dict(modes=modes, width=width)
@@ -379,30 +463,39 @@
 
     if n != 4 or lax.axis_size("grp") != 2 or n_parts != 4:
         every = lax.all_gather(bank, "day", axis=0, tiled=False)
-        meta = jnp.stack([day * days, grp, middle] + [jnp.int32(i) for i in range(n)])
-        source = stage(behind, series, ahead)
+        meta = jnp.stack([day * days, grp, middle, 1 - day % 2] + [jnp.int32(i) for i in range(n)])
+        behind = lax.ppermute(series[days - HALO :], "day", [(i, i + 1) for i in range(n - 1)])
+        ahead = lax.ppermute(series[:HALO], "day", [(i + 1, i) for i in range(n - 1)])
+        even = day % 2 == 0
+        source = stage(meta, jnp.where(even, ahead, behind), series, jnp.where(even, behind, ahead))
         rec, old = None, []
         for block in range(n):
-            pieces = [(every[block],)]
+            pieces = [(width * modes, [(every[block], 0)])]
             packed, bank = project(meta, source, pieces, whole, **shape)
             rec, small = rebuild(
                 meta, [(block, exchange(packed), bank, whole)], so_far=rec, old=old, last=block == n - 1, **shape, **rest
             )
             old.append((block, small))
-        return small, rec
-
-    def table(values):
-        return jnp.asarray(values, jnp.int32)[day]
-
-    meta = jnp.stack(
-        [day * days, grp, middle, day, table([1, 0, 3, 2]), table([2, 2, 1, 1]), table([3, 3, 0, 0])]
-    )
-    cuts = 4
+        return small.T, rec
+
+    entry = lax.broadcasted_iota(jnp.int32, (8,), 0)
+    meta = jnp.zeros((8,), jnp.int32)
+    low = day // 2
+    for i, value in enumerate([day * days, grp, middle, 1 - day % 2, day, day + 1 - 2 * (day % 2), 2 - low, 3 - 3 * low]):
+        meta = jnp.where(entry == i, value, meta)
     half = width * modes // 2
-    size = half // cuts
-    first = lax.dynamic_slice_in_dim(bank, grp * half, half, axis=0)
-    held = {("own", i): first[i * size : (i + 1) * size] for i in range(cuts)}
-    held["behind"], held["ahead"] = behind, ahead
+    cuts = CUTS
+    pieces, row = [], 0
+    for size in cuts:
+        pieces.append((row * half // sum(cuts), size * half // sum(cuts)))
+        row += size
+    held = {}
+    parts_out = cut(meta, bank, series, pieces, EXTENDED, half)
+    for i in range(len(pieces)):
+        held["own", i] = parts_out[i if i <= EXTENDED else i + 1]
+    extended = {"p1": parts_out[EXTENDED], "p2": parts_out[EXTENDED + 1]}
+    n_pieces = len(pieces)
+    last_piece = n_pieces - 1
     sent_from = {
         "p1": "own", "p2": "own", "q1": "p2", "q2": "p1", "f": "q2",
         "yp1": "p1", "yp2": "p2", "yq1": "q1", "yq2": "q2", "yf": "f", "h": "yp1", "g": "h",
@@ -428,30 +521,38 @@
     arrivals = {"a": ("p1",), "b": ("q1", "p2"), "c": ("f", "q2")}
     place = {"own": 0, "a": 1, "b": 2, "c": 3}
 
-    def pieces_of(block, which=range(2 * cuts)):
+    def pieces_of(block, which=range(4)):
         if block == "own":
-            return [(bank,)]
+            return [(width * modes, [(bank, 0)])]
+        names = arrivals[block]
         picked = []
-        for i in which:
-            names = arrivals[block] if i < cuts else ["y" + name for name in arrivals[block]]
-            if block == "c" and i == 2 * cuts - 1:
-                names = ("g", "h")
-            picked.append(tuple(held[name, i % cuts] for name in names))
+        for side in ("", "y"):
+            for i, (start, size) in enumerate(pieces):
+                ours = [side + name for name in names]
+                if block == "c" and side == "y":
+                    ours = ["g" if i == last_piece else "yf", "h"]
+                choices = [held[name, i] for name in ours]
+                for chunk in range(half // WIDE):
+                    first = max(start, chunk * WIDE)
+                    end = min(start + size, (chunk + 1) * WIDE)
+                    if first < end and (side == "y") * (half // WIDE) + chunk in which:
+                        picked.append((end - first, [(array, first - start) for array in choices]))
         return picked
 
     def run(kind, which):
         if kind == "stage":
-            held["source"] = stage(held["behind"], series, held["ahead"])
+            starts = (pieces[EXTENDED][1],) * 2
+            held["source"] = stage(meta, held["long", "p1"], series, held["long", "p2"], starts)
         elif kind == "project":
             source = held["source"]
             if which == "c1":
                 held["acc"], held["bank", "c"] = project(
-                    meta, source, pieces_of("c", range(6)), halves[:3], finish=False, **shape
+                    meta, source, pieces_of("c", (0, 1)), halves[:2], finish=False, **shape
                 )
             elif which == "c2":
                 before = (held["acc"], held["bank", "c"])
                 held["packed", "c"], held["bank", "c"] = project(
-                    meta, source, pieces_of("c", range(6, 8)), halves[3:], before=before, **shape
+                    meta, source, pieces_of("c", (2, 3)), halves[2:], before=before, **shape
                 )
             else:
                 parts = whole if which == "own" else halves
@@ -459,12 +560,14 @@
                     meta, source, pieces_of(which), parts, **shape
                 )
         elif kind == "exchange":
-            for i, array in enumerate(exchange(held["packed", which])):
-                held["sum", which, i] = array
+            if which == "c":
+                held["sum", which] = exchange(held["packed", which])
+            else:
+                held["sum", which] = [lax.all_gather(held["packed", which], "cell", axis=0)]
         else:
             blocks = []
             for block in which:
-                sums = [held["sum", block, i] for i in range(lax.axis_size("cell"))]
+                sums = held["sum", block]
                 parts = whole if block == "own" else halves
                 blocks.append((place[block], sums, held["bank", block], parts))
             last = "c" in which
@@ -477,52 +580,54 @@
                 held.update({("old", block): value for block, value in zip(which, done[1:])})
 
     tasks = {
-        2: [("stage", None), ("project", "own")],
-        3: [("exchange", "own")],
+        3: [("stage", None), ("project", "own")],
+        4: [("exchange", "own")],
         5: [("rebuild", ("own",))],
         7: [("project", "a")],
         8: [("exchange", "a")],
-        10: [("rebuild", ("a",))],
-        11: [("project", "b")],
-        12: [("exchange", "b"), ("project", "c1")],
-        13: [("rebuild", ("b",)), ("project", "c2")],
-        14: [("exchange", "c")],
-        15: [("rebuild", ("c",))],
+        13: [("project", "b"), ("exchange", "b"), ("project", "c1"), ("rebuild", ("a",))],
+        14: [("project", "c2")],
+        15: [("exchange", "c"), ("rebuild", ("b",))],
+        16: [("rebuild", ("c",))],
     }
-
     lag = 2
+    along = [[("p1", i), ("p2", i)] for i in range(n_pieces)]
+    along += [[("q1", i), ("q2", i)] for i in range(n_pieces)]
+    along += [[("f", i), ("h", (i - 1) % n_pieces)] for i in range(n_pieces)]
+    swaps = [[("yp1", i)] for i in range(n_pieces)]
+    swaps += [[("yp2", i), ("yq1", i)] for i in range(n_pieces)]
+    swaps += [[("yf", i)] for i in range(last_piece)]
+    along.append([("g", last_piece)])
+    last_slot = len(along) - 1
+
     done_at = []
-    for slot in range(16):
-        sends = []
-        if slot < cuts:
-            sends += [("p1", slot), ("p2", slot)]
-        elif slot < 2 * cuts:
-            sends += [("q1", slot - cuts), ("q2", slot - cuts)]
-        elif slot < 3 * cuts:
-            sends += [("f", slot - 2 * cuts)]
-        late = slot - lag
-        if 0 <= late < cuts:
-            sends += [("yp1", late)]
-        elif cuts <= late < 2 * cuts:
-            sends += [("yp2", late - cuts), ("yq1", late - cuts)]
-        elif 2 * cuts <= late < 3 * cuts - 1:
-            sends += [("yq2", late - 2 * cuts), ("yf", late - 2 * cuts)]
-        if slot == 2 * cuts:
-            sends += [("h", cuts - 1)]
-        if slot == 3 * cuts:
-            sends = [("g", cuts - 1)] + sends
-        if lag <= slot < 3 * cuts + 1:
+    for slot in range(last_slot + 6):
+        sends = list(along[slot]) if slot <= last_slot else []
+        if 0 <= slot - lag < len(swaps):
+            sends += swaps[slot - lag]
+        if lag <= slot <= last_slot:
             keys = [(sent_from[name], i) for name, i in sends] + done_at[slot - lag]
-            keys = list(dict.fromkeys(keys))
+            for kind, which in tasks.get(slot, []):
+                if kind == "exchange":
+                    keys.append(("packed", which))
+                if kind == "rebuild":
+                    keys += [("bank", block) for block in which]
+            keys = [key for key in dict.fromkeys(keys) if key in held]
             values = lax.optimization_barrier(tuple(held[key] for key in keys))
             held.update(zip(keys, values))
         before = dict(held)
+        if slot == EXTENDED + lag:
+            long = [held["long", name] for name in ("p1", "p2")]
+            held["p1", EXTENDED], held["p2", EXTENDED] = trim(long, pieces[EXTENDED][1])
         for name, i in sends:
+            if i == EXTENDED and name in extended:
+                held["long", name] = send(name, extended[name])
+                continue
             held[name, i] = send(name, held[sent_from[name], i])
         for task in tasks.get(slot, []):
             run(*task)
         done_at.append([key for key, value in held.items() if before.get(key) is not value])
-    return held["pcs"], held["rec"]
+    return held["pcs"].T, held["rec"]
 
 
 def solution(mesh):

time: 200 us -> 189 us (0.945)
  waiting for transfers between devices: 76.8 us -> 55.5 us
  blocking collectives: 0 us -> 17 us
  local copies, waits for them, and re-layouts: 9.62 us -> 0.01 us
    all_gather x0 -> x3, blocking collectives: none -> 17 us  [run(): held['sum', which] = [lax.all_gather(held['packed', which], 'cell', axis=0)]]
    ppermute x12 -> x3, waiting for transfers between devices: 12.7 us -> 0.01 us  [exchange(): lax.ppermute(packed, 'cell', [(i, i ^ step) for i in range(size)])]
    ppermute x9, waiting for transfers between devices: 36.7 us -> 28.3 us  [send(): return lax.ppermute(array, 'day', OUTWARD)]
    ppermute x4, starting transfers between devices: 9.1 us -> 17.2 us  [send(): return lax.ppermute(array, 'day', PAIRED)]
    ppermute x2 -> x0, starting transfers between devices: 6.22 us -> none  [the longest x1 4.93 us: on_device(): lax.ppermute(series[days - HALO:], 'day', [(i, i + 1) for i in range(n -...]
    slice x2 -> x0, local copies, waits for them, and re-layouts: 4.93 us -> none  [the longest x1 2.9 us: on_device(): held = {('own', i): first[i * size:(i + 1) * size] for i in range(cuts)}]
    ppermute x12 -> x3, starting transfers between devices: 5.25 us -> 1.93 us  [exchange(): lax.ppermute(packed, 'cell', [(i, i ^ step) for i in range(size)])]
    pallas_call x1 -> x3, Pallas kernels: 1.38 us -> 3.66 us  [the longest x1 2.71 us: cut(): pl.pallas_call(functools.partial(cut_kernel, pieces, extended, half), out...]
  transfers between devices with their start and end apart: 54 -> 43, of which waited for: 20 -> 10; matrix products, arithmetic and copies ran while one was open for 3% -> 0% of each run, Pallas kernels for 18% -> 17%
where the time goes in v3:
time: 189 us; the launch traced here: 188 us
  starting transfers between devices  71.1 us (38%)
  waiting for transfers between devices  55.5 us (29%)
  Pallas kernels  42.8 us (23%)
  blocking collectives  17 us (9%)
    ppermute x15, starting transfers between devices, across(): lax.ppermute(array, ('grp', 'day'), [(g * n + d, (1 - g) * n + d) for g i...  32.1 us
    ppermute x9, waiting for transfers between devices, send(): return lax.ppermute(array, 'day', OUTWARD)  28.3 us
    ppermute x4, waiting for transfers between devices, send(): return lax.ppermute(array, 'day', PAIRED)  20.9 us
    pallas_call x5, Pallas kernels, project(): pl.pallas_call(functools.partial(project_kernel, plan, parts, first_slot,...  20.5 us
    pallas_call x4, Pallas kernels, rebuild(): pl.pallas_call(functools.partial(rebuild_kernel, parts, width // lags, mo...  18.6 us
    ppermute x4, starting transfers between devices, send(): return lax.ppermute(array, 'day', PAIRED)  17.2 us
    all_gather x3, blocking collectives, run(): held['sum', which] = [lax.all_gather(held['packed', which], 'cell', axis=0)]  17 us
    ppermute x9, starting transfers between devices, send(): return lax.ppermute(array, 'day', OUTWARD)  11.6 us
  transfers between devices with their start and end apart: 43, of which 10 were waited for; matrix products, arithmetic and copies ran while one was open for 0% of the time, Pallas kernels for 17%

profile of v3, /device:TPU:0, one launch (start us, length us, event | category | flops | bytes accessed | tf_op | source)
XLA Modules:
  0.0 187.8 jit_solution(18029117649921179971)
XLA Ops:
  7.2 4.4 %collective-permute-start = (bf16[192,2048]{1,0:T(8,128)(2,1)S(1)}, bf16[192,2048]{1,0:T(8,128)(2,1)S(1)}, u32[]{:S(2)}, u32[]{:S(2)}) collective-permute-start(bf16[192,2048]{1,0:T(8,128)(2,1)S(1)} %get-tuple-element.94), channel_id=1, source_target_pairs={{0,4},{4,0},{8,12},{12,8},{1,5},{5,1},{9,13},{13,9},{2,6},{6,2},{1... | collective-permute-start | bytes 2359304 | tf_op jit(solution)/shard_map/ppermute | solution.py:513
  12.3 6.9 %collective-permute-done.5.refs_2_ = bf16[128,2048]{1,0:T(8,128)(2,1)S(1)} collective-permute-done((bf16[128,2048]{1,0:T(8,128)(2,1)S(1)}, bf16[128,2048]{1,0:T(8,128)(2,1)S(1)}, u32[]{:S(2)}, u32[]{:S(2)}) %collective-permute-start.5) | collective-permute-done | bytes 524320 | tf_op jit(solution)/shard_map/ppermute | solution.py:513
  19.3 5.1 %collective-permute-start.7 = (bf16[128,2048]{1,0:T(8,128)(2,1)S(1)}, bf16[128,2048]{1,0:T(8,128)(2,1)S(1)}, u32[]{:S(2)}, u32[]{:S(2)}) collective-permute-start(bf16[128,2048]{1,0:T(8,128)(2,1)S(1)} %get-tuple-element.105), channel_id=1, source_target_pairs={{0,4},{4,0},{8,12},{12,8},{1,5},{5,1},{9,13},{13,9},{2,6},{6,2},{1... | collective-permute-start | bytes 1572872 | tf_op jit(solution)/shard_map/ppermute | solution.py:513
  26.6 9.5 %collective-permute-done.refs_0_.paired = bf16[192,2048]{1,0:T(8,128)(2,1)S(1)} collective-permute-done((bf16[192,2048]{1,0:T(8,128)(2,1)S(1)}, bf16[192,2048]{1,0:T(8,128)(2,1)S(1)}, u32[]{:S(2)}, u32[]{:S(2)}) %collective-permute-start) | collective-permute-done | bytes 786464 | tf_op jit(solution)/shard_map/ppermute | solution.py:513
  38.3 4.6 %collective-permute-start.2 = (bf16[128,2048]{1,0:T(8,128)(2,1)S(1)}, bf16[128,2048]{1,0:T(8,128)(2,1)S(1)}, u32[]{:S(2)}, u32[]{:S(2)}) collective-permute-start(bf16[128,2048]{1,0:T(8,128)(2,1)S(1)} %get-tuple-element.100), channel_id=1, source_target_pairs={{0,4},{4,0},{8,12},{12,8},{1,5},{5,1},{9,13},{13,9},{2,6},{6,2},{1... | collective-permute-start | bytes 1572872 | tf_op jit(solution)/shard_map/ppermute | solution.py:513
  42.9 4.5 %collective-permute-done.7.refs_4_ = bf16[128,2048]{1,0:T(8,128)(2,1)S(1)} collective-permute-done((bf16[128,2048]{1,0:T(8,128)(2,1)S(1)}, bf16[128,2048]{1,0:T(8,128)(2,1)S(1)}, u32[]{:S(2)}, u32[]{:S(2)}) %collective-permute-start.7) | collective-permute-done | bytes 524320 | tf_op jit(solution)/shard_map/ppermute | solution.py:513
  48.9 4.7 %project.5 = (f32[104,128]{1,0:T(8,128)S(1)}, bf16[1024,2048]{1,0:T(8,128)(2,1)S(1)}) custom-call(s32[8]{0:T(128)S(1)} %compare_select_fusion.7.meta.refs_0_, bf16[896,2048]{1,0:T(8,128)(2,1)S(1)} %stage.1.refs_1_, bf16[1024,2048]{1,0:T(8,128)(2,1)S(1)} %bitcast.6), custom_call_target="tpu_custom_call" | custom-call | flops 3556769792 | bytes 4194304 | tf_op jit(solution)/shard_map/project/pallas_call | solution.py:361
  59.8 5.7 %all-gather = f32[416,128]{1,0:T(8,128)S(1)} all-gather(f32[104,128]{1,0:T(8,128)S(1)} %get-tuple-element.107), channel_id=2, replica_groups=mesh['grp'=2,'day'=4,'cell'=4] {'cell'}, dimensions={0}, use_global_device_ids=true | all-gather | bytes 266240 | tf_op jit(solution)/shard_map/all_gather | solution.py:566
  65.4 7.2 %collective-permute-done.10.refs_2_ = bf16[128,2048]{1,0:T(8,128)(2,1)S(1)} collective-permute-done((bf16[128,2048]{1,0:T(8,128)(2,1)S(1)}, bf16[128,2048]{1,0:T(8,128)(2,1)S(1)}, u32[]{:S(2)}, u32[]{:S(2)}) %collective-permute-start.10) | collective-permute-done | bytes 524320 | tf_op jit(solution)/shard_map/ppermute | solution.py:517
  76.2 6.4 %collective-permute-done.13.refs_4_ = bf16[128,2048]{1,0:T(8,128)(2,1)S(1)} collective-permute-done((bf16[128,2048]{1,0:T(8,128)(2,1)S(1)}, bf16[128,2048]{1,0:T(8,128)(2,1)S(1)}, u32[]{:S(2)}, u32[]{:S(2)}) %collective-permute-start.13) | collective-permute-done | bytes 524320 | tf_op jit(solution)/shard_map/ppermute | solution.py:517
  83.3 4.4 %collective-permute-start.19 = (bf16[128,2048]{1,0:T(8,128)(2,1)S(1)}, bf16[128,2048]{1,0:T(8,128)(2,1)S(1)}, u32[]{:S(2)}, u32[]{:S(2)}) collective-permute-start(bf16[128,2048]{1,0:T(8,128)(2,1)S(1)} %collective-permute-done.10.refs_2_), channel_id=1, source_target_pairs={{0,16},{12,28},{16,0},{28,12},{1,17},{13,29},{17,1},{29,13},{2,18}... | collective-permute-start | bytes 1572872 | tf_op jit(solution)/shard_map/ppermute | solution.py:505
  87.7 4.2 %rebuild.4 = (f32[768,2048]{1,0:T(8,128)S(1)}, f32[104,128]{1,0:T(8,128)S(1)}) custom-call(s32[8]{0:T(128)S(1)} %compare_select_fusion.7.meta.refs_0_, f32[4,104,128]{2,1,0:T(8,128)S(1)} %bitcast.8, bf16[1024,2048]{1,0:T(8,128)(2,1)S(1)} %get-tuple-element.119.refs_2_), custom_call_target="tpu_custom_call" | custom-call | flops 3221225472 | bytes 6291456 | tf_op jit(solution)/shard_map/rebuild/pallas_call | solution.py:412
  94.6 3.1 %collective-permute-start.30 = (bf16[128,2048]{1,0:T(8,128)(2,1)S(1)}, bf16[128,2048]{1,0:T(8,128)(2,1)S(1)}, u32[]{:S(2)}, u32[]{:S(2)}) collective-permute-start(bf16[128,2048]{1,0:T(8,128)(2,1)S(1)} %collective-permute-done.13.refs_4_), channel_id=1, source_target_pairs={{0,16},{12,28},{16,0},{28,12},{1,17},{13,29},{17,1},{29,13},{2,18}... | collective-permute-start | bytes 1572872 | tf_op jit(solution)/shard_map/ppermute | solution.py:505
  97.8 4.9 %project.6 = (f32[104,128]{1,0:T(8,128)S(1)}, bf16[1024,2048]{1,0:T(8,128)(2,1)S(1)}) custom-call(s32[8]{0:T(128)S(1)} %compare_select_fusion.7.meta.refs_0_, bf16[896,2048]{1,0:T(8,128)(2,1)S(1)} %stage.1.refs_1_, bf16[128,2048]{1,0:T(8,128)(2,1)S(1)} %collective-permute-done.5.refs_2_, bf16[128,2048]{1,0:T(8,128)(2,1)S(1)} %get-tuple-element.118.refs_3_, ...), custom_call_target="tpu_custom_call" | custom-call | flops 3556769792 | bytes 4194304 | tf_op jit(solution)/shard_map/project/pallas_call | solution.py:361
  109.8 11.6 %collective-permute-done.20.refs_2_ = bf16[128,2048]{1,0:T(8,128)(2,1)S(1)} collective-permute-done((bf16[128,2048]{1,0:T(8,128)(2,1)S(1)}, bf16[128,2048]{1,0:T(8,128)(2,1)S(1)}, u32[]{:S(2)}, u32[]{:S(2)}) %collective-permute-start.20) | collective-permute-done | bytes 524320 | tf_op jit(solution)/shard_map/ppermute | solution.py:517
  123.1 3.2 %collective-permute-start.34 = (bf16[128,2048]{1,0:T(8,128)(2,1)S(1)}, bf16[128,2048]{1,0:T(8,128)(2,1)S(1)}, u32[]{:S(2)}, u32[]{:S(2)}) collective-permute-start(bf16[128,2048]{1,0:T(8,128)(2,1)S(1)} %collective-permute-done.27.refs_8_), channel_id=1, source_target_pairs={{0,16},{12,28},{16,0},{28,12},{1,17},{13,29},{17,1},{29,13},{2,18}... | collective-permute-start | bytes 1572872 | tf_op jit(solution)/shard_map/ppermute | solution.py:505
  126.3 5.7 %all-gather.1 = f32[416,128]{1,0:T(8,128)S(1)} all-gather(f32[104,128]{1,0:T(8,128)S(1)} %get-tuple-element.137), channel_id=3, replica_groups=mesh['grp'=2,'day'=4,'cell'=4] {'cell'}, dimensions={0}, use_global_device_ids=true | all-gather | bytes 266240 | tf_op jit(solution)/shard_map/all_gather | solution.py:566
  137.9 4.4 %rebuild.5 = (f32[768,2048]{1,0:T(8,128)S(1)}, f32[104,128]{1,0:T(8,128)S(1)}) custom-call(s32[8]{0:T(128)S(1)} %compare_select_fusion.7.meta.refs_0_, f32[4,104,128]{2,1,0:T(8,128)S(1)} %bitcast.9, bf16[1024,2048]{1,0:T(8,128)(2,1)S(1)} %get-tuple-element.166.refs_2_, f32[768,2048]{1,0:T(8,128)S(1)} %get-tuple-element.167.refs_3_), custom_call_target="tpu_custom_call", output_to_operand_aliasing={{0}: (3, {})} | custom-call | flops 3221225472 | bytes 6291456 | tf_op jit(solution)/shard_map/rebuild/pallas_call | solution.py:412
  142.3 3.2 %collective-permute-start.35 = (bf16[128,2048]{1,0:T(8,128)(2,1)S(1)}, bf16[128,2048]{1,0:T(8,128)(2,1)S(1)}, u32[]{:S(2)}, u32[]{:S(2)}) collective-permute-start(bf16[128,2048]{1,0:T(8,128)(2,1)S(1)} %collective-permute-done.31.refs_4_), channel_id=1, source_target_pairs={{0,16},{12,28},{16,0},{28,12},{1,17},{13,29},{17,1},{29,13},{2,18}... | collective-permute-start | bytes 1572872 | tf_op jit(solution)/shard_map/ppermute | solution.py:505
  154.5 4.9 %project.9 = (f32[104,128]{1,0:T(8,128)S(1)}, bf16[1024,2048]{1,0:T(8,128)(2,1)S(1)}) custom-call(s32[8]{0:T(128)S(1)} %compare_select_fusion.7.meta.refs_0_, bf16[896,2048]{1,0:T(8,128)(2,1)S(1)} %stage.1.refs_1_, bf16[128,2048]{1,0:T(8,128)(2,1)S(1)} %collective-permute-done.10.refs_2_, bf16[128,2048]{1,0:T(8,128)(2,1)S(1)} %collective-permute-done.6.refs_3_, ...), custom_call_target="tpu_custom_call" | custom-call | flops 3556769792 | bytes 4194304 | tf_op jit(solution)/shard_map/project/pallas_call | solution.py:361
  159.5 5.7 %all-gather.2 = f32[416,128]{1,0:T(8,128)S(1)} all-gather(f32[104,128]{1,0:T(8,128)S(1)} %get-tuple-element.177), channel_id=4, replica_groups=mesh['grp'=2,'day'=4,'cell'=4] {'cell'}, dimensions={0}, use_global_device_ids=true | all-gather | bytes 266240 | tf_op jit(solution)/shard_map/all_gather | solution.py:566
  167.9 4.6 %collective-permute-done.36.refs_6_ = bf16[128,2048]{1,0:T(8,128)(2,1)S(1)} collective-permute-done((bf16[128,2048]{1,0:T(8,128)(2,1)S(1)}, bf16[128,2048]{1,0:T(8,128)(2,1)S(1)}, u32[]{:S(2)}, u32[]{:S(2)}) %collective-permute-start.36) | collective-permute-done | bytes 524320 | tf_op jit(solution)/shard_map/ppermute | solution.py:505
  177.6 4.4 %rebuild.6 = (f32[768,2048]{1,0:T(8,128)S(1)}, f32[104,128]{1,0:T(8,128)S(1)}) custom-call(s32[8]{0:T(128)S(1)} %compare_select_fusion.7.meta.refs_0_, f32[4,104,128]{2,1,0:T(8,128)S(1)} %bitcast.7, bf16[1024,2048]{1,0:T(8,128)(2,1)S(1)} %get-tuple-element.178.refs_2_, f32[768,2048]{1,0:T(8,128)S(1)} %get-tuple-element.179.refs_3_), custom_call_target="tpu_custom_call", output_to_operand_aliasing={{0}: (3, {})} | custom-call | flops 3221225472 | bytes 6291456 | tf_op jit(solution)/shard_map/rebuild/pallas_call | solution.py:412
  182.0 5.6 %rebuild.7 = (f32[768,2048]{1,0:T(8,128)}, f32[64,768]{1,0:T(8,128)}) custom-call(s32[8]{0:T(128)S(1)} %compare_select_fusion.7.meta.refs_0_, f32[104,128]{1,0:T(8,128)S(1)} %get-tuple-element.162.refs_1_, f32[104,128]{1,0:T(8,128)S(1)} %collective-permute-done.40.refs_2_, f32[104,128]{1,0:T(8,128)S(1)} %collective-permute-done.41.refs_3_, ...), custom_call_target="tpu_custom_call" | custom-call | flops 3221225472 | bytes 6291456 | tf_op jit(solution)/shard_map/rebuild/pallas_call | solution.py:412
  (82 shorter events, 57.3 us)
Async XLA Ops:
  7.2 28.9 %collective-permute-start = (bf16[192,2048]{1,0:T(8,128)(2,1)S(1)}, bf16[192,2048]{1,0:T(8,128)(2,1)S(1)}, u32[]{:S(2)}, u32[]{:S(2)}) collective-permute-start(bf16[192,2048]{1,0:T(8,128)(2,1)S(1)} %get-tuple-element.94), channel_id=1, source_target_pairs={{0,4},{4,0},{8,12},{12,8},{1,5},{5,1},{9,13},{13,9},{2,6},{6,2},{1... | collective-permute-start | bytes 2359304 | tf_op jit(solution)/shard_map/ppermute | solution.py:513
  11.6 24.5 %collective-permute-start.1 = (bf16[192,2048]{1,0:T(8,128)(2,1)S(1)}, bf16[192,2048]{1,0:T(8,128)(2,1)S(1)}, u32[]{:S(2)}, u32[]{:S(2)}) collective-permute-start(bf16[192,2048]{1,0:T(8,128)(2,1)S(1)} %get-tuple-element.95), channel_id=1, source_target_pairs={{4,8},{8,4},{5,9},{9,5},{6,10},{10,6},{7,11},{11,7},{20,24},{24,20... | collective-permute-start | bytes 2359304 | tf_op jit(solution)/shard_map/ppermute | solution.py:515
  19.3 28.1 %collective-permute-start.7 = (bf16[128,2048]{1,0:T(8,128)(2,1)S(1)}, bf16[128,2048]{1,0:T(8,128)(2,1)S(1)}, u32[]{:S(2)}, u32[]{:S(2)}) collective-permute-start(bf16[128,2048]{1,0:T(8,128)(2,1)S(1)} %get-tuple-element.105), channel_id=1, source_target_pairs={{0,4},{4,0},{8,12},{12,8},{1,5},{5,1},{9,13},{13,9},{2,6},{6,2},{1... | collective-permute-start | bytes 1572872 | tf_op jit(solution)/shard_map/ppermute | solution.py:513
  24.3 29.3 %collective-permute-start.8 = (bf16[128,2048]{1,0:T(8,128)(2,1)S(1)}, bf16[128,2048]{1,0:T(8,128)(2,1)S(1)}, u32[]{:S(2)}, u32[]{:S(2)}) collective-permute-start(bf16[128,2048]{1,0:T(8,128)(2,1)S(1)} %get-tuple-element.105), channel_id=1, source_target_pairs={{4,8},{8,4},{5,9},{9,5},{6,10},{10,6},{7,11},{11,7},{20,24},{24,20... | collective-permute-start | bytes 1572872 | tf_op jit(solution)/shard_map/ppermute | solution.py:515
  25.0 28.7 %collective-permute-start.9 = (bf16[128,2048]{1,0:T(8,128)(2,1)S(1)}, bf16[128,2048]{1,0:T(8,128)(2,1)S(1)}, u32[]{:S(2)}, u32[]{:S(2)}) collective-permute-start(bf16[128,2048]{1,0:T(8,128)(2,1)S(1)} %collective-permute-done.5.refs_2_), channel_id=1, source_target_pairs={{0,16},{12,28},{4,20},{8,24},{16,0},{28,12},{20,4},{24,8},{1,17},{... | collective-permute-start | bytes 1572872 | tf_op jit(solution)/shard_map/ppermute | solution.py:505
  36.2 19.5 %collective-permute-start.4 = (bf16[128,2048]{1,0:T(8,128)(2,1)S(1)}, bf16[128,2048]{1,0:T(8,128)(2,1)S(1)}, u32[]{:S(2)}, u32[]{:S(2)}) collective-permute-start(bf16[128,2048]{1,0:T(8,128)(2,1)S(1)} %get-tuple-element.118.refs_3_), channel_id=1, source_target_pairs={{0,16},{12,28},{4,20},{8,24},{16,0},{28,12},{20,4},{24,8},{1,17},{... | collective-permute-start | bytes 1572872 | tf_op jit(solution)/shard_map/ppermute | solution.py:505
  38.3 19.5 %collective-permute-start.2 = (bf16[128,2048]{1,0:T(8,128)(2,1)S(1)}, bf16[128,2048]{1,0:T(8,128)(2,1)S(1)}, u32[]{:S(2)}, u32[]{:S(2)}) collective-permute-start(bf16[128,2048]{1,0:T(8,128)(2,1)S(1)} %get-tuple-element.100), channel_id=1, source_target_pairs={{0,4},{4,0},{8,12},{12,8},{1,5},{5,1},{9,13},{13,9},{2,6},{6,2},{1... | collective-permute-start | bytes 1572872 | tf_op jit(solution)/shard_map/ppermute | solution.py:513
  53.7 19.0 %collective-permute-start.10 = (bf16[128,2048]{1,0:T(8,128)(2,1)S(1)}, bf16[128,2048]{1,0:T(8,128)(2,1)S(1)}, u32[]{:S(2)}, u32[]{:S(2)}) collective-permute-start(bf16[128,2048]{1,0:T(8,128)(2,1)S(1)} %collective-permute-done.6.refs_3_), channel_id=1, source_target_pairs={{4,0},{8,12},{5,1},{9,13},{6,2},{10,14},{7,3},{11,15},{20,16},{24,... | collective-permute-start | bytes 1572872 | tf_op jit(solution)/shard_map/ppermute | solution.py:517
  55.0 19.2 %collective-permute-start.11 = (bf16[128,2048]{1,0:T(8,128)(2,1)S(1)}, bf16[128,2048]{1,0:T(8,128)(2,1)S(1)}, u32[]{:S(2)}, u32[]{:S(2)}) collective-permute-start(bf16[128,2048]{1,0:T(8,128)(2,1)S(1)} %collective-permute-done.5.refs_2_), channel_id=1, source_target_pairs={{4,8},{8,4},{5,9},{9,5},{6,10},{10,6},{7,11},{11,7},{20,24},{24,20... | collective-permute-start | bytes 1572872 | tf_op jit(solution)/shard_map/ppermute | solution.py:515
  55.7 18.5 %collective-permute-start.12 = (bf16[128,2048]{1,0:T(8,128)(2,1)S(1)}, bf16[128,2048]{1,0:T(8,128)(2,1)S(1)}, u32[]{:S(2)}, u32[]{:S(2)}) collective-permute-start(bf16[128,2048]{1,0:T(8,128)(2,1)S(1)} %collective-permute-done.7.refs_4_), channel_id=1, source_target_pairs={{0,16},{12,28},{4,20},{8,24},{16,0},{28,12},{20,4},{24,8},{1,17},{... | collective-permute-start | bytes 1572872 | tf_op jit(solution)/shard_map/ppermute | solution.py:505
  57.8 24.8 %collective-permute-start.13 = (bf16[128,2048]{1,0:T(8,128)(2,1)S(1)}, bf16[128,2048]{1,0:T(8,128)(2,1)S(1)}, u32[]{:S(2)}, u32[]{:S(2)}) collective-permute-start(bf16[128,2048]{1,0:T(8,128)(2,1)S(1)} %get-tuple-element.145.refs_5_), channel_id=1, source_target_pairs={{4,0},{8,12},{5,1},{9,13},{6,2},{10,14},{7,3},{11,15},{20,16},{24,... | collective-permute-start | bytes 1572872 | tf_op jit(solution)/shard_map/ppermute | solution.py:517
  59.1 24.2 %collective-permute-start.14 = (bf16[128,2048]{1,0:T(8,128)(2,1)S(1)}, bf16[128,2048]{1,0:T(8,128)(2,1)S(1)}, u32[]{:S(2)}, u32[]{:S(2)}) collective-permute-start(bf16[128,2048]{1,0:T(8,128)(2,1)S(1)} %get-tuple-element.118.refs_3_), channel_id=1, source_target_pairs={{4,8},{8,4},{5,9},{9,5},{6,10},{10,6},{7,11},{11,7},{20,24},{24,20... | collective-permute-start | bytes 1572872 | tf_op jit(solution)/shard_map/ppermute | solution.py:515
  72.6 19.2 %collective-permute-start.15 = (bf16[128,2048]{1,0:T(8,128)(2,1)S(1)}, bf16[128,2048]{1,0:T(8,128)(2,1)S(1)}, u32[]{:S(2)}, u32[]{:S(2)}) collective-permute-start(bf16[128,2048]{1,0:T(8,128)(2,1)S(1)} %collective-permute-done.2.refs_5_), channel_id=1, source_target_pairs={{0,16},{12,28},{4,20},{8,24},{16,0},{28,12},{20,4},{24,8},{1,17},{... | collective-permute-start | bytes 1572872 | tf_op jit(solution)/shard_map/ppermute | solution.py:505
  74.2 19.0 %collective-permute-start.16 = (bf16[128,2048]{1,0:T(8,128)(2,1)S(1)}, bf16[128,2048]{1,0:T(8,128)(2,1)S(1)}, u32[]{:S(2)}, u32[]{:S(2)}) collective-permute-start(bf16[128,2048]{1,0:T(8,128)(2,1)S(1)} %collective-permute-done.8.refs_7_), channel_id=1, source_target_pairs={{4,0},{8,12},{5,1},{9,13},{6,2},{10,14},{7,3},{11,15},{20,16},{24,... | collective-permute-start | bytes 1572872 | tf_op jit(solution)/shard_map/ppermute | solution.py:517
  75.5 18.5 %collective-permute-start.17 = (bf16[128,2048]{1,0:T(8,128)(2,1)S(1)}, bf16[128,2048]{1,0:T(8,128)(2,1)S(1)}, u32[]{:S(2)}, u32[]{:S(2)}) collective-permute-start(bf16[128,2048]{1,0:T(8,128)(2,1)S(1)} %collective-permute-done.7.refs_4_), channel_id=1, source_target_pairs={{4,8},{8,4},{5,9},{9,5},{6,10},{10,6},{7,11},{11,7},{20,24},{24,20... | collective-permute-start | bytes 1572872 | tf_op jit(solution)/shard_map/ppermute | solution.py:515
  83.3 19.4 %collective-permute-start.19 = (bf16[128,2048]{1,0:T(8,128)(2,1)S(1)}, bf16[128,2048]{1,0:T(8,128)(2,1)S(1)}, u32[]{:S(2)}, u32[]{:S(2)}) collective-permute-start(bf16[128,2048]{1,0:T(8,128)(2,1)S(1)} %collective-permute-done.10.refs_2_), channel_id=1, source_target_pairs={{0,16},{12,28},{16,0},{28,12},{1,17},{13,29},{17,1},{29,13},{2,18}... | collective-permute-start | bytes 1572872 | tf_op jit(solution)/shard_map/ppermute | solution.py:505
  102.7 18.7 %collective-permute-start.20 = (bf16[128,2048]{1,0:T(8,128)(2,1)S(1)}, bf16[128,2048]{1,0:T(8,128)(2,1)S(1)}, u32[]{:S(2)}, u32[]{:S(2)}) collective-permute-start(bf16[128,2048]{1,0:T(8,128)(2,1)S(1)} %collective-permute-done.11.refs_3_), channel_id=1, source_target_pairs={{4,0},{8,12},{5,1},{9,13},{6,2},{10,14},{7,3},{11,15},{20,16},{24,... | collective-permute-start | bytes 1572872 | tf_op jit(solution)/shard_map/ppermute | solution.py:517
  105.5 26.5 %collective-permute-start.23 = (bf16[128,2048]{1,0:T(8,128)(2,1)S(1)}, bf16[128,2048]{1,0:T(8,128)(2,1)S(1)}, u32[]{:S(2)}, u32[]{:S(2)}) collective-permute-start(bf16[128,2048]{1,0:T(8,128)(2,1)S(1)} %collective-permute-done.16.refs_6_), channel_id=1, source_target_pairs={{0,16},{12,28},{16,0},{28,12},{1,17},{13,29},{17,1},{29,13},{2,18}... | collective-permute-start | bytes 1572872 | tf_op jit(solution)/shard_map/ppermute | solution.py:505
  108.5 24.7 %collective-permute-start.31 = (bf16[128,2048]{1,0:T(8,128)(2,1)S(1)}, bf16[128,2048]{1,0:T(8,128)(2,1)S(1)}, u32[]{:S(2)}, u32[]{:S(2)}) collective-permute-start(bf16[128,2048]{1,0:T(8,128)(2,1)S(1)} %collective-permute-done.14.refs_5_), channel_id=1, source_target_pairs={{4,0},{8,12},{5,1},{9,13},{6,2},{10,14},{7,3},{11,15},{20,16},{24,... | collective-permute-start | bytes 1572872 | tf_op jit(solution)/shard_map/ppermute | solution.py:517
  136.6 28.5 %collective-permute-start.39 = (bf16[128,2048]{1,0:T(8,128)(2,1)S(1)}, bf16[128,2048]{1,0:T(8,128)(2,1)S(1)}, u32[]{:S(2)}, u32[]{:S(2)}) collective-permute-start(bf16[128,2048]{1,0:T(8,128)(2,1)S(1)} %collective-permute-done.28.refs_9_), channel_id=1, source_target_pairs={{4,0},{8,12},{5,1},{9,13},{6,2},{10,14},{7,3},{11,15},{20,16},{24,... | collective-permute-start | bytes 1572872 | tf_op jit(solution)/shard_map/ppermute | solution.py:517
  142.3 25.6 %collective-permute-start.35 = (bf16[128,2048]{1,0:T(8,128)(2,1)S(1)}, bf16[128,2048]{1,0:T(8,128)(2,1)S(1)}, u32[]{:S(2)}, u32[]{:S(2)}) collective-permute-start(bf16[128,2048]{1,0:T(8,128)(2,1)S(1)} %collective-permute-done.31.refs_4_), channel_id=1, source_target_pairs={{0,16},{12,28},{16,0},{28,12},{1,17},{13,29},{17,1},{29,13},{2,18}... | collective-permute-start | bytes 1572872 | tf_op jit(solution)/shard_map/ppermute | solution.py:505
  148.6 19.3 %collective-permute-start.37 = (bf16[128,2048]{1,0:T(8,128)(2,1)S(1)}, bf16[128,2048]{1,0:T(8,128)(2,1)S(1)}, u32[]{:S(2)}, u32[]{:S(2)}) collective-permute-start(bf16[128,2048]{1,0:T(8,128)(2,1)S(1)} %collective-permute-done.12.refs_8_), channel_id=1, source_target_pairs={{4,8},{8,4},{5,9},{9,5},{6,10},{10,6},{7,11},{11,7},{20,24},{24,20... | collective-permute-start | bytes 1572872 | tf_op jit(solution)/shard_map/ppermute | solution.py:515
  150.6 21.9 %collective-permute-start.36 = (bf16[128,2048]{1,0:T(8,128)(2,1)S(1)}, bf16[128,2048]{1,0:T(8,128)(2,1)S(1)}, u32[]{:S(2)}, u32[]{:S(2)}) collective-permute-start(bf16[128,2048]{1,0:T(8,128)(2,1)S(1)} %collective-permute-done.24.refs_6_), channel_id=1, source_target_pairs={{0,16},{12,28},{16,0},{28,12},{1,17},{13,29},{17,1},{29,13},{2,18}... | collective-permute-start | bytes 1572872 | tf_op jit(solution)/shard_map/ppermute | solution.py:505
  153.2 19.3 %collective-permute-start.38 = (bf16[128,2048]{1,0:T(8,128)(2,1)S(1)}, bf16[128,2048]{1,0:T(8,128)(2,1)S(1)}, u32[]{:S(2)}, u32[]{:S(2)}) collective-permute-start(bf16[128,2048]{1,0:T(8,128)(2,1)S(1)} %collective-permute-done.21.refs_9_), channel_id=1, source_target_pairs={{4,0},{8,12},{5,1},{9,13},{6,2},{10,14},{7,3},{11,15},{20,16},{24,... | collective-permute-start | bytes 1572872 | tf_op jit(solution)/shard_map/ppermute | solution.py:517
  (21 other events, 303.8 us)

commit v4 on v3

--- a/solution.py
+++ b/solution.py
@@ -540,19 +540,22 @@
         return picked
 
     def run(kind, which):
-        if kind == "stage":
+        if kind == "after":
+            key, other = which
+            held[key], held[other] = lax.optimization_barrier((held[key], held[other]))
+        elif kind == "stage":
             starts = (pieces[EXTENDED][1],) * 2
             held["source"] = stage(meta, held["long", "p1"], series, held["long", "p2"], starts)
         elif kind == "project":
             source = held["source"]
             if which == "c1":
                 held["acc"], held["bank", "c"] = project(
-                    meta, source, pieces_of("c", (0, 1)), halves[:2], finish=False, **shape
+                    meta, source, pieces_of("c", (0, 1, 2)), halves[:3], finish=False, **shape
                 )
             elif which == "c2":
                 before = (held["acc"], held["bank", "c"])
                 held["packed", "c"], held["bank", "c"] = project(
-                    meta, source, pieces_of("c", (2, 3)), halves[2:], before=before, **shape
+                    meta, source, pieces_of("c", (3,)), halves[3:], before=before, **shape
                 )
             else:
                 parts = whole if which == "own" else halves
@@ -585,14 +588,20 @@
         5: [("rebuild", ("own",))],
         7: [("project", "a")],
         8: [("exchange", "a")],
-        13: [("project", "b"), ("exchange", "b"), ("project", "c1"), ("rebuild", ("a",))],
+        13: [
+            ("project", "b"),
+            ("after", (("bank", "a"), ("packed", "b"))),
+            ("exchange", "b"),
+            ("project", "c1"),
+            ("rebuild", ("a",)),
+        ],
         14: [("project", "c2")],
         15: [("exchange", "c"), ("rebuild", ("b",))],
         16: [("rebuild", ("c",))],
     }
     lag = 2
     along = [[("p1", i), ("p2", i)] for i in range(n_pieces)]
-    along += [[("q1", i), ("q2", i)] for i in range(n_pieces)]
+    along += [[("q2", i), ("q1", i)] for i in range(n_pieces)]
     along += [[("f", i), ("h", (i - 1) % n_pieces)] for i in range(n_pieces)]
     swaps = [[("yp1", i)] for i in range(n_pieces)]
     swaps += [[("yp2", i), ("yq1", i)] for i in range(n_pieces)]
@@ -604,7 +613,7 @@
     for slot in range(last_slot + 6):
         sends = list(along[slot]) if slot <= last_slot else []
         if 0 <= slot - lag < len(swaps):
-            sends += swaps[slot - lag]
+            sends = swaps[slot - lag] + sends
         if lag <= slot <= last_slot:
             keys = [(sent_from[name], i) for name, i in sends] + done_at[slot - lag]
             for kind, which in tasks.get(slot, []):

time: 189 us -> 185 us (0.979)
  waiting for transfers between devices: 55.5 us -> 51.5 us
    ppermute x9, waiting for transfers between devices: 28.3 us -> 23.3 us  [send(): return lax.ppermute(array, 'day', OUTWARD)]
  transfers between devices with their start and end apart: 43 -> 43, of which waited for: 10 -> 10; matrix products, arithmetic and copies ran while one was open for 0% -> 0% of each run, Pallas kernels for 17% -> 18%
where the time goes in v4:
time: 185 us; the launch traced here: 184 us
  starting transfers between devices  71.5 us (39%)
  waiting for transfers between devices  51.5 us (28%)
  Pallas kernels  42.6 us (23%)
  blocking collectives  16.9 us (9%)
    ppermute x15, starting transfers between devices, across(): lax.ppermute(array, ('grp', 'day'), [(g * n + d, (1 - g) * n + d) for g i...  32.5 us
    ppermute x9, waiting for transfers between devices, send(): return lax.ppermute(array, 'day', OUTWARD)  23.3 us
    ppermute x4, waiting for transfers between devices, send(): return lax.ppermute(array, 'day', PAIRED)  20.9 us
    pallas_call x5, Pallas kernels, project(): pl.pallas_call(functools.partial(project_kernel, plan, parts, first_slot,...  20.4 us
    pallas_call x4, Pallas kernels, rebuild(): pl.pallas_call(functools.partial(rebuild_kernel, parts, width // lags, mo...  18.6 us
    ppermute x4, starting transfers between devices, send(): return lax.ppermute(array, 'day', PAIRED)  17.2 us
    all_gather x3, blocking collectives, run(): held['sum', which] = [lax.all_gather(held['packed', which], 'cell', axis=0)]  16.9 us
    ppermute x9, starting transfers between devices, send(): return lax.ppermute(array, 'day', OUTWARD)  11.6 us
  transfers between devices with their start and end apart: 43, of which 10 were waited for; matrix products, arithmetic and copies ran while one was open for 0% of the time, Pallas kernels for 18%

profile of v4, /device:TPU:0, one launch (start us, length us, event | category | flops | bytes accessed | tf_op | source)
XLA Modules:
  0.0 184.0 jit_solution(6841978692765091759)
XLA Ops:
  7.2 4.4 %collective-permute-start = (bf16[192,2048]{1,0:T(8,128)(2,1)S(1)}, bf16[192,2048]{1,0:T(8,128)(2,1)S(1)}, u32[]{:S(2)}, u32[]{:S(2)}) collective-permute-start(bf16[192,2048]{1,0:T(8,128)(2,1)S(1)} %get-tuple-element.96), channel_id=1, source_target_pairs={{0,4},{4,0},{8,12},{12,8},{1,5},{5,1},{9,13},{13,9},{2,6},{6,2},{1... | collective-permute-start | bytes 2359304 | tf_op jit(solution)/shard_map/ppermute | solution.py:513
  12.3 6.9 %collective-permute-done.5.refs_2_ = bf16[128,2048]{1,0:T(8,128)(2,1)S(1)} collective-permute-done((bf16[128,2048]{1,0:T(8,128)(2,1)S(1)}, bf16[128,2048]{1,0:T(8,128)(2,1)S(1)}, u32[]{:S(2)}, u32[]{:S(2)}) %collective-permute-start.5) | collective-permute-done | bytes 524320 | tf_op jit(solution)/shard_map/ppermute | solution.py:513
  19.3 5.1 %collective-permute-start.7 = (bf16[128,2048]{1,0:T(8,128)(2,1)S(1)}, bf16[128,2048]{1,0:T(8,128)(2,1)S(1)}, u32[]{:S(2)}, u32[]{:S(2)}) collective-permute-start(bf16[128,2048]{1,0:T(8,128)(2,1)S(1)} %get-tuple-element.105), channel_id=1, source_target_pairs={{0,4},{4,0},{8,12},{12,8},{1,5},{5,1},{9,13},{13,9},{2,6},{6,2},{1... | collective-permute-start | bytes 1572872 | tf_op jit(solution)/shard_map/ppermute | solution.py:513
  26.6 9.5 %collective-permute-done.refs_0_.paired = bf16[192,2048]{1,0:T(8,128)(2,1)S(1)} collective-permute-done((bf16[192,2048]{1,0:T(8,128)(2,1)S(1)}, bf16[192,2048]{1,0:T(8,128)(2,1)S(1)}, u32[]{:S(2)}, u32[]{:S(2)}) %collective-permute-start) | collective-permute-done | bytes 786464 | tf_op jit(solution)/shard_map/ppermute | solution.py:513
  38.3 4.6 %collective-permute-start.2 = (bf16[128,2048]{1,0:T(8,128)(2,1)S(1)}, bf16[128,2048]{1,0:T(8,128)(2,1)S(1)}, u32[]{:S(2)}, u32[]{:S(2)}) collective-permute-start(bf16[128,2048]{1,0:T(8,128)(2,1)S(1)} %get-tuple-element.98), channel_id=1, source_target_pairs={{0,4},{4,0},{8,12},{12,8},{1,5},{5,1},{9,13},{13,9},{2,6},{6,2},{1... | collective-permute-start | bytes 1572872 | tf_op jit(solution)/shard_map/ppermute | solution.py:513
  42.9 4.5 %collective-permute-done.7.refs_4_ = bf16[128,2048]{1,0:T(8,128)(2,1)S(1)} collective-permute-done((bf16[128,2048]{1,0:T(8,128)(2,1)S(1)}, bf16[128,2048]{1,0:T(8,128)(2,1)S(1)}, u32[]{:S(2)}, u32[]{:S(2)}) %collective-permute-start.7) | collective-permute-done | bytes 524320 | tf_op jit(solution)/shard_map/ppermute | solution.py:513
  48.9 4.7 %project.5 = (f32[104,128]{1,0:T(8,128)S(1)}, bf16[1024,2048]{1,0:T(8,128)(2,1)S(1)}) custom-call(s32[8]{0:T(128)S(1)} %compare_select_fusion.7.meta.refs_0_, bf16[896,2048]{1,0:T(8,128)(2,1)S(1)} %stage.1.refs_1_, bf16[1024,2048]{1,0:T(8,128)(2,1)S(1)} %bitcast.6), custom_call_target="tpu_custom_call" | custom-call | flops 3556769792 | bytes 4194304 | tf_op jit(solution)/shard_map/project/pallas_call | solution.py:361
  60.8 5.6 %all-gather = f32[416,128]{1,0:T(8,128)S(1)} all-gather(f32[104,128]{1,0:T(8,128)S(1)} %get-tuple-element.109), channel_id=2, replica_groups=mesh['grp'=2,'day'=4,'cell'=4] {'cell'}, dimensions={0}, use_global_device_ids=true | all-gather | bytes 266240 | tf_op jit(solution)/shard_map/all_gather | solution.py:569
  66.4 6.2 %collective-permute-done.10.refs_2_ = bf16[128,2048]{1,0:T(8,128)(2,1)S(1)} collective-permute-done((bf16[128,2048]{1,0:T(8,128)(2,1)S(1)}, bf16[128,2048]{1,0:T(8,128)(2,1)S(1)}, u32[]{:S(2)}, u32[]{:S(2)}) %collective-permute-start.10) | collective-permute-done | bytes 524320 | tf_op jit(solution)/shard_map/ppermute | solution.py:517
  75.4 7.4 %collective-permute-done.14.refs_4_ = bf16[128,2048]{1,0:T(8,128)(2,1)S(1)} collective-permute-done((bf16[128,2048]{1,0:T(8,128)(2,1)S(1)}, bf16[128,2048]{1,0:T(8,128)(2,1)S(1)}, u32[]{:S(2)}, u32[]{:S(2)}) %collective-permute-start.14) | collective-permute-done | bytes 524320 | tf_op jit(solution)/shard_map/ppermute | solution.py:517
  82.8 4.5 %collective-permute-start.18 = (bf16[128,2048]{1,0:T(8,128)(2,1)S(1)}, bf16[128,2048]{1,0:T(8,128)(2,1)S(1)}, u32[]{:S(2)}, u32[]{:S(2)}) collective-permute-start(bf16[128,2048]{1,0:T(8,128)(2,1)S(1)} %collective-permute-done.10.refs_2_), channel_id=1, source_target_pairs={{0,16},{12,28},{16,0},{28,12},{1,17},{13,29},{17,1},{29,13},{2,18}... | collective-permute-start | bytes 1572872 | tf_op jit(solution)/shard_map/ppermute | solution.py:505
  88.0 4.2 %rebuild.4 = (f32[768,2048]{1,0:T(8,128)S(1)}, f32[104,128]{1,0:T(8,128)S(1)}) custom-call(s32[8]{0:T(128)S(1)} %compare_select_fusion.7.meta.refs_0_, f32[4,104,128]{2,1,0:T(8,128)S(1)} %bitcast.9, bf16[1024,2048]{1,0:T(8,128)(2,1)S(1)} %get-tuple-element.122.refs_2_), custom_call_target="tpu_custom_call" | custom-call | flops 3221225472 | bytes 6291456 | tf_op jit(solution)/shard_map/rebuild/pallas_call | solution.py:412
  94.2 4.0 %collective-permute-start.30 = (bf16[128,2048]{1,0:T(8,128)(2,1)S(1)}, bf16[128,2048]{1,0:T(8,128)(2,1)S(1)}, u32[]{:S(2)}, u32[]{:S(2)}) collective-permute-start(bf16[128,2048]{1,0:T(8,128)(2,1)S(1)} %collective-permute-done.14.refs_4_), channel_id=1, source_target_pairs={{0,16},{12,28},{16,0},{28,12},{1,17},{13,29},{17,1},{29,13},{2,18}... | collective-permute-start | bytes 1572872 | tf_op jit(solution)/shard_map/ppermute | solution.py:505
  98.9 4.8 %project.6 = (f32[104,128]{1,0:T(8,128)S(1)}, bf16[1024,2048]{1,0:T(8,128)(2,1)S(1)}) custom-call(s32[8]{0:T(128)S(1)} %compare_select_fusion.7.meta.refs_0_, bf16[896,2048]{1,0:T(8,128)(2,1)S(1)} %stage.1.refs_1_, bf16[128,2048]{1,0:T(8,128)(2,1)S(1)} %collective-permute-done.5.refs_2_, bf16[128,2048]{1,0:T(8,128)(2,1)S(1)} %get-tuple-element.121.refs_3_, ...), custom_call_target="tpu_custom_call" | custom-call | flops 3556769792 | bytes 4194304 | tf_op jit(solution)/shard_map/project/pallas_call | solution.py:361
  109.8 9.5 %collective-permute-done.20.refs_2_ = bf16[128,2048]{1,0:T(8,128)(2,1)S(1)} collective-permute-done((bf16[128,2048]{1,0:T(8,128)(2,1)S(1)}, bf16[128,2048]{1,0:T(8,128)(2,1)S(1)}, u32[]{:S(2)}, u32[]{:S(2)}) %collective-permute-start.20) | collective-permute-done | bytes 524320 | tf_op jit(solution)/shard_map/ppermute | solution.py:517
  120.1 3.5 %collective-permute-start.34 = (bf16[128,2048]{1,0:T(8,128)(2,1)S(1)}, bf16[128,2048]{1,0:T(8,128)(2,1)S(1)}, u32[]{:S(2)}, u32[]{:S(2)}) collective-permute-start(bf16[128,2048]{1,0:T(8,128)(2,1)S(1)} %collective-permute-done.28.refs_8_), channel_id=1, source_target_pairs={{0,16},{12,28},{16,0},{28,12},{1,17},{13,29},{17,1},{29,13},{2,18}... | collective-permute-start | bytes 1572872 | tf_op jit(solution)/shard_map/ppermute | solution.py:505
  124.3 5.7 %all-gather.1 = f32[416,128]{1,0:T(8,128)S(1)} all-gather(f32[104,128]{1,0:T(8,128)S(1)} %get-tuple-element.139), channel_id=3, replica_groups=mesh['grp'=2,'day'=4,'cell'=4] {'cell'}, dimensions={0}, use_global_device_ids=true | all-gather | bytes 266240 | tf_op jit(solution)/shard_map/all_gather | solution.py:569
  139.1 4.9 %project.9 = (f32[104,128]{1,0:T(8,128)S(1)}, bf16[1024,2048]{1,0:T(8,128)(2,1)S(1)}) custom-call(s32[8]{0:T(128)S(1)} %compare_select_fusion.7.meta.refs_0_, bf16[896,2048]{1,0:T(8,128)(2,1)S(1)} %stage.1.refs_1_, bf16[128,2048]{1,0:T(8,128)(2,1)S(1)} %collective-permute-done.10.refs_2_, bf16[128,2048]{1,0:T(8,128)(2,1)S(1)} %collective-permute-done.6.refs_3_, ...), custom_call_target="tpu_custom_call" | custom-call | flops 3556769792 | bytes 4194304 | tf_op jit(solution)/shard_map/project/pallas_call | solution.py:361
  144.1 5.7 %all-gather.2 = f32[416,128]{1,0:T(8,128)S(1)} all-gather(f32[104,128]{1,0:T(8,128)S(1)} %get-tuple-element.181), channel_id=4, replica_groups=mesh['grp'=2,'day'=4,'cell'=4] {'cell'}, dimensions={0}, use_global_device_ids=true | all-gather | bytes 266240 | tf_op jit(solution)/shard_map/all_gather | solution.py:569
  154.3 4.4 %rebuild.5 = (f32[768,2048]{1,0:T(8,128)S(1)}, f32[104,128]{1,0:T(8,128)S(1)}) custom-call(s32[8]{0:T(128)S(1)} %compare_select_fusion.7.meta.refs_0_, f32[4,104,128]{2,1,0:T(8,128)S(1)} %bitcast.8, bf16[1024,2048]{1,0:T(8,128)(2,1)S(1)} %get-tuple-element.178.refs_2_, f32[768,2048]{1,0:T(8,128)S(1)} %get-tuple-element.179.refs_3_), custom_call_target="tpu_custom_call", output_to_operand_aliasing={{0}: (3, {})} | custom-call | flops 3221225472 | bytes 6291456 | tf_op jit(solution)/shard_map/rebuild/pallas_call | solution.py:412
  159.1 3.8 %project.7 = (f32[848,256]{1,0:T(8,128)S(1)}, bf16[1024,2048]{1,0:T(8,128)(2,1)S(1)}) custom-call(s32[8]{0:T(128)S(1)} %compare_select_fusion.7.meta.refs_0_, bf16[896,2048]{1,0:T(8,128)(2,1)S(1)} %stage.1.refs_1_, bf16[128,2048]{1,0:T(8,128)(2,1)S(1)} %collective-permute-done.20.refs_2_, bf16[128,2048]{1,0:T(8,128)(2,1)S(1)} %collective-permute-done.12.refs_3_, ...), custom_call_target="tpu_custom_call" | custom-call | flops 2667577344 | bytes 3145728 | tf_op jit(solution)/shard_map/project/pallas_call | solution.py:361
  162.9 6.9 %collective-permute-done.27.refs_2_ = bf16[128,2048]{1,0:T(8,128)(2,1)S(1)} collective-permute-done((bf16[128,2048]{1,0:T(8,128)(2,1)S(1)}, bf16[128,2048]{1,0:T(8,128)(2,1)S(1)}, u32[]{:S(2)}, u32[]{:S(2)}) %collective-permute-start.27) | collective-permute-done | bytes 524320 | tf_op jit(solution)/shard_map/ppermute | solution.py:505
  173.8 4.4 %rebuild.6 = (f32[768,2048]{1,0:T(8,128)S(1)}, f32[104,128]{1,0:T(8,128)S(1)}) custom-call(s32[8]{0:T(128)S(1)} %compare_select_fusion.7.meta.refs_0_, f32[4,104,128]{2,1,0:T(8,128)S(1)} %bitcast.7, bf16[1024,2048]{1,0:T(8,128)(2,1)S(1)} %get-tuple-element.182.refs_2_, f32[768,2048]{1,0:T(8,128)S(1)} %get-tuple-element.183.refs_3_), custom_call_target="tpu_custom_call", output_to_operand_aliasing={{0}: (3, {})} | custom-call | flops 3221225472 | bytes 6291456 | tf_op jit(solution)/shard_map/rebuild/pallas_call | solution.py:412
  178.3 5.6 %rebuild.7 = (f32[768,2048]{1,0:T(8,128)}, f32[64,768]{1,0:T(8,128)}) custom-call(s32[8]{0:T(128)S(1)} %compare_select_fusion.7.meta.refs_0_, f32[104,128]{1,0:T(8,128)S(1)} %get-tuple-element.164.refs_1_, f32[104,128]{1,0:T(8,128)S(1)} %collective-permute-done.40.refs_2_, f32[104,128]{1,0:T(8,128)S(1)} %collective-permute-done.41.refs_3_, ...), custom_call_target="tpu_custom_call" | custom-call | flops 3221225472 | bytes 6291456 | tf_op jit(solution)/shard_map/rebuild/pallas_call | solution.py:412
  (82 shorter events, 51.8 us)
Async XLA Ops:
  7.2 28.9 %collective-permute-start = (bf16[192,2048]{1,0:T(8,128)(2,1)S(1)}, bf16[192,2048]{1,0:T(8,128)(2,1)S(1)}, u32[]{:S(2)}, u32[]{:S(2)}) collective-permute-start(bf16[192,2048]{1,0:T(8,128)(2,1)S(1)} %get-tuple-element.96), channel_id=1, source_target_pairs={{0,4},{4,0},{8,12},{12,8},{1,5},{5,1},{9,13},{13,9},{2,6},{6,2},{1... | collective-permute-start | bytes 2359304 | tf_op jit(solution)/shard_map/ppermute | solution.py:513
  11.6 24.5 %collective-permute-start.1 = (bf16[192,2048]{1,0:T(8,128)(2,1)S(1)}, bf16[192,2048]{1,0:T(8,128)(2,1)S(1)}, u32[]{:S(2)}, u32[]{:S(2)}) collective-permute-start(bf16[192,2048]{1,0:T(8,128)(2,1)S(1)} %get-tuple-element.97), channel_id=1, source_target_pairs={{4,8},{8,4},{5,9},{9,5},{6,10},{10,6},{7,11},{11,7},{20,24},{24,20... | collective-permute-start | bytes 2359304 | tf_op jit(solution)/shard_map/ppermute | solution.py:515
  19.3 28.1 %collective-permute-start.7 = (bf16[128,2048]{1,0:T(8,128)(2,1)S(1)}, bf16[128,2048]{1,0:T(8,128)(2,1)S(1)}, u32[]{:S(2)}, u32[]{:S(2)}) collective-permute-start(bf16[128,2048]{1,0:T(8,128)(2,1)S(1)} %get-tuple-element.105), channel_id=1, source_target_pairs={{0,4},{4,0},{8,12},{12,8},{1,5},{5,1},{9,13},{13,9},{2,6},{6,2},{1... | collective-permute-start | bytes 1572872 | tf_op jit(solution)/shard_map/ppermute | solution.py:513
  24.3 29.3 %collective-permute-start.9 = (bf16[128,2048]{1,0:T(8,128)(2,1)S(1)}, bf16[128,2048]{1,0:T(8,128)(2,1)S(1)}, u32[]{:S(2)}, u32[]{:S(2)}) collective-permute-start(bf16[128,2048]{1,0:T(8,128)(2,1)S(1)} %get-tuple-element.105), channel_id=1, source_target_pairs={{4,8},{8,4},{5,9},{9,5},{6,10},{10,6},{7,11},{11,7},{20,24},{24,20... | collective-permute-start | bytes 1572872 | tf_op jit(solution)/shard_map/ppermute | solution.py:515
  25.0 28.6 %collective-permute-start.8 = (bf16[128,2048]{1,0:T(8,128)(2,1)S(1)}, bf16[128,2048]{1,0:T(8,128)(2,1)S(1)}, u32[]{:S(2)}, u32[]{:S(2)}) collective-permute-start(bf16[128,2048]{1,0:T(8,128)(2,1)S(1)} %collective-permute-done.5.refs_2_), channel_id=1, source_target_pairs={{0,16},{12,28},{4,20},{8,24},{16,0},{28,12},{20,4},{24,8},{1,17},{... | collective-permute-start | bytes 1572872 | tf_op jit(solution)/shard_map/ppermute | solution.py:505
  36.2 20.8 %collective-permute-start.3 = (bf16[128,2048]{1,0:T(8,128)(2,1)S(1)}, bf16[128,2048]{1,0:T(8,128)(2,1)S(1)}, u32[]{:S(2)}, u32[]{:S(2)}) collective-permute-start(bf16[128,2048]{1,0:T(8,128)(2,1)S(1)} %get-tuple-element.121.refs_3_), channel_id=1, source_target_pairs={{0,16},{12,28},{4,20},{8,24},{16,0},{28,12},{20,4},{24,8},{1,17},{... | collective-permute-start | bytes 1572872 | tf_op jit(solution)/shard_map/ppermute | solution.py:505
  38.3 19.5 %collective-permute-start.2 = (bf16[128,2048]{1,0:T(8,128)(2,1)S(1)}, bf16[128,2048]{1,0:T(8,128)(2,1)S(1)}, u32[]{:S(2)}, u32[]{:S(2)}) collective-permute-start(bf16[128,2048]{1,0:T(8,128)(2,1)S(1)} %get-tuple-element.98), channel_id=1, source_target_pairs={{0,4},{4,0},{8,12},{12,8},{1,5},{5,1},{9,13},{13,9},{2,6},{6,2},{1... | collective-permute-start | bytes 1572872 | tf_op jit(solution)/shard_map/ppermute | solution.py:513
  53.7 19.0 %collective-permute-start.10 = (bf16[128,2048]{1,0:T(8,128)(2,1)S(1)}, bf16[128,2048]{1,0:T(8,128)(2,1)S(1)}, u32[]{:S(2)}, u32[]{:S(2)}) collective-permute-start(bf16[128,2048]{1,0:T(8,128)(2,1)S(1)} %collective-permute-done.6.refs_3_), channel_id=1, source_target_pairs={{4,0},{8,12},{5,1},{9,13},{6,2},{10,14},{7,3},{11,15},{20,16},{24,... | collective-permute-start | bytes 1572872 | tf_op jit(solution)/shard_map/ppermute | solution.py:517
  55.0 18.4 %collective-permute-start.11 = (bf16[128,2048]{1,0:T(8,128)(2,1)S(1)}, bf16[128,2048]{1,0:T(8,128)(2,1)S(1)}, u32[]{:S(2)}, u32[]{:S(2)}) collective-permute-start(bf16[128,2048]{1,0:T(8,128)(2,1)S(1)} %collective-permute-done.7.refs_4_), channel_id=1, source_target_pairs={{0,16},{12,28},{4,20},{8,24},{16,0},{28,12},{20,4},{24,8},{1,17},{... | collective-permute-start | bytes 1572872 | tf_op jit(solution)/shard_map/ppermute | solution.py:505
  57.8 25.0 %collective-permute-start.14 = (bf16[128,2048]{1,0:T(8,128)(2,1)S(1)}, bf16[128,2048]{1,0:T(8,128)(2,1)S(1)}, u32[]{:S(2)}, u32[]{:S(2)}) collective-permute-start(bf16[128,2048]{1,0:T(8,128)(2,1)S(1)} %get-tuple-element.147.refs_5_), channel_id=1, source_target_pairs={{4,0},{8,12},{5,1},{9,13},{6,2},{10,14},{7,3},{11,15},{20,16},{24,... | collective-permute-start | bytes 1572872 | tf_op jit(solution)/shard_map/ppermute | solution.py:517
  59.1 28.2 %collective-permute-start.15 = (bf16[128,2048]{1,0:T(8,128)(2,1)S(1)}, bf16[128,2048]{1,0:T(8,128)(2,1)S(1)}, u32[]{:S(2)}, u32[]{:S(2)}) collective-permute-start(bf16[128,2048]{1,0:T(8,128)(2,1)S(1)} %collective-permute-done.2.refs_5_), channel_id=1, source_target_pairs={{0,16},{12,28},{4,20},{8,24},{16,0},{28,12},{20,4},{24,8},{1,17},{... | collective-permute-start | bytes 1572872 | tf_op jit(solution)/shard_map/ppermute | solution.py:505
  72.6 19.6 %collective-permute-start.16 = (bf16[128,2048]{1,0:T(8,128)(2,1)S(1)}, bf16[128,2048]{1,0:T(8,128)(2,1)S(1)}, u32[]{:S(2)}, u32[]{:S(2)}) collective-permute-start(bf16[128,2048]{1,0:T(8,128)(2,1)S(1)} %get-tuple-element.121.refs_3_), channel_id=1, source_target_pairs={{4,8},{8,4},{5,9},{9,5},{6,10},{10,6},{7,11},{11,7},{20,24},{24,20... | collective-permute-start | bytes 1572872 | tf_op jit(solution)/shard_map/ppermute | solution.py:515
  73.3 20.2 %collective-permute-start.13 = (bf16[128,2048]{1,0:T(8,128)(2,1)S(1)}, bf16[128,2048]{1,0:T(8,128)(2,1)S(1)}, u32[]{:S(2)}, u32[]{:S(2)}) collective-permute-start(bf16[128,2048]{1,0:T(8,128)(2,1)S(1)} %collective-permute-done.9.refs_7_), channel_id=1, source_target_pairs={{4,0},{8,12},{5,1},{9,13},{6,2},{10,14},{7,3},{11,15},{20,16},{24,... | collective-permute-start | bytes 1572872 | tf_op jit(solution)/shard_map/ppermute | solution.py:517
  74.6 19.6 %collective-permute-start.17 = (bf16[128,2048]{1,0:T(8,128)(2,1)S(1)}, bf16[128,2048]{1,0:T(8,128)(2,1)S(1)}, u32[]{:S(2)}, u32[]{:S(2)}) collective-permute-start(bf16[128,2048]{1,0:T(8,128)(2,1)S(1)} %collective-permute-done.6.refs_3_), channel_id=1, source_target_pairs={{4,20},{8,24},{20,4},{24,8},{5,21},{9,25},{21,5},{25,9},{6,22},{10... | collective-permute-start | bytes 1572872 | tf_op jit(solution)/shard_map/ppermute | solution.py:505
  105.8 17.8 %collective-permute-start.22 = (bf16[128,2048]{1,0:T(8,128)(2,1)S(1)}, bf16[128,2048]{1,0:T(8,128)(2,1)S(1)}, u32[]{:S(2)}, u32[]{:S(2)}) collective-permute-start(bf16[128,2048]{1,0:T(8,128)(2,1)S(1)} %collective-permute-done.13.refs_6_), channel_id=1, source_target_pairs={{0,16},{12,28},{16,0},{28,12},{1,17},{13,29},{17,1},{29,13},{2,18}... | collective-permute-start | bytes 1572872 | tf_op jit(solution)/shard_map/ppermute | solution.py:505
  107.8 22.1 %collective-permute-start.23 = (bf16[128,2048]{1,0:T(8,128)(2,1)S(1)}, bf16[128,2048]{1,0:T(8,128)(2,1)S(1)}, u32[]{:S(2)}, u32[]{:S(2)}) collective-permute-start(bf16[128,2048]{1,0:T(8,128)(2,1)S(1)} %collective-permute-done.15.refs_9_), channel_id=1, source_target_pairs={{4,8},{8,4},{5,9},{9,5},{6,10},{10,6},{7,11},{11,7},{20,24},{24,20... | collective-permute-start | bytes 1572872 | tf_op jit(solution)/shard_map/ppermute | solution.py:515
  108.5 22.7 %collective-permute-start.32 = (bf16[128,2048]{1,0:T(8,128)(2,1)S(1)}, bf16[128,2048]{1,0:T(8,128)(2,1)S(1)}, u32[]{:S(2)}, u32[]{:S(2)}) collective-permute-start(bf16[128,2048]{1,0:T(8,128)(2,1)S(1)} %collective-permute-done.16.refs_5_), channel_id=1, source_target_pairs={{4,0},{8,12},{5,1},{9,13},{6,2},{10,14},{7,3},{11,15},{20,16},{24,... | collective-permute-start | bytes 1572872 | tf_op jit(solution)/shard_map/ppermute | solution.py:517
  129.9 19.8 %collective-permute-start.24 = (bf16[128,2048]{1,0:T(8,128)(2,1)S(1)}, bf16[128,2048]{1,0:T(8,128)(2,1)S(1)}, u32[]{:S(2)}, u32[]{:S(2)}) collective-permute-start(bf16[128,2048]{1,0:T(8,128)(2,1)S(1)} %collective-permute-done.19.refs_7_), channel_id=1, source_target_pairs={{4,0},{8,12},{5,1},{9,13},{6,2},{10,14},{7,3},{11,15},{20,16},{24,... | collective-permute-start | bytes 1572872 | tf_op jit(solution)/shard_map/ppermute | solution.py:517
  131.2 19.2 %collective-permute-start.25 = (bf16[128,2048]{1,0:T(8,128)(2,1)S(1)}, bf16[128,2048]{1,0:T(8,128)(2,1)S(1)}, u32[]{:S(2)}, u32[]{:S(2)}) collective-permute-start(bf16[128,2048]{1,0:T(8,128)(2,1)S(1)} %collective-permute-done.20.refs_2_), channel_id=1, source_target_pairs={{0,16},{12,28},{16,0},{28,12},{1,17},{13,29},{17,1},{29,13},{2,18}... | collective-permute-start | bytes 1572872 | tf_op jit(solution)/shard_map/ppermute | solution.py:505
  133.8 16.7 %collective-permute-start.26 = (bf16[128,2048]{1,0:T(8,128)(2,1)S(1)}, bf16[128,2048]{1,0:T(8,128)(2,1)S(1)}, u32[]{:S(2)}, u32[]{:S(2)}) collective-permute-start(bf16[128,2048]{1,0:T(8,128)(2,1)S(1)} %collective-permute-done.3.refs_7_), channel_id=1, source_target_pairs={{4,8},{8,4},{5,9},{9,5},{6,10},{10,6},{7,11},{11,7},{20,24},{24,20... | collective-permute-start | bytes 1572872 | tf_op jit(solution)/shard_map/ppermute | solution.py:515
  134.5 24.3 %collective-permute-start.38 = (bf16[128,2048]{1,0:T(8,128)(2,1)S(1)}, bf16[128,2048]{1,0:T(8,128)(2,1)S(1)}, u32[]{:S(2)}, u32[]{:S(2)}) collective-permute-start(bf16[128,2048]{1,0:T(8,128)(2,1)S(1)} %collective-permute-done.31.refs_9_), channel_id=1, source_target_pairs={{4,0},{8,12},{5,1},{9,13},{6,2},{10,14},{7,3},{11,15},{20,16},{24,... | collective-permute-start | bytes 1572872 | tf_op jit(solution)/shard_map/ppermute | solution.py:517
  135.8 23.3 %collective-permute-start.39 = (bf16[128,2048]{1,0:T(8,128)(2,1)S(1)}, bf16[128,2048]{1,0:T(8,128)(2,1)S(1)}, u32[]{:S(2)}, u32[]{:S(2)}) collective-permute-start(bf16[128,2048]{1,0:T(8,128)(2,1)S(1)} %collective-permute-done.32.refs_4_), channel_id=1, source_target_pairs={{0,16},{12,28},{16,0},{28,12},{1,17},{13,29},{17,1},{29,13},{2,18}... | collective-permute-start | bytes 1572872 | tf_op jit(solution)/shard_map/ppermute | solution.py:505
  150.5 19.3 %collective-permute-start.27 = (bf16[128,2048]{1,0:T(8,128)(2,1)S(1)}, bf16[128,2048]{1,0:T(8,128)(2,1)S(1)}, u32[]{:S(2)}, u32[]{:S(2)}) collective-permute-start(bf16[128,2048]{1,0:T(8,128)(2,1)S(1)} %collective-permute-done.24.refs_6_), channel_id=1, source_target_pairs={{0,16},{12,28},{16,0},{28,12},{1,17},{13,29},{17,1},{29,13},{2,18}... | collective-permute-start | bytes 1572872 | tf_op jit(solution)/shard_map/ppermute | solution.py:505
  153.0 16.8 %collective-permute-start.37 = (bf16[128,2048]{1,0:T(8,128)(2,1)S(1)}, bf16[128,2048]{1,0:T(8,128)(2,1)S(1)}, u32[]{:S(2)}, u32[]{:S(2)}) collective-permute-start(bf16[128,2048]{1,0:T(8,128)(2,1)S(1)} %collective-permute-done.23.refs_5_), channel_id=1, source_target_pairs={{4,0},{8,12},{5,1},{9,13},{6,2},{10,14},{7,3},{11,15},{20,16},{24,... | collective-permute-start | bytes 1572872 | tf_op jit(solution)/shard_map/ppermute | solution.py:517
  (21 other events, 297.1 us)

commit v5 on v4

--- a/solution.py
+++ b/solution.py
@@ -217,8 +217,16 @@
         scale = 1.0 / windows.astype(jnp.float32)
     copies = []
     depth = per_block * WIDE
-    for i, start in enumerate(range(0, cells, TILE)):
-        tile = slice(start, start + TILE)
+    edges = list(range(0, cells, TILE)) + [cells]
+    if last:
+        edges.insert(-1, cells - TILE // 2)
+        values = [ref[...] for ref in olds] + values
+    for start, end in zip(edges, edges[1:]):
+        tile = slice(start, end)
+        if last and end == cells:
+            unpack_modes([(meta[BLOCKS + i], v) for i, v in zip(order, values)], pcs_done, scratch, modes, HALO)
+            copies.append(pltpu.make_async_copy(pcs_done, pcs_out, sems.at[len(copies)]))
+            copies[-1].start()
         total = rec_in[:, tile] if has_in else None
         for block, bank in enumerate(banks):
             term = jnp.dot(
@@ -229,15 +237,11 @@
             total = term if total is None else total + term
         if last:
             done[:, tile] = total * scale
-            copies.append(pltpu.make_async_copy(done.at[:, tile], rec_out.at[:, tile], sems.at[i]))
+            copies.append(pltpu.make_async_copy(done.at[:, tile], rec_out.at[:, tile], sems.at[len(copies)]))
             copies[-1].start()
         else:
             rec_out[:, tile] = total
     if last:
-        values = [ref[...] for ref in olds] + values
-        unpack_modes([(meta[BLOCKS + i], v) for i, v in zip(order, values)], pcs_done, scratch, modes, HALO)
-        copies.append(pltpu.make_async_copy(pcs_done, pcs_out, sems.at[len(copies)]))
-        copies[-1].start()
         for copy in copies:
             copy.wait()
 
@@ -402,7 +406,7 @@
         scratch += [
             pltpu.VMEM((days, cells), jnp.float32),
             pltpu.VMEM((all_modes, days), jnp.float32),
-            pltpu.SemaphoreType.DMA((cells // TILE + 1,)),
+            pltpu.SemaphoreType.DMA((cells // TILE + 2,)),
         ]
     else:
         out_shape = [pltpu.VMEM((days, cells), jnp.float32)]

time: 185 us -> 185 us (level)
  transfers between devices with their start and end apart: 43 -> 43, of which waited for: 10 -> 10; matrix products, arithmetic and copies ran while one was open for 0% -> 0% of each run, Pallas kernels for 18% -> 17%
where the time goes in v5:
time: 185 us; the launch traced here: 184 us
  starting transfers between devices  71.5 us (39%)
  waiting for transfers between devices  51.5 us (28%)
  Pallas kernels  42.7 us (23%)
  blocking collectives  16.9 us (9%)
    ppermute x15, starting transfers between devices, across(): lax.ppermute(array, ('grp', 'day'), [(g * n + d, (1 - g) * n + d) for g i...  32.5 us
    ppermute x9, waiting for transfers between devices, send(): return lax.ppermute(array, 'day', OUTWARD)  23.3 us
    ppermute x4, waiting for transfers between devices, send(): return lax.ppermute(array, 'day', PAIRED)  20.9 us
    pallas_call x5, Pallas kernels, project(): pl.pallas_call(functools.partial(project_kernel, plan, parts, first_slot,...  20.4 us
    pallas_call x4, Pallas kernels, rebuild(): pl.pallas_call(functools.partial(rebuild_kernel, parts, width // lags, mo...  18.6 us
    ppermute x4, starting transfers between devices, send(): return lax.ppermute(array, 'day', PAIRED)  17.2 us
    all_gather x3, blocking collectives, run(): held['sum', which] = [lax.all_gather(held['packed', which], 'cell', axis=0)]  16.9 us
    ppermute x9, starting transfers between devices, send(): return lax.ppermute(array, 'day', OUTWARD)  11.6 us
  transfers between devices with their start and end apart: 43, of which 10 were waited for; matrix products, arithmetic and copies ran while one was open for 0% of the time, Pallas kernels for 17%

profile of v5, /device:TPU:0, one launch (start us, length us, event | category | flops | bytes accessed | tf_op | source)
XLA Modules:
  0.0 184.1 jit_solution(15060321861429617144)
XLA Ops:
  7.2 4.4 %collective-permute-start = (bf16[192,2048]{1,0:T(8,128)(2,1)S(1)}, bf16[192,2048]{1,0:T(8,128)(2,1)S(1)}, u32[]{:S(2)}, u32[]{:S(2)}) collective-permute-start(bf16[192,2048]{1,0:T(8,128)(2,1)S(1)} %get-tuple-element.96), channel_id=1, source_target_pairs={{0,4},{4,0},{8,12},{12,8},{1,5},{5,1},{9,13},{13,9},{2,6},{6,2},{1... | collective-permute-start | bytes 2359304 | tf_op jit(solution)/shard_map/ppermute | solution.py:517
  12.3 6.9 %collective-permute-done.5.refs_2_ = bf16[128,2048]{1,0:T(8,128)(2,1)S(1)} collective-permute-done((bf16[128,2048]{1,0:T(8,128)(2,1)S(1)}, bf16[128,2048]{1,0:T(8,128)(2,1)S(1)}, u32[]{:S(2)}, u32[]{:S(2)}) %collective-permute-start.5) | collective-permute-done | bytes 524320 | tf_op jit(solution)/shard_map/ppermute | solution.py:517
  19.3 5.1 %collective-permute-start.7 = (bf16[128,2048]{1,0:T(8,128)(2,1)S(1)}, bf16[128,2048]{1,0:T(8,128)(2,1)S(1)}, u32[]{:S(2)}, u32[]{:S(2)}) collective-permute-start(bf16[128,2048]{1,0:T(8,128)(2,1)S(1)} %get-tuple-element.105), channel_id=1, source_target_pairs={{0,4},{4,0},{8,12},{12,8},{1,5},{5,1},{9,13},{13,9},{2,6},{6,2},{1... | collective-permute-start | bytes 1572872 | tf_op jit(solution)/shard_map/ppermute | solution.py:517
  26.6 9.5 %collective-permute-done.refs_0_.paired = bf16[192,2048]{1,0:T(8,128)(2,1)S(1)} collective-permute-done((bf16[192,2048]{1,0:T(8,128)(2,1)S(1)}, bf16[192,2048]{1,0:T(8,128)(2,1)S(1)}, u32[]{:S(2)}, u32[]{:S(2)}) %collective-permute-start) | collective-permute-done | bytes 786464 | tf_op jit(solution)/shard_map/ppermute | solution.py:517
  38.3 4.6 %collective-permute-start.2 = (bf16[128,2048]{1,0:T(8,128)(2,1)S(1)}, bf16[128,2048]{1,0:T(8,128)(2,1)S(1)}, u32[]{:S(2)}, u32[]{:S(2)}) collective-permute-start(bf16[128,2048]{1,0:T(8,128)(2,1)S(1)} %get-tuple-element.98), channel_id=1, source_target_pairs={{0,4},{4,0},{8,12},{12,8},{1,5},{5,1},{9,13},{13,9},{2,6},{6,2},{1... | collective-permute-start | bytes 1572872 | tf_op jit(solution)/shard_map/ppermute | solution.py:517
  42.9 4.5 %collective-permute-done.7.refs_4_ = bf16[128,2048]{1,0:T(8,128)(2,1)S(1)} collective-permute-done((bf16[128,2048]{1,0:T(8,128)(2,1)S(1)}, bf16[128,2048]{1,0:T(8,128)(2,1)S(1)}, u32[]{:S(2)}, u32[]{:S(2)}) %collective-permute-start.7) | collective-permute-done | bytes 524320 | tf_op jit(solution)/shard_map/ppermute | solution.py:517
  48.9 4.7 %project.5 = (f32[104,128]{1,0:T(8,128)S(1)}, bf16[1024,2048]{1,0:T(8,128)(2,1)S(1)}) custom-call(s32[8]{0:T(128)S(1)} %compare_select_fusion.7.meta.refs_0_, bf16[896,2048]{1,0:T(8,128)(2,1)S(1)} %stage.1.refs_1_, bf16[1024,2048]{1,0:T(8,128)(2,1)S(1)} %bitcast.6), custom_call_target="tpu_custom_call" | custom-call | flops 3556769792 | bytes 4194304 | tf_op jit(solution)/shard_map/project/pallas_call | solution.py:365
  60.8 5.6 %all-gather = f32[416,128]{1,0:T(8,128)S(1)} all-gather(f32[104,128]{1,0:T(8,128)S(1)} %get-tuple-element.109), channel_id=2, replica_groups=mesh['grp'=2,'day'=4,'cell'=4] {'cell'}, dimensions={0}, use_global_device_ids=true | all-gather | bytes 266240 | tf_op jit(solution)/shard_map/all_gather | solution.py:573
  66.4 6.2 %collective-permute-done.10.refs_2_ = bf16[128,2048]{1,0:T(8,128)(2,1)S(1)} collective-permute-done((bf16[128,2048]{1,0:T(8,128)(2,1)S(1)}, bf16[128,2048]{1,0:T(8,128)(2,1)S(1)}, u32[]{:S(2)}, u32[]{:S(2)}) %collective-permute-start.10) | collective-permute-done | bytes 524320 | tf_op jit(solution)/shard_map/ppermute | solution.py:521
  75.4 7.4 %collective-permute-done.14.refs_4_ = bf16[128,2048]{1,0:T(8,128)(2,1)S(1)} collective-permute-done((bf16[128,2048]{1,0:T(8,128)(2,1)S(1)}, bf16[128,2048]{1,0:T(8,128)(2,1)S(1)}, u32[]{:S(2)}, u32[]{:S(2)}) %collective-permute-start.14) | collective-permute-done | bytes 524320 | tf_op jit(solution)/shard_map/ppermute | solution.py:521
  82.8 4.5 %collective-permute-start.18 = (bf16[128,2048]{1,0:T(8,128)(2,1)S(1)}, bf16[128,2048]{1,0:T(8,128)(2,1)S(1)}, u32[]{:S(2)}, u32[]{:S(2)}) collective-permute-start(bf16[128,2048]{1,0:T(8,128)(2,1)S(1)} %collective-permute-done.10.refs_2_), channel_id=1, source_target_pairs={{0,16},{12,28},{16,0},{28,12},{1,17},{13,29},{17,1},{29,13},{2,18}... | collective-permute-start | bytes 1572872 | tf_op jit(solution)/shard_map/ppermute | solution.py:509
  88.0 4.2 %rebuild.4 = (f32[768,2048]{1,0:T(8,128)S(1)}, f32[104,128]{1,0:T(8,128)S(1)}) custom-call(s32[8]{0:T(128)S(1)} %compare_select_fusion.7.meta.refs_0_, f32[4,104,128]{2,1,0:T(8,128)S(1)} %bitcast.9, bf16[1024,2048]{1,0:T(8,128)(2,1)S(1)} %get-tuple-element.122.refs_2_), custom_call_target="tpu_custom_call" | custom-call | flops 3221225472 | bytes 6291456 | tf_op jit(solution)/shard_map/rebuild/pallas_call | solution.py:416
  94.2 4.0 %collective-permute-start.30 = (bf16[128,2048]{1,0:T(8,128)(2,1)S(1)}, bf16[128,2048]{1,0:T(8,128)(2,1)S(1)}, u32[]{:S(2)}, u32[]{:S(2)}) collective-permute-start(bf16[128,2048]{1,0:T(8,128)(2,1)S(1)} %collective-permute-done.14.refs_4_), channel_id=1, source_target_pairs={{0,16},{12,28},{16,0},{28,12},{1,17},{13,29},{17,1},{29,13},{2,18}... | collective-permute-start | bytes 1572872 | tf_op jit(solution)/shard_map/ppermute | solution.py:509
  98.9 4.8 %project.6 = (f32[104,128]{1,0:T(8,128)S(1)}, bf16[1024,2048]{1,0:T(8,128)(2,1)S(1)}) custom-call(s32[8]{0:T(128)S(1)} %compare_select_fusion.7.meta.refs_0_, bf16[896,2048]{1,0:T(8,128)(2,1)S(1)} %stage.1.refs_1_, bf16[128,2048]{1,0:T(8,128)(2,1)S(1)} %collective-permute-done.5.refs_2_, bf16[128,2048]{1,0:T(8,128)(2,1)S(1)} %get-tuple-element.121.refs_3_, ...), custom_call_target="tpu_custom_call" | custom-call | flops 3556769792 | bytes 4194304 | tf_op jit(solution)/shard_map/project/pallas_call | solution.py:365
  109.8 9.5 %collective-permute-done.20.refs_2_ = bf16[128,2048]{1,0:T(8,128)(2,1)S(1)} collective-permute-done((bf16[128,2048]{1,0:T(8,128)(2,1)S(1)}, bf16[128,2048]{1,0:T(8,128)(2,1)S(1)}, u32[]{:S(2)}, u32[]{:S(2)}) %collective-permute-start.20) | collective-permute-done | bytes 524320 | tf_op jit(solution)/shard_map/ppermute | solution.py:521
  120.1 3.5 %collective-permute-start.34 = (bf16[128,2048]{1,0:T(8,128)(2,1)S(1)}, bf16[128,2048]{1,0:T(8,128)(2,1)S(1)}, u32[]{:S(2)}, u32[]{:S(2)}) collective-permute-start(bf16[128,2048]{1,0:T(8,128)(2,1)S(1)} %collective-permute-done.28.refs_8_), channel_id=1, source_target_pairs={{0,16},{12,28},{16,0},{28,12},{1,17},{13,29},{17,1},{29,13},{2,18}... | collective-permute-start | bytes 1572872 | tf_op jit(solution)/shard_map/ppermute | solution.py:509
  124.3 5.7 %all-gather.1 = f32[416,128]{1,0:T(8,128)S(1)} all-gather(f32[104,128]{1,0:T(8,128)S(1)} %get-tuple-element.139), channel_id=3, replica_groups=mesh['grp'=2,'day'=4,'cell'=4] {'cell'}, dimensions={0}, use_global_device_ids=true | all-gather | bytes 266240 | tf_op jit(solution)/shard_map/all_gather | solution.py:573
  139.1 4.9 %project.9 = (f32[104,128]{1,0:T(8,128)S(1)}, bf16[1024,2048]{1,0:T(8,128)(2,1)S(1)}) custom-call(s32[8]{0:T(128)S(1)} %compare_select_fusion.7.meta.refs_0_, bf16[896,2048]{1,0:T(8,128)(2,1)S(1)} %stage.1.refs_1_, bf16[128,2048]{1,0:T(8,128)(2,1)S(1)} %collective-permute-done.10.refs_2_, bf16[128,2048]{1,0:T(8,128)(2,1)S(1)} %collective-permute-done.6.refs_3_, ...), custom_call_target="tpu_custom_call" | custom-call | flops 3556769792 | bytes 4194304 | tf_op jit(solution)/shard_map/project/pallas_call | solution.py:365
  144.1 5.7 %all-gather.2 = f32[416,128]{1,0:T(8,128)S(1)} all-gather(f32[104,128]{1,0:T(8,128)S(1)} %get-tuple-element.181), channel_id=4, replica_groups=mesh['grp'=2,'day'=4,'cell'=4] {'cell'}, dimensions={0}, use_global_device_ids=true | all-gather | bytes 266240 | tf_op jit(solution)/shard_map/all_gather | solution.py:573
  154.3 4.4 %rebuild.5 = (f32[768,2048]{1,0:T(8,128)S(1)}, f32[104,128]{1,0:T(8,128)S(1)}) custom-call(s32[8]{0:T(128)S(1)} %compare_select_fusion.7.meta.refs_0_, f32[4,104,128]{2,1,0:T(8,128)S(1)} %bitcast.8, bf16[1024,2048]{1,0:T(8,128)(2,1)S(1)} %get-tuple-element.178.refs_2_, f32[768,2048]{1,0:T(8,128)S(1)} %get-tuple-element.179.refs_3_), custom_call_target="tpu_custom_call", output_to_operand_aliasing={{0}: (3, {})} | custom-call | flops 3221225472 | bytes 6291456 | tf_op jit(solution)/shard_map/rebuild/pallas_call | solution.py:416
  159.1 3.8 %project.7 = (f32[848,256]{1,0:T(8,128)S(1)}, bf16[1024,2048]{1,0:T(8,128)(2,1)S(1)}) custom-call(s32[8]{0:T(128)S(1)} %compare_select_fusion.7.meta.refs_0_, bf16[896,2048]{1,0:T(8,128)(2,1)S(1)} %stage.1.refs_1_, bf16[128,2048]{1,0:T(8,128)(2,1)S(1)} %collective-permute-done.20.refs_2_, bf16[128,2048]{1,0:T(8,128)(2,1)S(1)} %collective-permute-done.12.refs_3_, ...), custom_call_target="tpu_custom_call" | custom-call | flops 2667577344 | bytes 3145728 | tf_op jit(solution)/shard_map/project/pallas_call | solution.py:365
  162.9 6.9 %collective-permute-done.27.refs_2_ = bf16[128,2048]{1,0:T(8,128)(2,1)S(1)} collective-permute-done((bf16[128,2048]{1,0:T(8,128)(2,1)S(1)}, bf16[128,2048]{1,0:T(8,128)(2,1)S(1)}, u32[]{:S(2)}, u32[]{:S(2)}) %collective-permute-start.27) | collective-permute-done | bytes 524320 | tf_op jit(solution)/shard_map/ppermute | solution.py:509
  173.8 4.4 %rebuild.6 = (f32[768,2048]{1,0:T(8,128)S(1)}, f32[104,128]{1,0:T(8,128)S(1)}) custom-call(s32[8]{0:T(128)S(1)} %compare_select_fusion.7.meta.refs_0_, f32[4,104,128]{2,1,0:T(8,128)S(1)} %bitcast.7, bf16[1024,2048]{1,0:T(8,128)(2,1)S(1)} %get-tuple-element.182.refs_2_, f32[768,2048]{1,0:T(8,128)S(1)} %get-tuple-element.183.refs_3_), custom_call_target="tpu_custom_call", output_to_operand_aliasing={{0}: (3, {})} | custom-call | flops 3221225472 | bytes 6291456 | tf_op jit(solution)/shard_map/rebuild/pallas_call | solution.py:416
  178.3 5.7 %rebuild.7 = (f32[768,2048]{1,0:T(8,128)}, f32[64,768]{1,0:T(8,128)}) custom-call(s32[8]{0:T(128)S(1)} %compare_select_fusion.7.meta.refs_0_, f32[104,128]{1,0:T(8,128)S(1)} %get-tuple-element.164.refs_1_, f32[104,128]{1,0:T(8,128)S(1)} %collective-permute-done.40.refs_2_, f32[104,128]{1,0:T(8,128)S(1)} %collective-permute-done.41.refs_3_, ...), custom_call_target="tpu_custom_call" | custom-call | flops 3221225472 | bytes 6291456 | tf_op jit(solution)/shard_map/rebuild/pallas_call | solution.py:416
  (82 shorter events, 51.8 us)
Async XLA Ops:
  7.2 28.9 %collective-permute-start = (bf16[192,2048]{1,0:T(8,128)(2,1)S(1)}, bf16[192,2048]{1,0:T(8,128)(2,1)S(1)}, u32[]{:S(2)}, u32[]{:S(2)}) collective-permute-start(bf16[192,2048]{1,0:T(8,128)(2,1)S(1)} %get-tuple-element.96), channel_id=1, source_target_pairs={{0,4},{4,0},{8,12},{12,8},{1,5},{5,1},{9,13},{13,9},{2,6},{6,2},{1... | collective-permute-start | bytes 2359304 | tf_op jit(solution)/shard_map/ppermute | solution.py:517
  11.6 24.5 %collective-permute-start.1 = (bf16[192,2048]{1,0:T(8,128)(2,1)S(1)}, bf16[192,2048]{1,0:T(8,128)(2,1)S(1)}, u32[]{:S(2)}, u32[]{:S(2)}) collective-permute-start(bf16[192,2048]{1,0:T(8,128)(2,1)S(1)} %get-tuple-element.97), channel_id=1, source_target_pairs={{4,8},{8,4},{5,9},{9,5},{6,10},{10,6},{7,11},{11,7},{20,24},{24,20... | collective-permute-start | bytes 2359304 | tf_op jit(solution)/shard_map/ppermute | solution.py:519
  19.3 28.1 %collective-permute-start.7 = (bf16[128,2048]{1,0:T(8,128)(2,1)S(1)}, bf16[128,2048]{1,0:T(8,128)(2,1)S(1)}, u32[]{:S(2)}, u32[]{:S(2)}) collective-permute-start(bf16[128,2048]{1,0:T(8,128)(2,1)S(1)} %get-tuple-element.105), channel_id=1, source_target_pairs={{0,4},{4,0},{8,12},{12,8},{1,5},{5,1},{9,13},{13,9},{2,6},{6,2},{1... | collective-permute-start | bytes 1572872 | tf_op jit(solution)/shard_map/ppermute | solution.py:517
  24.3 29.3 %collective-permute-start.9 = (bf16[128,2048]{1,0:T(8,128)(2,1)S(1)}, bf16[128,2048]{1,0:T(8,128)(2,1)S(1)}, u32[]{:S(2)}, u32[]{:S(2)}) collective-permute-start(bf16[128,2048]{1,0:T(8,128)(2,1)S(1)} %get-tuple-element.105), channel_id=1, source_target_pairs={{4,8},{8,4},{5,9},{9,5},{6,10},{10,6},{7,11},{11,7},{20,24},{24,20... | collective-permute-start | bytes 1572872 | tf_op jit(solution)/shard_map/ppermute | solution.py:519
  25.0 28.6 %collective-permute-start.8 = (bf16[128,2048]{1,0:T(8,128)(2,1)S(1)}, bf16[128,2048]{1,0:T(8,128)(2,1)S(1)}, u32[]{:S(2)}, u32[]{:S(2)}) collective-permute-start(bf16[128,2048]{1,0:T(8,128)(2,1)S(1)} %collective-permute-done.5.refs_2_), channel_id=1, source_target_pairs={{0,16},{12,28},{4,20},{8,24},{16,0},{28,12},{20,4},{24,8},{1,17},{... | collective-permute-start | bytes 1572872 | tf_op jit(solution)/shard_map/ppermute | solution.py:509
  36.2 20.8 %collective-permute-start.3 = (bf16[128,2048]{1,0:T(8,128)(2,1)S(1)}, bf16[128,2048]{1,0:T(8,128)(2,1)S(1)}, u32[]{:S(2)}, u32[]{:S(2)}) collective-permute-start(bf16[128,2048]{1,0:T(8,128)(2,1)S(1)} %get-tuple-element.121.refs_3_), channel_id=1, source_target_pairs={{0,16},{12,28},{4,20},{8,24},{16,0},{28,12},{20,4},{24,8},{1,17},{... | collective-permute-start | bytes 1572872 | tf_op jit(solution)/shard_map/ppermute | solution.py:509
  38.3 19.5 %collective-permute-start.2 = (bf16[128,2048]{1,0:T(8,128)(2,1)S(1)}, bf16[128,2048]{1,0:T(8,128)(2,1)S(1)}, u32[]{:S(2)}, u32[]{:S(2)}) collective-permute-start(bf16[128,2048]{1,0:T(8,128)(2,1)S(1)} %get-tuple-element.98), channel_id=1, source_target_pairs={{0,4},{4,0},{8,12},{12,8},{1,5},{5,1},{9,13},{13,9},{2,6},{6,2},{1... | collective-permute-start | bytes 1572872 | tf_op jit(solution)/shard_map/ppermute | solution.py:517
  53.7 19.0 %collective-permute-start.10 = (bf16[128,2048]{1,0:T(8,128)(2,1)S(1)}, bf16[128,2048]{1,0:T(8,128)(2,1)S(1)}, u32[]{:S(2)}, u32[]{:S(2)}) collective-permute-start(bf16[128,2048]{1,0:T(8,128)(2,1)S(1)} %collective-permute-done.6.refs_3_), channel_id=1, source_target_pairs={{4,0},{8,12},{5,1},{9,13},{6,2},{10,14},{7,3},{11,15},{20,16},{24,... | collective-permute-start | bytes 1572872 | tf_op jit(solution)/shard_map/ppermute | solution.py:521
  55.0 18.4 %collective-permute-start.11 = (bf16[128,2048]{1,0:T(8,128)(2,1)S(1)}, bf16[128,2048]{1,0:T(8,128)(2,1)S(1)}, u32[]{:S(2)}, u32[]{:S(2)}) collective-permute-start(bf16[128,2048]{1,0:T(8,128)(2,1)S(1)} %collective-permute-done.7.refs_4_), channel_id=1, source_target_pairs={{0,16},{12,28},{4,20},{8,24},{16,0},{28,12},{20,4},{24,8},{1,17},{... | collective-permute-start | bytes 1572872 | tf_op jit(solution)/shard_map/ppermute | solution.py:509
  57.8 25.0 %collective-permute-start.14 = (bf16[128,2048]{1,0:T(8,128)(2,1)S(1)}, bf16[128,2048]{1,0:T(8,128)(2,1)S(1)}, u32[]{:S(2)}, u32[]{:S(2)}) collective-permute-start(bf16[128,2048]{1,0:T(8,128)(2,1)S(1)} %get-tuple-element.147.refs_5_), channel_id=1, source_target_pairs={{4,0},{8,12},{5,1},{9,13},{6,2},{10,14},{7,3},{11,15},{20,16},{24,... | collective-permute-start | bytes 1572872 | tf_op jit(solution)/shard_map/ppermute | solution.py:521
  59.1 28.2 %collective-permute-start.15 = (bf16[128,2048]{1,0:T(8,128)(2,1)S(1)}, bf16[128,2048]{1,0:T(8,128)(2,1)S(1)}, u32[]{:S(2)}, u32[]{:S(2)}) collective-permute-start(bf16[128,2048]{1,0:T(8,128)(2,1)S(1)} %collective-permute-done.2.refs_5_), channel_id=1, source_target_pairs={{0,16},{12,28},{4,20},{8,24},{16,0},{28,12},{20,4},{24,8},{1,17},{... | collective-permute-start | bytes 1572872 | tf_op jit(solution)/shard_map/ppermute | solution.py:509
  72.6 19.6 %collective-permute-start.16 = (bf16[128,2048]{1,0:T(8,128)(2,1)S(1)}, bf16[128,2048]{1,0:T(8,128)(2,1)S(1)}, u32[]{:S(2)}, u32[]{:S(2)}) collective-permute-start(bf16[128,2048]{1,0:T(8,128)(2,1)S(1)} %get-tuple-element.121.refs_3_), channel_id=1, source_target_pairs={{4,8},{8,4},{5,9},{9,5},{6,10},{10,6},{7,11},{11,7},{20,24},{24,20... | collective-permute-start | bytes 1572872 | tf_op jit(solution)/shard_map/ppermute | solution.py:519
  73.3 20.2 %collective-permute-start.13 = (bf16[128,2048]{1,0:T(8,128)(2,1)S(1)}, bf16[128,2048]{1,0:T(8,128)(2,1)S(1)}, u32[]{:S(2)}, u32[]{:S(2)}) collective-permute-start(bf16[128,2048]{1,0:T(8,128)(2,1)S(1)} %collective-permute-done.9.refs_7_), channel_id=1, source_target_pairs={{4,0},{8,12},{5,1},{9,13},{6,2},{10,14},{7,3},{11,15},{20,16},{24,... | collective-permute-start | bytes 1572872 | tf_op jit(solution)/shard_map/ppermute | solution.py:521
  74.6 19.6 %collective-permute-start.17 = (bf16[128,2048]{1,0:T(8,128)(2,1)S(1)}, bf16[128,2048]{1,0:T(8,128)(2,1)S(1)}, u32[]{:S(2)}, u32[]{:S(2)}) collective-permute-start(bf16[128,2048]{1,0:T(8,128)(2,1)S(1)} %collective-permute-done.6.refs_3_), channel_id=1, source_target_pairs={{4,20},{8,24},{20,4},{24,8},{5,21},{9,25},{21,5},{25,9},{6,22},{10... | collective-permute-start | bytes 1572872 | tf_op jit(solution)/shard_map/ppermute | solution.py:509
  105.8 17.8 %collective-permute-start.22 = (bf16[128,2048]{1,0:T(8,128)(2,1)S(1)}, bf16[128,2048]{1,0:T(8,128)(2,1)S(1)}, u32[]{:S(2)}, u32[]{:S(2)}) collective-permute-start(bf16[128,2048]{1,0:T(8,128)(2,1)S(1)} %collective-permute-done.13.refs_6_), channel_id=1, source_target_pairs={{0,16},{12,28},{16,0},{28,12},{1,17},{13,29},{17,1},{29,13},{2,18}... | collective-permute-start | bytes 1572872 | tf_op jit(solution)/shard_map/ppermute | solution.py:509
  107.8 22.1 %collective-permute-start.23 = (bf16[128,2048]{1,0:T(8,128)(2,1)S(1)}, bf16[128,2048]{1,0:T(8,128)(2,1)S(1)}, u32[]{:S(2)}, u32[]{:S(2)}) collective-permute-start(bf16[128,2048]{1,0:T(8,128)(2,1)S(1)} %collective-permute-done.15.refs_9_), channel_id=1, source_target_pairs={{4,8},{8,4},{5,9},{9,5},{6,10},{10,6},{7,11},{11,7},{20,24},{24,20... | collective-permute-start | bytes 1572872 | tf_op jit(solution)/shard_map/ppermute | solution.py:519
  108.5 22.7 %collective-permute-start.32 = (bf16[128,2048]{1,0:T(8,128)(2,1)S(1)}, bf16[128,2048]{1,0:T(8,128)(2,1)S(1)}, u32[]{:S(2)}, u32[]{:S(2)}) collective-permute-start(bf16[128,2048]{1,0:T(8,128)(2,1)S(1)} %collective-permute-done.16.refs_5_), channel_id=1, source_target_pairs={{4,0},{8,12},{5,1},{9,13},{6,2},{10,14},{7,3},{11,15},{20,16},{24,... | collective-permute-start | bytes 1572872 | tf_op jit(solution)/shard_map/ppermute | solution.py:521
  129.9 19.8 %collective-permute-start.24 = (bf16[128,2048]{1,0:T(8,128)(2,1)S(1)}, bf16[128,2048]{1,0:T(8,128)(2,1)S(1)}, u32[]{:S(2)}, u32[]{:S(2)}) collective-permute-start(bf16[128,2048]{1,0:T(8,128)(2,1)S(1)} %collective-permute-done.19.refs_7_), channel_id=1, source_target_pairs={{4,0},{8,12},{5,1},{9,13},{6,2},{10,14},{7,3},{11,15},{20,16},{24,... | collective-permute-start | bytes 1572872 | tf_op jit(solution)/shard_map/ppermute | solution.py:521
  131.2 19.2 %collective-permute-start.25 = (bf16[128,2048]{1,0:T(8,128)(2,1)S(1)}, bf16[128,2048]{1,0:T(8,128)(2,1)S(1)}, u32[]{:S(2)}, u32[]{:S(2)}) collective-permute-start(bf16[128,2048]{1,0:T(8,128)(2,1)S(1)} %collective-permute-done.20.refs_2_), channel_id=1, source_target_pairs={{0,16},{12,28},{16,0},{28,12},{1,17},{13,29},{17,1},{29,13},{2,18}... | collective-permute-start | bytes 1572872 | tf_op jit(solution)/shard_map/ppermute | solution.py:509
  133.8 16.7 %collective-permute-start.26 = (bf16[128,2048]{1,0:T(8,128)(2,1)S(1)}, bf16[128,2048]{1,0:T(8,128)(2,1)S(1)}, u32[]{:S(2)}, u32[]{:S(2)}) collective-permute-start(bf16[128,2048]{1,0:T(8,128)(2,1)S(1)} %collective-permute-done.3.refs_7_), channel_id=1, source_target_pairs={{4,8},{8,4},{5,9},{9,5},{6,10},{10,6},{7,11},{11,7},{20,24},{24,20... | collective-permute-start | bytes 1572872 | tf_op jit(solution)/shard_map/ppermute | solution.py:519
  134.5 24.3 %collective-permute-start.38 = (bf16[128,2048]{1,0:T(8,128)(2,1)S(1)}, bf16[128,2048]{1,0:T(8,128)(2,1)S(1)}, u32[]{:S(2)}, u32[]{:S(2)}) collective-permute-start(bf16[128,2048]{1,0:T(8,128)(2,1)S(1)} %collective-permute-done.31.refs_9_), channel_id=1, source_target_pairs={{4,0},{8,12},{5,1},{9,13},{6,2},{10,14},{7,3},{11,15},{20,16},{24,... | collective-permute-start | bytes 1572872 | tf_op jit(solution)/shard_map/ppermute | solution.py:521
  135.8 23.3 %collective-permute-start.39 = (bf16[128,2048]{1,0:T(8,128)(2,1)S(1)}, bf16[128,2048]{1,0:T(8,128)(2,1)S(1)}, u32[]{:S(2)}, u32[]{:S(2)}) collective-permute-start(bf16[128,2048]{1,0:T(8,128)(2,1)S(1)} %collective-permute-done.32.refs_4_), channel_id=1, source_target_pairs={{0,16},{12,28},{16,0},{28,12},{1,17},{13,29},{17,1},{29,13},{2,18}... | collective-permute-start | bytes 1572872 | tf_op jit(solution)/shard_map/ppermute | solution.py:509
  150.5 19.3 %collective-permute-start.27 = (bf16[128,2048]{1,0:T(8,128)(2,1)S(1)}, bf16[128,2048]{1,0:T(8,128)(2,1)S(1)}, u32[]{:S(2)}, u32[]{:S(2)}) collective-permute-start(bf16[128,2048]{1,0:T(8,128)(2,1)S(1)} %collective-permute-done.24.refs_6_), channel_id=1, source_target_pairs={{0,16},{12,28},{16,0},{28,12},{1,17},{13,29},{17,1},{29,13},{2,18}... | collective-permute-start | bytes 1572872 | tf_op jit(solution)/shard_map/ppermute | solution.py:509
  153.0 16.8 %collective-permute-start.37 = (bf16[128,2048]{1,0:T(8,128)(2,1)S(1)}, bf16[128,2048]{1,0:T(8,128)(2,1)S(1)}, u32[]{:S(2)}, u32[]{:S(2)}) collective-permute-start(bf16[128,2048]{1,0:T(8,128)(2,1)S(1)} %collective-permute-done.23.refs_5_), channel_id=1, source_target_pairs={{4,0},{8,12},{5,1},{9,13},{6,2},{10,14},{7,3},{11,15},{20,16},{24,... | collective-permute-start | bytes 1572872 | tf_op jit(solution)/shard_map/ppermute | solution.py:521
  (21 other events, 297.1 us)
